TPU v7x, 32 devices: a whole 2x2x4 slice. The times are simulated.
32 devices in a mesh: mem: 4 (over z), head: 2 (over y), span: 4 (over x, core).
Axes of the slice: x: 2, y: 2, z: 4, core: 2. Of those that a mesh axis runs over, the one named last changes fastest.
Arguments:
- query: bfloat16 [4, 512, 8, 8, 128], P('span', 'mem', 'head'), may hold values from -6 to 6
- new_keys: bfloat16 [4, 512, 8, 128], P('span', 'mem', 'head'), may hold values from -6 to 6
- new_values: bfloat16 [4, 512, 8, 128], P('span', 'mem', 'head'), may hold values from -5 to 5
- memory_keys: bfloat16 [128, 128, 8, 128], P('mem', None, 'head'), may hold values from -5 to 5
- memory_values: bfloat16 [128, 128, 8, 128], P('mem', None, 'head'), may hold values from -5 to 5
- retrieved: int32 [4, 8, 16], P('span', 'head'), may hold values from 0 to 127, as said below
Outputs:
- attended: bfloat16 [4, 512, 8192], P('span', ('mem', 'head'))
Inputs may be any that keep to these rules, and one draw needn't show every extreme that they name: Each list retrieved[b, h, :] names 16 different units. The units o * 32 to (o + 1) * 32 - 1 appear at most 8 times in one list, and in every list some o has exactly 8.
All inputs are finite; a program needn't handle non-finite values.
Results may differ from a plain program's by a relative error of at most 0.005.
Values may be sent and summed in bfloat16 or wider, within the bound.
No kernel may reach another device: no remote copies, remote signals or barrier semaphores. Data moves between devices by JAX's collectives and lax.ppermute only.
A program may use at most 64 MiB of HBM per device.

v0:
```python
import math

import jax
import jax.numpy as jnp
from jax import lax
from jax.sharding import PartitionSpec as P

NEG = -1e30


def shifted(value, axis, steps):
    count = lax.axis_size(axis)
    first, last = (max(0, -steps), min(count, count - steps))
    return lax.ppermute(value, axis, [(source, source + steps) for source in range(first, last)])


def local(query, new_keys, new_values, memory_keys, memory_values, retrieved):
    queries = query[0]
    row_count, head_count, group_size, head_width = queries.shape
    score_scale = 1.0 / math.sqrt(head_width)
    mem_index = lax.axis_index("mem")
    block_index = lax.axis_index("span")
    row_position = mem_index * row_count + jnp.arange(row_count, dtype=jnp.int32)

    def update(carry_state, key_pair, key_mask):
        old_peak, old_total, old_accum = carry_state
        scores = (
            jnp.einsum("rhgd,khd->rhgk", queries, key_pair[0], preferred_element_type=jnp.float32)
            * score_scale
        )
        scores = jnp.where(key_mask, scores, NEG)
        new_peak = jnp.maximum(old_peak, jnp.max(scores, axis=-1))
        weights = jnp.where(key_mask, jnp.exp(scores - new_peak[..., None]), 0.0)
        factor = jnp.exp(old_peak - new_peak)
        new_total = old_total * factor + jnp.sum(weights, axis=-1)
        new_accum = old_accum * factor[..., None] + jnp.einsum(
            "rhgk,khd->rhgd",
            weights.astype(jnp.bfloat16),
            key_pair[1],
            preferred_element_type=jnp.float32,
        )
        return (new_peak, new_total, new_accum)

    def sweep(carry_state, key_pair, first_key, mask_maker):
        key_count = key_pair.shape[1]
        step_size = key_count if key_count <= 1024 else math.gcd(key_count, 512)

        def advance(step_index, loop_state):
            sub_pair = lax.dynamic_slice_in_dim(key_pair, step_index * step_size, step_size, 1)
            key_position = (
                first_key + step_index * step_size + jnp.arange(step_size, dtype=jnp.int32)
            )
            return update(loop_state, sub_pair, mask_maker(key_position))

        return lax.fori_loop(0, key_count // step_size, advance, carry_state)

    def current_mask(key_position):
        return (key_position[None, :] <= row_position[:, None])[:, None, None, :]

    def prior_mask(key_position):
        return ((key_position[None, :] > row_position[:, None]) & (block_index > 0))[
            :, None, None, :
        ]

    def full_mask(key_position):
        return jnp.ones((1, 1, 1, key_position.shape[0]), bool)

    carry_state = (
        jnp.full((row_count, head_count, group_size), NEG, jnp.float32),
        jnp.zeros((row_count, head_count, group_size), jnp.float32),
        jnp.zeros((row_count, head_count, group_size, head_width), jnp.float32),
    )
    own_pair = jnp.stack([new_keys[0], new_values[0]])
    prior_pair = shifted(own_pair, "span", 1)
    loop_state = carry_state
    first_key = jnp.int32(0)
    loop_state = sweep(
        loop_state, lax.all_gather(own_pair, "mem", axis=1, tiled=True), first_key, current_mask
    )
    carry_state = sweep(
        loop_state, lax.all_gather(prior_pair, "mem", axis=1, tiled=True), first_key, prior_mask
    )
    unit_lists = retrieved[0]
    units_dev = memory_keys.shape[0]
    owners = unit_lists // units_dev
    local_units = unit_lists % units_dev
    owned_here = owners == mem_index
    gathered_pair = []
    for source_array in (memory_keys, memory_values):
        per_head = [
            source_array[local_units[head_at], :, head_at, :] for head_at in range(head_count)
        ]
        gathered_pair.append(jnp.stack(per_head, axis=2))
    gathered_units = jnp.stack(gathered_pair)
    keep_mask = jnp.transpose(owned_here)[None, :, None, :, None]
    slot_terms = jnp.where(keep_mask, gathered_units, jnp.zeros((), jnp.bfloat16))
    slot_terms = slot_terms.reshape(2, -1, head_count, head_width)
    summed_pair = lax.psum(slot_terms, "mem").astype(jnp.float32).astype(jnp.bfloat16)
    carry_state = sweep(carry_state, summed_pair, 0, full_mask)
    final_peak, final_total, final_accum = carry_state
    attended = (final_accum / final_total[..., None]).astype(jnp.bfloat16)
    attended = attended.reshape(row_count, head_count * group_size * head_width)
    moved = lax.all_to_all(attended, "head", split_axis=0, concat_axis=1, tiled=True)
    return moved[None]


def solution(mesh):
    return jax.shard_map(
        local,
        mesh=mesh,
        in_specs=(
            P("span", "mem", "head", None, None),
            P("span", "mem", "head", None),
            P("span", "mem", "head", None),
            P("mem", None, "head", None),
            P("mem", None, "head", None),
            P("span", "head", None),
        ),
        out_specs=P("span", ("mem", "head"), None),
        check_vma=False,
    )
```

profile of v0, /device:TPU:17, one launch (start us, length us, event | category | flops | bytes accessed | tf_op | source)
XLA Modules:
  0.0 301.1 jit_solution(8670590640695691922)
XLA Ops:
  6.5 0.9 copy_dynamic-update-slice_fusion.1
  7.5 0.9 copy_dynamic-update-slice_fusion
  8.4 0.7 copy-done.4
  9.1 0.0 all-gather.3.cloned.1.call-update
  9.1 0.0 all-gather.5.cloned.1.call-start
  9.2 3.7 %collective-permute-start = (bf16[2,128,4,128]{3,1,2,0:T(8,128)(2,1)}, bf16[2,128,4,128]{3,1,2,0:T(8,128)(2,1)S(1)}, u32[]{:S(2)}, u32[]{:S(2)}) collective-permute-start(bf16[2,128,4,128]{3,1,2,0:T(8,128)(2,1)} %copy-done.4), channel_id=1, source_target_pairs={{0,1},{1,2},{2,3},{4,5},{5,6},{6,7},{8,9},{9,10},{10,11},{12,13},{... | collective-permute-start | bytes 786440 | tf_op jit(solution)/shard_map/ppermute | solution.py:14
  12.9 0.7 add_select_fusion
  13.6 2.9 collective-permute-done
  16.5 0.7 copy-done.5
  17.2 0.0 all-gather.5.cloned.1.call-update
  17.2 0.0 all-reduce.6.cloned.1.call-start
  17.3 2.6 gather_fusion
  19.9 2.6 gather_fusion.1
  22.5 2.6 gather_fusion.4
  25.1 2.6 gather_fusion.5
  27.7 3.4 %gather_fusion.2 = bf16[16,128,128]{2,0,1:T(8,128)(2,1)} fusion(bf16[32,128,4,128]{3,2,1,0:T(4,128)(2,1)} %param.11, s32[16]{0:T(128)S(1)} %get-tuple-element.191), kind=kCustom, calls=%fused_computation.2 | custom fusion | bytes 1048704 | tf_op jit(solution)/shard_map/gather | solution.py:91
  31.1 2.6 gather_fusion.6
  33.7 3.4 %gather_fusion.3 = bf16[16,128,128]{2,0,1:T(8,128)(2,1)} fusion(bf16[32,128,4,128]{3,2,1,0:T(4,128)(2,1)} %param.11, s32[16]{0:T(128)S(1)} %get-tuple-element.190), kind=kCustom, calls=%fused_computation.3 | custom fusion | bytes 1048704 | tf_op jit(solution)/shard_map/gather | solution.py:91
  37.1 2.6 gather_fusion.7
  39.7 0.1 copy.44
  39.8 0.1 copy.45
  40.0 1.2 copy.46
  41.1 1.2 copy.47
  42.3 0.1 copy.48
  42.5 0.1 copy.49
  42.6 0.1 copy.50
  42.8 0.1 copy.51
  42.9 0.1 broadcast_bitcast_fusion
  43.0 4.6 %maximum_select_fusion = bf16[2,2048,4,128]{3,1,2,0:T(8,128)(2,1)} fusion(bf16[1,2048,1,128]{3,1,2,0:T(8,128)(2,1)S(1)} %bitcast.186, bf16[1,2048,1,128]{3,1,2,0:T(8,128)(2,1)S(1)} %bitcast.185, bf16[1,2048,1,128]{3,1,2,0:T(8,128)(2,1)S(1)} %bitcast.184, bf16[1,2048,1,128]{3,1,2,0:T(8,128)(2,1)S(1)} %bitcast.183, bf16[1,2048,1,128]{3,1,2,0:T(8,128)(2,1)S(1)} %bitcast.182, ...), kind=kLoop, calls=%fused_computation.35 | loop fusion | flops 16777216 | bytes 8396800 | tf_op jit(solution)/shard_map/jit(_where)/select_n | solution.py:96
  47.6 0.0 all-reduce.6.cloned.1.call-update
  47.7 0.4 copy.80
  48.1 0.1 iota_compare_fusion.1
  48.2 0.0 all-gather.3.cloned.1.call-done
  48.2 5.9 %fusion.13 = (f32[128,4,8]{0,2,1:T(8,128)S(1)}, f32[4,512,128,8]{2,1,3,0:T(8,128)}) fusion(pred[128,512]{0,1:T(8,128)(4,1)S(1)} %get-tuple-element.193, bf16[1,128,4,8,128]{4,3,2,1,0:T(8,128)(2,1)S(1)} %copy-done.1, bf16[2,512,4,128]{3,1,2,0:T(8,128)(2,1)} %all-gather.3.cloned.1.call-done), kind=kOutput, calls=%fused_computation.29 | convolution fusion | flops 543158272 | bytes 10043392 | tf_op jit(solution)/shard_map/while/body/eval_jaxpr/rhgd,khd->rhgk/dot_general | solution.py:28
  54.1 12.7 %all-gather.5.cloned.1.call-done = bf16[2,512,4,128]{3,1,2,0:T(8,128)(2,1)} async-done(((bf16[2,128,4,128]{3,1,2,0:T(8,128)(2,1)}), bf16[2,512,4,128]{3,1,2,0:T(8,128)(2,1)}) %all-gather.5.cloned.1.call-update) | async-done | bytes 1048592 | tf_op jit(solution)/shard_map/all_gather | solution.py:81
  66.8 2.8 fusion.14
  69.7 0.8 slice-done.1
  70.5 4.6 %fusion.16 = (f32[128,4,8]{0,2,1:T(8,128)S(1)}, f32[128,4,8]{0,2,1:T(8,128)S(1)}) fusion(f32[4,512,128,8]{2,1,3,0:T(8,128)S(1)} %bitcast.177, f32[128,4,8]{0,2,1:T(8,128)S(1)} %get-tuple-element.188, pred[128,512]{0,1:T(8,128)(4,1)S(1)} %get-tuple-element.193, f32[128,4,8]{0,2,1:T(8,128)S(1)} %get-tuple-element.247, ...), kind=kLoop, calls=%fused_computation.32 | loop fusion | flops 20963328 | bytes 16973824 | tf_op jit(solution)/shard_map/while/body/eval_jaxpr/reduce_sum | solution.py:35
  75.1 2.1 fusion.21
  77.2 2.2 bitcast_add_fusion.1
  79.4 143.8 %all-reduce.6.cloned.1.call-done = bf16[2,2048,4,128]{3,1,2,0:T(8,128)(2,1)} async-done(((bf16[2,2048,4,128]{3,1,2,0:T(8,128)(2,1)}), bf16[2,2048,4,128]{3,1,2,0:T(8,128)(2,1)}) %all-reduce.6.cloned.1.call-update) | async-done | bytes 4194320 | tf_op jit(solution)/shard_map/psum | solution.py:98
  223.2 51.6 %while.4 = (s32[]{:T(128)}, f32[128,4,8]{0,2,1:T(8,128)S(1)}, f32[128,4,8]{0,2,1:T(8,128)S(1)}, f32[128,4,8,128]{0,3,2,1:T(8,128)S(1)}, bf16[2,2048,4,128]{3,1,2...) while((s32[]{:T(128)}, f32[128,4,8]{0,2,1:T(8,128)S(1)}, ...), condition=%wide.region_8.9_spmd, body=%wide.region_5.8_spmd.sunk | while | flops 1091575808 | bytes 65274060 | solution.py:55
  223.2 2.3 bitcast_reduce_fusion.2
  225.5 3.2 %copy-done = f32[4,512,128,8]{2,1,3,0:T(8,128)} copy-done((f32[4,512,128,8]{2,1,3,0:T(8,128)}, f32[4,512,128,8]{2,1,3,0:T(8,128)S(1)}, u32[]{:S(2)}) %copy-start) | copy-done | bytes 8388632 | tf_op jit(solution)/shard_map/while
  228.7 1.6 fusion.63
  230.3 5.7 %bitcast_add_fusion.4 = f32[128,4,8,128]{0,3,2,1:T(8,128)S(1)} fusion(f32[128,4,8,128]{0,3,2,1:T(8,128)S(1)} %get-tuple-element.260, f32[4,512,128,8]{2,1,3,0:T(8,128)} %copy-done, f32[128,4,8]{0,2,1:T(8,128)S(1)} %max.54, f32[128,4,8]{0,2,1:T(8,128)S(1)} %get-tuple-element.245, bf16[2,2048,4,128]{3,1,2,0:T(8,128)(2,1)} %get-tuple-element.272, ...), kind=kOutput, calls=%fused_computation.16.clone.1 | convolution fusion | flops 544210944 | bytes 13139976 | tf_op jit(solution)/shard_map/while/body/eval_jaxpr/rhgk,khd->rhgd/dot_general | solution.py:36
  236.1 2.3 bitcast_reduce_fusion.2
  238.4 3.2 %copy-done = f32[4,512,128,8]{2,1,3,0:T(8,128)} copy-done((f32[4,512,128,8]{2,1,3,0:T(8,128)}, f32[4,512,128,8]{2,1,3,0:T(8,128)S(1)}, u32[]{:S(2)}) %copy-start) | copy-done | bytes 8388632 | tf_op jit(solution)/shard_map/while
  241.6 1.6 fusion.63
  243.2 5.7 %bitcast_add_fusion.4 = f32[128,4,8,128]{0,3,2,1:T(8,128)S(1)} fusion(f32[128,4,8,128]{0,3,2,1:T(8,128)S(1)} %get-tuple-element.260, f32[4,512,128,8]{2,1,3,0:T(8,128)} %copy-done, f32[128,4,8]{0,2,1:T(8,128)S(1)} %max.54, f32[128,4,8]{0,2,1:T(8,128)S(1)} %get-tuple-element.245, bf16[2,2048,4,128]{3,1,2,0:T(8,128)(2,1)} %get-tuple-element.272, ...), kind=kOutput, calls=%fused_computation.16.clone.1 | convolution fusion | flops 544210944 | bytes 13139976 | tf_op jit(solution)/shard_map/while/body/eval_jaxpr/rhgk,khd->rhgd/dot_general | solution.py:36
  249.0 2.3 bitcast_reduce_fusion.2
  251.3 3.2 %copy-done = f32[4,512,128,8]{2,1,3,0:T(8,128)} copy-done((f32[4,512,128,8]{2,1,3,0:T(8,128)}, f32[4,512,128,8]{2,1,3,0:T(8,128)S(1)}, u32[]{:S(2)}) %copy-start) | copy-done | bytes 8388632 | tf_op jit(solution)/shard_map/while
  254.5 1.6 fusion.63
  256.1 5.7 %bitcast_add_fusion.4 = f32[128,4,8,128]{0,3,2,1:T(8,128)S(1)} fusion(f32[128,4,8,128]{0,3,2,1:T(8,128)S(1)} %get-tuple-element.260, f32[4,512,128,8]{2,1,3,0:T(8,128)} %copy-done, f32[128,4,8]{0,2,1:T(8,128)S(1)} %max.54, f32[128,4,8]{0,2,1:T(8,128)S(1)} %get-tuple-element.245, bf16[2,2048,4,128]{3,1,2,0:T(8,128)(2,1)} %get-tuple-element.272, ...), kind=kOutput, calls=%fused_computation.16.clone.1 | convolution fusion | flops 544210944 | bytes 13139976 | tf_op jit(solution)/shard_map/while/body/eval_jaxpr/rhgk,khd->rhgd/dot_general | solution.py:36
  261.9 2.3 bitcast_reduce_fusion.2
  264.2 3.2 %copy-done = f32[4,512,128,8]{2,1,3,0:T(8,128)} copy-done((f32[4,512,128,8]{2,1,3,0:T(8,128)}, f32[4,512,128,8]{2,1,3,0:T(8,128)S(1)}, u32[]{:S(2)}) %copy-start) | copy-done | bytes 8388632 | tf_op jit(solution)/shard_map/while
  267.4 1.6 fusion.63
  269.0 5.7 %bitcast_add_fusion.4 = f32[128,4,8,128]{0,3,2,1:T(8,128)S(1)} fusion(f32[128,4,8,128]{0,3,2,1:T(8,128)S(1)} %get-tuple-element.260, f32[4,512,128,8]{2,1,3,0:T(8,128)} %copy-done, f32[128,4,8]{0,2,1:T(8,128)S(1)} %max.54, f32[128,4,8]{0,2,1:T(8,128)S(1)} %get-tuple-element.245, bf16[2,2048,4,128]{3,1,2,0:T(8,128)(2,1)} %get-tuple-element.272, ...), kind=kOutput, calls=%fused_computation.16.clone.1 | convolution fusion | flops 544210944 | bytes 13139976 | tf_op jit(solution)/shard_map/while/body/eval_jaxpr/rhgk,khd->rhgd/dot_general | solution.py:36
  274.8 0.3 divide_convert_fusion
  275.1 1.0 copy.52
  276.0 0.5 all_to_all.12
  276.5 15.4 %all_to_all.16 = bf16[2,64,4096]{2,1,0:T(8,128)(2,1)S(1)} all-to-all(bf16[2,64,4096]{2,1,0:T(8,128)(2,1)S(1)} %all_to_all.12), channel_id=1, replica_groups=mesh['mem'=4,'head'=2,'span'=4] {'head'}, dimensions={0} | all-to-all | bytes 2097152 | tf_op jit(solution)/shard_map/all_to_all | solution.py:103
  291.9 1.1 copy.53
  293.0 1.6 broadcast_in_dim.132
  (37 shorter events, 0.2 us)
Async XLA Ops:
  6.5 41.7 %all-gather.3.cloned.1.call-start = ((), (), s32[]{:S(2)}) async-start(), calls=%async_computation.1 | async-start | bytes 1310720 | tf_op jit(solution)/shard_map/all_gather | solution.py:78
  8.4 0.7 copy-start.4
  9.1 57.7 %all-gather.5.cloned.1.call-start = ((), (), s32[]{:S(2)}) async-start(), calls=%async_computation.2 | async-start | bytes 1310720 | tf_op jit(solution)/shard_map/all_gather | solution.py:81
  9.2 7.3 %collective-permute-start = (bf16[2,128,4,128]{3,1,2,0:T(8,128)(2,1)}, bf16[2,128,4,128]{3,1,2,0:T(8,128)(2,1)S(1)}, u32[]{:S(2)}, u32[]{:S(2)}) collective-permute-start(bf16[2,128,4,128]{3,1,2,0:T(8,128)(2,1)} %copy-done.4), channel_id=1, source_target_pairs={{0,1},{1,2},{2,3},{4,5},{5,6},{6,7},{8,9},{9,10},{10,11},{12,13},{... | collective-permute-start | bytes 786440 | tf_op jit(solution)/shard_map/ppermute | solution.py:14
  16.5 0.7 copy-start.5
  17.2 206.0 %all-reduce.6.cloned.1.call-start = ((), (), s32[]{:S(2)}) async-start(), calls=%async_computation.3 | async-start | bytes 8388608 | tf_op jit(solution)/shard_map/psum | solution.py:98
  33.7 9.2 %copy-start.6 = (s32[1,4,16]{2,1,0:T(4,128)S(1)}, s32[1,4,16]{2,1,0:T(4,128)}, u32[]{:S(2)}) copy-start(s32[1,4,16]{2,1,0:T(4,128)} %param.13) | copy-start | bytes 772
  42.3 5.3 %copy-start.1 = (bf16[1,128,4,8,128]{4,3,2,1,0:T(8,128)(2,1)S(1)}, bf16[1,128,4,8,128]{4,3,2,1,0:T(8,128)(2,1)}, u32[]{:S(2)}) copy-start(bf16[1,128,4,8,128]{4,3,2,1,0:T(8,128)(2,1)} %param.8) | copy-start | bytes 3145732
  66.8 2.9 slice-start
  66.8 3.6 %slice-start.1 = ((s8[8388608]{0:T(1024)(128)(4,1)}), s8[4194304]{0:T(1024)(128)(4,1)S(1)}, s32[]{:S(2)}) async-start(s8[8388608]{0:T(1024)(128)(4,1)} %bitcast.176), calls=%async_computation.5 | async-start | bytes 8388608
  70.5 4.6 %copy-start.2 = (bf16[2,512,4,128]{3,1,2,0:T(8,128)(2,1)S(1)}, bf16[2,512,4,128]{3,1,2,0:T(8,128)(2,1)}, u32[]{:S(2)}) copy-start(bf16[2,512,4,128]{3,1,2,0:T(8,128)(2,1)} %all-gather.3.cloned.1.call-done) | copy-start | bytes 3145732
  75.0 2.1 copy-start.3
  225.5 3.2 %copy-start = (f32[4,512,128,8]{2,1,3,0:T(8,128)}, f32[4,512,128,8]{2,1,3,0:T(8,128)S(1)}, u32[]{:S(2)}) copy-start(f32[4,512,128,8]{2,1,3,0:T(8,128)S(1)} %get-tuple-element.243) | copy-start | bytes 25165828 | tf_op jit(solution)/shard_map/while
  238.4 3.2 %copy-start = (f32[4,512,128,8]{2,1,3,0:T(8,128)}, f32[4,512,128,8]{2,1,3,0:T(8,128)S(1)}, u32[]{:S(2)}) copy-start(f32[4,512,128,8]{2,1,3,0:T(8,128)S(1)} %get-tuple-element.243) | copy-start | bytes 25165828 | tf_op jit(solution)/shard_map/while
  251.3 3.2 %copy-start = (f32[4,512,128,8]{2,1,3,0:T(8,128)}, f32[4,512,128,8]{2,1,3,0:T(8,128)S(1)}, u32[]{:S(2)}) copy-start(f32[4,512,128,8]{2,1,3,0:T(8,128)S(1)} %get-tuple-element.243) | copy-start | bytes 25165828 | tf_op jit(solution)/shard_map/while
  264.2 3.2 %copy-start = (f32[4,512,128,8]{2,1,3,0:T(8,128)}, f32[4,512,128,8]{2,1,3,0:T(8,128)S(1)}, u32[]{:S(2)}) copy-start(f32[4,512,128,8]{2,1,3,0:T(8,128)S(1)} %get-tuple-element.243) | copy-start | bytes 25165828 | tf_op jit(solution)/shard_map/while
Sparse Core Ops, SparseCore 0:
  9.2 28.4 all-gather.2
  39.4 27.4 all-gather.4
  69.2 153.9 all-reduce.5
where the time goes:
time: 306 us; the launch traced here: 301 us
  waiting for transfers between devices  159 us (52%)
  local copies, waits for them, and re-layouts  47.1 us (15%)
  matrix products  45.2 us (15%)
  other arithmetic  16.6 us (5%)
  blocking collectives  15.4 us (5%)
  between operations  13.4 us (4%)
  starting transfers between devices  3.76 us (1%)
    psum x1, waiting for transfers between devices, local(): lax.psum(slot_terms, 'mem').astype(jnp.float32).astype(jnp.bfloat16)  144 us
    dot_general x6, matrix products, update(): jnp.einsum('rhgk,khd->rhgd', weights.astype(jnp.bfloat16), key_pair[1], p...  27.3 us
    gather x16, local copies, waits for them, and re-layouts, local(): source_array[local_units[head_at], :, head_at, :]  25.5 us
    dot_general x6, matrix products, update(): jnp.einsum('rhgd,khd->rhgk', queries, key_pair[0], preferred_element_type...  18 us
    all_to_all x1, blocking collectives, local(): lax.all_to_all(attended, 'head', split_axis=0, concat_axis=1, tiled=True)  15.4 us
    while x12, local copies, waits for them, and re-layouts  12.8 us
    all_gather x1, waiting for transfers between devices, local(): lax.all_gather(prior_pair, 'mem', axis=1, tiled=True)  12.7 us
    reduce_sum x5, other arithmetic, update(): new_total = old_total * factor + jnp.sum(weights, axis=-1)  10.8 us
  transfers between devices with their start and end apart: 4, of which 3 were waited for; matrix products, arithmetic and copies ran while one was open for 16% of the time, Pallas kernels for 0%

commit v1 on v0

--- a/solution.py
+++ b/solution.py
@@ -1,11 +1,424 @@
+import functools
 import math
 
 import jax
 import jax.numpy as jnp
 from jax import lax
+from jax.experimental import pallas as pl
+from jax.experimental.pallas import tpu as pltpu
 from jax.sharding import PartitionSpec as P
 
 NEG = -1e30
+LANES = 256
+VMEM = 56 * 1024 * 1024
+
+PIECES = (8, 8, 16)
+CHUNKS = (8, 24, 32)
+
+
+def spec_smem():
+    return pl.BlockSpec(memory_space=pltpu.SMEM)
+
+
+def spec_vmem():
+    return pl.BlockSpec(memory_space=pltpu.VMEM)
+
+
+def spec_any():
+    return pl.BlockSpec(memory_space=pl.ANY)
+
+
+OWN, END, SEND, RECV, COUNT = range(5)
+OFFSET = 64
+
+
+def plan_kernel(units_dev, first, who_ref, list_ref, plan_ref):
+    heads, topk = list_ref.shape
+    width = plan_ref.shape[1]
+    me, end, opp_mid, opp_end = (who_ref[index] for index in range(4))
+
+    def clear(at, _):
+        plan_ref[SEND, at] = -1
+        plan_ref[RECV, at] = -1
+        plan_ref[OWN, at] = 0
+        plan_ref[END, at] = -1
+        return 0
+
+    lax.fori_loop(0, width, clear, 0)
+
+    def walk(at, counts):
+        head = at // topk
+        unit = list_ref[head, at % topk]
+        owner = unit // units_dev
+        n_own, n_end, n_mid, n_far = counts
+
+        @pl.when(owner == me)
+        def _():
+            plan_ref[OWN, n_own] = (unit % units_dev) * heads + head
+            plan_ref[SEND, n_own] = n_own
+
+        @pl.when(owner == end)
+        def _():
+            plan_ref[END, n_end] = head
+
+        @pl.when(owner == opp_mid)
+        def _():
+            plan_ref[RECV, n_mid] = head
+
+        return (
+            n_own + (owner == me).astype(jnp.int32),
+            n_end + (owner == end).astype(jnp.int32),
+            n_mid + (owner == opp_mid).astype(jnp.int32),
+            n_far + (owner == opp_end).astype(jnp.int32),
+        )
+
+    zero = jnp.int32(0)
+    n_own, n_end, n_mid, n_far = lax.fori_loop(0, heads * topk, walk, (zero, zero, zero, zero))
+    send_base = jnp.maximum(n_own, first)
+    recv_base = jnp.maximum(n_mid, first)
+
+    def forward(at, _):
+        plan_ref[SEND, send_base + at] = OFFSET + at
+        return 0
+
+    lax.fori_loop(0, n_end, forward, 0)
+
+    def tail(at, slot):
+        head = at // topk
+        here = (list_ref[head, at % topk] // units_dev) == opp_end
+
+        @pl.when(here)
+        def _():
+            plan_ref[RECV, recv_base + slot] = head
+
+        return slot + here.astype(jnp.int32)
+
+    lax.fori_loop(0, heads * topk, tail, zero)
+    plan_ref[COUNT, 0] = n_own
+    plan_ref[COUNT, 1] = n_end
+    plan_ref[COUNT, 2] = recv_base + n_far
+
+
+def make_plan(who, unit_lists, units_dev, first):
+    return pl.pallas_call(
+        functools.partial(plan_kernel, units_dev, first),
+        out_shape=jax.ShapeDtypeStruct((5, 128), jnp.int32),
+        in_specs=[spec_smem(), spec_smem()],
+        out_specs=spec_smem(),
+    )(who, unit_lists)
+
+
+def gather_kernel(first, plan_ref, keys_ref, values_ref, out_ref):
+    slot = first + pl.program_id(0)
+    rows, width = keys_ref.shape[1:]
+    tokens = out_ref.shape[2]
+    heads = rows // tokens
+
+    @pl.when(slot < plan_ref[COUNT, 0])
+    def _():
+        head = plan_ref[OWN, slot] % heads
+        token = lax.broadcasted_iota(jnp.int32, (tokens, rows), 0)
+        row = lax.broadcasted_iota(jnp.int32, (tokens, rows), 1)
+        pick = (row == token * heads + head).astype(jnp.bfloat16)
+        out_ref[0, 0] = jnp.dot(
+            pick, keys_ref[0], preferred_element_type=jnp.float32
+        ).astype(jnp.bfloat16)
+        out_ref[0, 1] = lax.dot_general(
+            values_ref[0], pick, (((0,), (1,)), ((), ())), preferred_element_type=jnp.float32
+        ).astype(jnp.bfloat16)
+
+
+def gather(plan, keys, values, tokens, first, count):
+    units, rows, width = keys.shape
+    heads = rows // tokens
+
+    def unit_at(step, plan_ref):
+        return (plan_ref[OWN, first + step] // heads, 0, 0)
+
+    return pl.pallas_call(
+        functools.partial(gather_kernel, first),
+        out_shape=jax.ShapeDtypeStruct((count, 2, tokens, width), jnp.bfloat16),
+        grid_spec=pltpu.PrefetchScalarGridSpec(
+            num_scalar_prefetch=1,
+            grid=(count,),
+            in_specs=[pl.BlockSpec((1, rows, width), unit_at)] * 2,
+            out_specs=pl.BlockSpec((1, 2, tokens, width), lambda step, plan_ref: (step, 0, 0, 0)),
+        ),
+    )(plan, keys, values)
+
+
+def pack_kernel(first, count, piece_sizes, plan_ref, *refs):
+    n_piece = len(piece_sizes)
+    own_refs, end_refs = refs[:n_piece], refs[n_piece : 2 * n_piece]
+    out_ref, sems = refs[2 * n_piece :]
+
+    def each(act):
+        for slot in range(count):
+            source = plan_ref[SEND, first + slot]
+            base = 0
+            for size, own_ref, end_ref in zip(piece_sizes, own_refs, end_refs):
+                for offset, ref in ((0, own_ref), (OFFSET, end_ref)):
+                    at = source - offset - base
+
+                    @pl.when((at >= 0) & (at < size))
+                    def _(ref=ref, at=at, slot=slot):
+                        act(pltpu.make_async_copy(ref.at[at], out_ref.at[slot], sems.at[slot]))
+
+                base += size
+
+    each(lambda copy: copy.start())
+    each(lambda copy: copy.wait())
+
+
+def pack(plan, own, end, first, count):
+    sizes = tuple(piece.shape[0] for piece in own)
+    return pl.pallas_call(
+        functools.partial(pack_kernel, first, count, sizes),
+        out_shape=jax.ShapeDtypeStruct((count,) + own[0].shape[1:], jnp.bfloat16),
+        in_specs=[spec_smem()] + [spec_any()] * (2 * len(own)),
+        out_specs=spec_any(),
+        scratch_shapes=[pltpu.SemaphoreType.DMA((count,))],
+    )(plan, *own, *end)
+
+
+def attend(scale, keys, values_t, queries_t, mask, state):
+    peak, total, accum = state
+    scores = jnp.dot(keys, queries_t, preferred_element_type=jnp.float32)
+    if mask is not None:
+        scores = jnp.where(mask, scores, NEG)
+    new_peak = jnp.maximum(peak, jnp.max(scores, axis=0, keepdims=True))
+    weights = jnp.exp2((scores - new_peak) * scale)
+    factor = jnp.exp2((peak - new_peak) * scale)
+    total = total * factor + jnp.sum(weights, axis=0, keepdims=True)
+    accum = accum * factor + jnp.dot(
+        values_t, weights.astype(jnp.bfloat16), preferred_element_type=jnp.float32
+    )
+    return new_peak, total, accum
+
+
+def new_kernel(scale, who_ref, cur_ref, prior_ref, own_ref, end_ref, peak_ref, total_ref, accum_ref):
+    low, has_prior, is_mid = who_ref[4] == 1, who_ref[5] == 1, who_ref[6] == 1
+    tokens = cur_ref.shape[3]
+    rows = own_ref.shape[2]
+
+    def masks():
+        key = lax.broadcasted_iota(jnp.int32, (tokens, LANES), 0)
+        position = lax.broadcasted_iota(jnp.int32, (tokens, LANES), 1) % tokens
+        return key <= position, (key > position) & has_prior
+
+    @pl.when(is_mid)
+    def _():
+        for group, (query_ref, diagonal, others) in enumerate(
+            ((own_ref, 0, ((1, True), (2, False), (3, False))), (end_ref, 1, ((0, False), (2, False), (3, False))))
+        ):
+            for start in range(0, rows, LANES):
+                lanes = pl.ds(start, LANES)
+                state_lanes = pl.ds(group * rows + start, LANES)
+                queries_t = query_ref[0, :, lanes]
+                state = (
+                    jnp.full((1, LANES), NEG, jnp.float32),
+                    jnp.zeros((1, LANES), jnp.float32),
+                    jnp.zeros((cur_ref.shape[4], LANES), jnp.float32),
+                )
+                causal, after = masks()
+                state = attend(
+                    scale, cur_ref[diagonal, 0, 0], cur_ref[diagonal, 0, 1], queries_t, causal, state
+                )
+                state = attend(
+                    scale, prior_ref[diagonal, 0, 0], prior_ref[diagonal, 0, 1], queries_t, after, state
+                )
+                peak_ref[0, :, state_lanes], total_ref[0, :, state_lanes], accum_ref[0, :, state_lanes] = state
+            for tile, low_is_cur in others:
+                is_cur = low == low_is_cur
+
+                @pl.when(is_cur | has_prior)
+                def _(tile=tile, is_cur=is_cur, group=group, query_ref=query_ref):
+                    keys = jnp.where(is_cur, cur_ref[tile, 0, 0], prior_ref[tile, 0, 0])
+                    values_t = jnp.where(is_cur, cur_ref[tile, 0, 1], prior_ref[tile, 0, 1])
+                    for start in range(0, rows, LANES):
+                        lanes = pl.ds(start, LANES)
+                        state_lanes = pl.ds(group * rows + start, LANES)
+                        state = (
+                            peak_ref[0, :, state_lanes],
+                            total_ref[0, :, state_lanes],
+                            accum_ref[0, :, state_lanes],
+                        )
+                        state = attend(scale, keys, values_t, query_ref[0, :, lanes], None, state)
+                        peak_ref[0, :, state_lanes], total_ref[0, :, state_lanes], accum_ref[0, :, state_lanes] = state
+
+
+def attend_new(scale, who, cur, prior, own_t, end_t):
+    tiles, heads, _, tokens, width = cur.shape
+    rows = own_t.shape[2]
+    kv_spec = pl.BlockSpec((tiles, 1, 2, tokens, width), lambda head: (0, head, 0, 0, 0))
+    query_spec = pl.BlockSpec((1, width, rows), lambda head: (head, 0, 0))
+    stat_spec = pl.BlockSpec((1, 1, 2 * rows), lambda head: (head, 0, 0))
+    return pl.pallas_call(
+        functools.partial(new_kernel, scale),
+        grid=(heads,),
+        out_shape=(
+            jax.ShapeDtypeStruct((heads, 1, 2 * rows), jnp.float32),
+            jax.ShapeDtypeStruct((heads, 1, 2 * rows), jnp.float32),
+            jax.ShapeDtypeStruct((heads, width, 2 * rows), jnp.float32),
+        ),
+        in_specs=[spec_smem(), kv_spec, kv_spec, query_spec, query_spec],
+        out_specs=(stat_spec, stat_spec, pl.BlockSpec((1, width, 2 * rows), lambda head: (head, 0, 0))),
+        compiler_params=pltpu.CompilerParams(vmem_limit_bytes=VMEM),
+        cost_estimate=pl.CostEstimate(flops=4 * 10 * tokens * heads * rows * width, bytes_accessed=10**7, transcendentals=0),
+    )(who, cur, prior, own_t, end_t)
+
+
+def units_kernel(scale, layout, last, who_ref, plan_ref, own_ref, end_ref, *refs):
+    n_buffer = len(layout)
+    buffers = refs[:n_buffer]
+    peak_in, total_in, accum_in = refs[n_buffer : n_buffer + 3]
+    outs = refs[n_buffer + 3 :]
+    if last:
+        out_own, out_end, peak_ref, total_ref, accum_ref = outs
+    else:
+        peak_ref, total_ref, accum_ref = outs
+    rows = own_ref.shape[2]
+    heads = own_ref.shape[0]
+
+    @pl.when(who_ref[6] == 1)
+    def _():
+        peak_ref[...] = peak_in[...]
+        total_ref[...] = total_in[...]
+        accum_ref[...] = accum_in[...]
+        for (kind, first), buffer in zip(layout, buffers):
+
+            def item(slot, _, kind=kind, first=first, buffer=buffer):
+                if kind == OWN:
+                    head = plan_ref[OWN, first + slot] % heads
+                else:
+                    head = plan_ref[kind, first + slot]
+
+                @pl.when(head >= 0)
+                def _():
+                    keys, values_t = buffer[slot, 0], buffer[slot, 1]
+                    for group, query_ref in enumerate((own_ref, end_ref)):
+                        for start in range(0, rows, LANES):
+                            state_lanes = pl.ds(group * rows + start, LANES)
+                            state = (
+                                peak_ref[head, :, state_lanes],
+                                total_ref[head, :, state_lanes],
+                                accum_ref[head, :, state_lanes],
+                            )
+                            state = attend(
+                                scale, keys, values_t, query_ref[head, :, pl.ds(start, LANES)], None, state
+                            )
+                            (
+                                peak_ref[head, :, state_lanes],
+                                total_ref[head, :, state_lanes],
+                                accum_ref[head, :, state_lanes],
+                            ) = state
+
+                return 0
+
+            size = buffer.shape[0]
+            if kind == RECV:
+                used = plan_ref[COUNT, 2]
+            else:
+                used = plan_ref[COUNT, 0 if kind == OWN else 1]
+            lax.fori_loop(0, jnp.clip(used - first, 0, size), item, 0)
+        if last:
+            tokens, width = out_own.shape[0], accum_ref.shape[1]
+            group_size = rows // tokens
+            for group, out_ref in enumerate((out_own, out_end)):
+                for head in range(heads):
+                    for member in range(group_size):
+                        lanes = pl.ds(group * rows + member * tokens, tokens)
+                        result = accum_ref[head, :, lanes] / total_ref[head, :, lanes]
+                        out_ref[:, pl.ds((head * group_size + member) * width, width)] = (
+                            result.T.astype(jnp.bfloat16)
+                        )
+
+
+def attend_units(scale, who, plan, own_t, end_t, buffers, state, last, tokens):
+    layout = tuple((kind, first) for kind, first, _ in buffers)
+    arrays = [array for _, _, array in buffers]
+    heads, width, rows = own_t.shape
+    state_shapes = [jax.ShapeDtypeStruct(part.shape, part.dtype) for part in state]
+    outs = []
+    scratch = []
+    if last:
+        outs = [jax.ShapeDtypeStruct((tokens, heads * rows // tokens * width), jnp.bfloat16)] * 2
+        scratch = [pltpu.VMEM(part.shape, part.dtype) for part in state]
+    else:
+        outs = state_shapes
+    n_units = sum(array.shape[0] for array in arrays)
+    return pl.pallas_call(
+        functools.partial(units_kernel, scale, layout, last),
+        out_shape=tuple(outs),
+        in_specs=[spec_smem(), spec_smem()] + [spec_vmem()] * (2 + len(arrays) + 3),
+        out_specs=tuple([spec_vmem()] * len(outs)),
+        scratch_shapes=scratch,
+        compiler_params=pltpu.CompilerParams(vmem_limit_bytes=VMEM),
+        cost_estimate=pl.CostEstimate(
+            flops=8 * n_units * 128 * rows * width, bytes_accessed=10**7, transcendentals=0
+        ),
+    )(who, plan, own_t, end_t, *arrays, *state)
+
+
+def line_of_four(query, new_keys, new_values, memory_keys, memory_values, retrieved):
+    queries = query[0]
+    tokens, heads, group_size, width = queries.shape
+    units_dev = memory_keys.shape[0]
+    scale = math.log2(math.e) / math.sqrt(width)
+    me = lax.axis_index("mem")
+    span = lax.axis_index("span")
+    low = (me < 2).astype(jnp.int32)
+    is_mid = ((me == 1) | (me == 2)).astype(jnp.int32)
+    end = jnp.where(low == 1, 0, 3)
+    who = jnp.stack(
+        [me, end, 3 - me, 3 - end, low, (span > 0).astype(jnp.int32), is_mid, jnp.int32(0)]
+    ).astype(jnp.int32)
+
+    def inward(value):
+        return lax.ppermute(value, "mem", [(0, 1), (3, 2)])
+
+    def across(value):
+        return lax.ppermute(value, "mem", [(1, 2), (2, 1)])
+
+    def far(value):
+        return lax.ppermute(value, "mem", [(0, 2), (3, 1)])
+
+    plan = make_plan(who, retrieved[0], units_dev, CHUNKS[0])
+    keys = memory_keys.reshape(units_dev, -1, width)
+    values = memory_values.reshape(units_dev, -1, width)
+    unit_tokens = memory_keys.shape[1]
+    own, first = [], 0
+    for count in PIECES:
+        own.append(gather(plan, keys, values, unit_tokens, first, count))
+        first += count
+    ends = [inward(piece) for piece in own]
+    own_t = jnp.transpose(queries, (1, 3, 2, 0)).reshape(heads, width, group_size * tokens)
+    end_t = inward(own_t)
+
+    tile = jnp.stack(
+        [jnp.transpose(new_keys[0], (1, 0, 2)), jnp.transpose(new_values[0], (1, 2, 0))], axis=1
+    )
+    cur = jnp.stack([tile, inward(tile), across(tile), far(tile)])
+    prior = lax.ppermute(cur, "span", [(at, at + 1) for at in range(lax.axis_size("span") - 1)])
+
+    arrived = [across(own[0])]
+    first = CHUNKS[0]
+    for count in CHUNKS[1:]:
+        arrived.append(across(pack(plan, own, ends, first, count)))
+        first += count
+
+    state = attend_new(scale, who, cur, prior, own_t, end_t)
+    one = [(OWN, 0, own[0]), (OWN, PIECES[0], own[1]), (OWN, PIECES[0] + PIECES[1], own[2]), (RECV, 0, arrived[0])]
+    state = attend_units(scale, who, plan, own_t, end_t, one, state, False, tokens)
+    two = [(END, 0, ends[0]), (END, PIECES[0], ends[1]), (RECV, CHUNKS[0], arrived[1])]
+    state = attend_units(scale, who, plan, own_t, end_t, two, state, False, tokens)
+    three = [(END, PIECES[0] + PIECES[1], ends[2]), (RECV, CHUNKS[0] + CHUNKS[1], arrived[2])]
+    out_own, out_end = attend_units(scale, who, plan, own_t, end_t, three, state, True, tokens)
+
+    returned = lax.ppermute(out_end, "mem", [(1, 0), (2, 3)])
+    rows = jnp.where(is_mid == 1, out_own, returned)
+    moved = lax.all_to_all(rows, "head", split_axis=0, concat_axis=1, tiled=True)
+    return moved[None]
 
 
 def shifted(value, axis, steps):
@@ -14,7 +427,7 @@
     return lax.ppermute(value, axis, [(source, source + steps) for source in range(first, last)])
 
 
-def local(query, new_keys, new_values, memory_keys, memory_values, retrieved):
+def any_line(query, new_keys, new_values, memory_keys, memory_values, retrieved):
     queries = query[0]
     row_count, head_count, group_size, head_width = queries.shape
     score_scale = 1.0 / math.sqrt(head_width)
@@ -105,6 +518,7 @@
 
 
 def solution(mesh):
+    local = line_of_four if mesh.shape["mem"] == 4 and mesh.shape["head"] == 2 else any_line
     return jax.shard_map(
         local,
         mesh=mesh,

time: 306 us -> 294 us (0.961)
  Pallas kernels: 0 us -> 172 us
  waiting for transfers between devices: 159 us -> 72 us
  matrix products: 45.2 us -> 0 us
  local copies, waits for them, and re-layouts: 47.1 us -> 10.8 us
  starting transfers between devices: 3.76 us -> 20.3 us
  other arithmetic: 16.6 us -> 3.32 us
  between operations: 13.4 us -> 0.27 us
    pallas_call x0 -> x10, Pallas kernels: none -> 172 us  [the longest x2 67.7 us: pack(): pl.pallas_call(functools.partial(pack_kernel, first, count, sizes), out_s...]
    psum x1 -> x0, waiting for transfers between devices: 144 us -> none  [local(): lax.psum(slot_terms, 'mem').astype(jnp.float32).astype(jnp.bfloat16)]
    ppermute x1 -> x12, waiting for transfers between devices: 2.91 us -> 72 us  [the longest x5 29.7 us: inward(): return lax.ppermute(value, 'mem', [(0, 1), (3, 2)])]
    dot_general x12 -> x0, matrix products: 45.2 us -> none  [the longest x6 27.3 us: update(): jnp.einsum('rhgk,khd->rhgd', weights.astype(jnp.bfloat16), key_pair[1], p...]
    gather x16 -> x0, local copies, waits for them, and re-layouts: 25.5 us -> none  [local(): source_array[local_units[head_at], :, head_at, :]]
    ppermute x1 -> x12, starting transfers between devices: 3.68 us -> 20.3 us  [the longest x4 9.26 us: across(): return lax.ppermute(value, 'mem', [(1, 2), (2, 1)])]
    while x12 -> x0, local copies, waits for them, and re-layouts: 12.8 us -> none
    all_gather x2 -> x0, waiting for transfers between devices: 12.7 us -> none  [the longest x1 12.7 us: local(): lax.all_gather(prior_pair, 'mem', axis=1, tiled=True)]
  transfers between devices with their start and end apart: 4 -> 12, of which waited for: 3 -> 5; matrix products, arithmetic and copies ran while one was open for 16% -> 2% of each run, Pallas kernels for 0% -> 51%
where the time goes in v1:
time: 294 us; the launch traced here: 292 us
  Pallas kernels  172 us (59%)
  waiting for transfers between devices  72 us (24%)
  starting transfers between devices  20.3 us (7%)
  blocking collectives  13.2 us (4%)
  local copies, waits for them, and re-layouts  10.8 us (4%)
  other arithmetic  3.32 us (1%)
    pallas_call x2, Pallas kernels, pack(): pl.pallas_call(functools.partial(pack_kernel, first, count, sizes), out_s...  67.7 us
    pallas_call x3, Pallas kernels, attend_units(): pl.pallas_call(functools.partial(units_kernel, scale, layout, last), out_...  58.4 us
    ppermute x5, waiting for transfers between devices, inward(): return lax.ppermute(value, 'mem', [(0, 1), (3, 2)])  29.7 us
    pallas_call x3, Pallas kernels, gather(): pl.pallas_call(functools.partial(gather_kernel, first), out_shape=jax.Sha...  25.1 us
    ppermute x4, waiting for transfers between devices, across(): return lax.ppermute(value, 'mem', [(1, 2), (2, 1)])  23 us
    ppermute x1, waiting for transfers between devices, line_of_four(): returned = lax.ppermute(out_end, 'mem', [(1, 0), (2, 3)])  19.3 us
    pallas_call x1, Pallas kernels, attend_new(): pl.pallas_call(functools.partial(new_kernel, scale), grid=(heads,), out_s...  15.2 us
    all_to_all x1, blocking collectives, line_of_four(): lax.all_to_all(rows, 'head', split_axis=0, concat_axis=1, tiled=True)  13.2 us
  transfers between devices with their start and end apart: 12, of which 5 were waited for; matrix products, arithmetic and copies ran while one was open for 2% of the time, Pallas kernels for 51%

profile of v1, /device:TPU:17, one launch (start us, length us, event | category | flops | bytes accessed | tf_op | source)
XLA Modules:
  0.0 292.0 jit_solution(5009466918631907181)
XLA Ops:
  0.0 0.7 stack.59.who_ref
  0.7 5.6 %shard_map.64.plan_ref = s32[5,128]{1,0:T(8,128)} custom-call(s32[8]{0:T(128)} %stack.59.who_ref, s32[4,16]{1,0:T(4,128)} %bitcast.45), custom_call_target="tpu_custom_call" | custom-call | tf_op jit(solution)/shard_map/pallas_call | solution.py:103
  6.3 0.0 copy-start.5
  6.4 0.0 copy-start.6
  6.4 11.0 %shard_map.65.refs_2_ = bf16[16,2,128,128]{3,2,1,0:T(8,128)(2,1)} custom-call(s32[5,128]{1,0:T(8,128)} %shard_map.64.plan_ref, bf16[32,512,128]{2,1,0:T(8,128)(2,1)} %bitcast.34, bf16[32,512,128]{2,1,0:T(8,128)(2,1)} %bitcast.37), custom_call_target="tpu_custom_call" | custom-call | tf_op jit(solution)/shard_map/pallas_call | solution.py:138
  17.3 1.3 collective-permute-start.1
  18.6 0.0 copy-done.5
  18.6 0.1 copy.9
  18.8 0.0 copy-done.6
  18.8 0.7 fusion
  19.6 1.3 collective-permute-start.7
  20.8 1.9 collective-permute-start.8
  22.8 1.3 collective-permute-start.9
  24.1 7.0 %shard_map.66.refs_0_ = bf16[8,2,128,128]{3,2,1,0:T(8,128)(2,1)} custom-call(s32[5,128]{1,0:T(8,128)} %shard_map.64.plan_ref, bf16[32,512,128]{2,1,0:T(8,128)(2,1)} %bitcast.35, bf16[32,512,128]{2,1,0:T(8,128)(2,1)} %bitcast.38), custom_call_target="tpu_custom_call" | custom-call | tf_op jit(solution)/shard_map/pallas_call | solution.py:138
  31.1 1.3 collective-permute-start.2
  32.4 7.0 %shard_map.67.refs_1_ = bf16[8,2,128,128]{3,2,1,0:T(8,128)(2,1)} custom-call(s32[5,128]{1,0:T(8,128)} %shard_map.64.plan_ref, bf16[32,512,128]{2,1,0:T(8,128)(2,1)} %bitcast.36, bf16[32,512,128]{2,1,0:T(8,128)(2,1)} %bitcast.39), custom_call_target="tpu_custom_call" | custom-call | tf_op jit(solution)/shard_map/pallas_call | solution.py:138
  39.5 10.8 %collective-permute-done.7 = bf16[4,2,128,128]{3,2,1,0:T(8,128)(2,1)} collective-permute-done((bf16[4,2,128,128]{3,2,1,0:T(8,128)(2,1)}, bf16[4,2,128,128]{3,2,1,0:T(8,128)(2,1)}, u32[]{:S(2)}, u32[]{:S(2)}) %collective-permute-start.7) | collective-permute-done | bytes 262176 | tf_op jit(solution)/shard_map/ppermute | solution.py:378
  50.3 1.3 collective-permute-start.3
  51.6 2.2 copy.7
  53.8 1.3 reshape.13.own_ref
  55.1 0.0 collective-permute-done.8
  55.1 1.3 collective-permute-start
  56.4 0.0 collective-permute-done.9
  56.4 1.2 pad_maximum_fusion.cur_ref
  57.6 0.0 copy-start.4
  57.6 2.0 collective-permute-start.10
  59.7 7.5 %collective-permute-done.2.refs_3_.refs_0_ = bf16[8,2,128,128]{3,2,1,0:T(8,128)(2,1)S(1)} collective-permute-done((bf16[8,2,128,128]{3,2,1,0:T(8,128)(2,1)}, bf16[8,2,128,128]{3,2,1,0:T(8,128)(2,1)S(1)}, u32[]{:S(2)}, u32[]{:S(2)}) %collective-permute-start.2) | collective-permute-done | bytes 524320 | tf_op jit(solution)/shard_map/ppermute | solution.py:378
  67.1 0.0 copy-start.2
  67.1 11.3 %collective-permute-done.3.refs_4_.refs_1_ = bf16[8,2,128,128]{3,2,1,0:T(8,128)(2,1)S(1)} collective-permute-done((bf16[8,2,128,128]{3,2,1,0:T(8,128)(2,1)}, bf16[8,2,128,128]{3,2,1,0:T(8,128)(2,1)S(1)}, u32[]{:S(2)}, u32[]{:S(2)}) %collective-permute-start.3) | collective-permute-done | bytes 524320 | tf_op jit(solution)/shard_map/ppermute | solution.py:378
  78.5 0.0 copy-start.3
  78.5 0.0 collective-permute-done.1.refs_5_.refs_0_
  78.5 0.0 copy-done.2
  78.5 0.8 copy-done.3
  79.3 0.0 copy-start.1
  79.3 1.0 copy-done.1
  80.3 18.0 %shard_map.68 = bf16[32,2,128,128]{3,2,1,0:T(8,128)(2,1)} custom-call(s32[5,128]{1,0:T(8,128)} %shard_map.64.plan_ref, bf16[8,2,128,128]{3,2,1,0:T(8,128)(2,1)} %shard_map.66.refs_0_, bf16[8,2,128,128]{3,2,1,0:T(8,128)(2,1)} %shard_map.67.refs_1_, bf16[16,2,128,128]{3,2,1,0:T(8,128)(2,1)} %shard_map.65.refs_2_, bf16[8,2,128,128]{3,2,1,0:T(8,128)(2,1)} %copy-done.2, ...), custom_call_target="tpu_custom_call" | custom-call | tf_op jit(solution)/shard_map/pallas_call | solution.py:175
  98.3 0.0 copy-start
  98.3 2.1 collective-permute-start.4
  100.4 49.7 %shard_map.69 = bf16[24,2,128,128]{3,2,1,0:T(8,128)(2,1)} custom-call(s32[5,128]{1,0:T(8,128)} %shard_map.64.plan_ref, bf16[8,2,128,128]{3,2,1,0:T(8,128)(2,1)} %shard_map.66.refs_0_, bf16[8,2,128,128]{3,2,1,0:T(8,128)(2,1)} %shard_map.67.refs_1_, bf16[16,2,128,128]{3,2,1,0:T(8,128)(2,1)} %shard_map.65.refs_2_, bf16[8,2,128,128]{3,2,1,0:T(8,128)(2,1)} %copy-done.2, ...), custom_call_target="tpu_custom_call" | custom-call | tf_op jit(solution)/shard_map/pallas_call | solution.py:175
  150.1 1.9 collective-permute-start.5
  152.0 0.0 copy-done
  152.0 3.4 %collective-permute-start.6 = (bf16[8,2,128,128]{3,2,1,0:T(8,128)(2,1)S(1)}, bf16[8,2,128,128]{3,2,1,0:T(8,128)(2,1)S(1)}, u32[]{:S(2)}, u32[]{:S(2)}) collective-permute-start(bf16[8,2,128,128]{3,2,1,0:T(8,128)(2,1)S(1)} %copy-done), channel_id=1, source_target_pairs={{8,16},{16,8},{9,17},{17,9},{10,18},{18,10},{11,19},{19,11},{12,20... | collective-permute-start | bytes 1572872 | tf_op jit(solution)/shard_map/ppermute | solution.py:381
  155.4 0.0 collective-permute-done.end_ref
  155.4 0.0 collective-permute-done.10.prior_ref
  155.4 0.0 copy-done.4
  155.4 15.2 %shard_map.70 = (f32[4,1,2048]{2,1,0:T(1,128)}, f32[4,1,2048]{2,1,0:T(1,128)}, f32[4,128,2048]{2,1,0:T(8,128)}) custom-call(s32[8]{0:T(128)} %stack.59.who_ref, bf16[4,4,2,128,128]{4,3,2,1,0:T(8,128)(2,1)} %copy-done.4, bf16[4,4,2,128,128]{4,3,2,1,0:T(8,128)(2,1)} %collective-permute-done.10.prior_ref, bf16[4,128,1024]{2,1,0:T(8,128)(2,1)} %reshape.13.own_ref, ...), custom_call_target="tpu_custom_call" | custom-call | flops 2684354560 | bytes 10000000 | tf_op jit(solution)/shard_map/pallas_call | solution.py:256
  170.6 23.0 %collective-permute-done.6.refs_3_ = bf16[8,2,128,128]{3,2,1,0:T(8,128)(2,1)S(1)} collective-permute-done((bf16[8,2,128,128]{3,2,1,0:T(8,128)(2,1)S(1)}, bf16[8,2,128,128]{3,2,1,0:T(8,128)(2,1)S(1)}, u32[]{:S(2)}, u32[]{:S(2)}) %collective-permute-start.6) | collective-permute-done | bytes 524320 | tf_op jit(solution)/shard_map/ppermute | solution.py:381
  193.6 0.0 copy-start.8
  193.6 0.8 copy-done.8
  194.4 28.6 %shard_map.71 = (f32[4,1,2048]{2,1,0:T(1,128)}, f32[4,1,2048]{2,1,0:T(1,128)}, f32[4,128,2048]{2,1,0:T(8,128)}) custom-call(s32[8]{0:T(128)} %stack.59.who_ref, s32[5,128]{1,0:T(8,128)} %shard_map.64.plan_ref, bf16[4,128,1024]{2,1,0:T(8,128)(2,1)} %reshape.13.own_ref, bf16[4,128,1024]{2,1,0:T(8,128)(2,1)} %collective-permute-done.end_ref, ...), custom_call_target="tpu_custom_call" | custom-call | flops 5368709120 | bytes 10000000 | tf_op jit(solution)/shard_map/pallas_call | solution.py:350
  223.0 0.0 collective-permute-done.5.refs_2_
  223.0 0.0 copy-start.7
  223.0 1.2 copy-done.7
  224.2 23.8 %shard_map.72 = (f32[4,1,2048]{2,1,0:T(1,128)}, f32[4,1,2048]{2,1,0:T(1,128)}, f32[4,128,2048]{2,1,0:T(8,128)}) custom-call(s32[8]{0:T(128)} %stack.59.who_ref, s32[5,128]{1,0:T(8,128)} %shard_map.64.plan_ref, bf16[4,128,1024]{2,1,0:T(8,128)(2,1)} %reshape.13.own_ref, bf16[4,128,1024]{2,1,0:T(8,128)(2,1)} %collective-permute-done.end_ref, ...), custom_call_target="tpu_custom_call" | custom-call | flops 5368709120 | bytes 10000000 | tf_op jit(solution)/shard_map/pallas_call | solution.py:350
  247.9 0.0 collective-permute-done.4.refs_1_
  247.9 6.1 %shard_map.73 = (bf16[128,4096]{1,0:T(8,128)(2,1)}, bf16[128,4096]{1,0:T(8,128)(2,1)}) custom-call(s32[8]{0:T(128)} %stack.59.who_ref, s32[5,128]{1,0:T(8,128)} %shard_map.64.plan_ref, bf16[4,128,1024]{2,1,0:T(8,128)(2,1)} %reshape.13.own_ref, bf16[4,128,1024]{2,1,0:T(8,128)(2,1)} %collective-permute-done.end_ref, bf16[16,2,128,128]{3,2,1,0:T(8,128)(2,1)} %copy-done.1, ...), custom_call_target="tpu_custom_call" | custom-call | flops 6442450944 | bytes 10000000 | tf_op jit(solution)/shard_map/pallas_call | solution.py:350
  254.0 1.3 collective-permute-start.11
  255.4 19.3 %collective-permute-done.11 = bf16[128,4096]{1,0:T(8,128)(2,1)S(1)} collective-permute-done((bf16[128,4096]{1,0:T(8,128)(2,1)}, bf16[128,4096]{1,0:T(8,128)(2,1)S(1)}, u32[]{:S(2)}, u32[]{:S(2)}) %collective-permute-start.11) | collective-permute-done | bytes 1048608 | tf_op jit(solution)/shard_map/ppermute | solution.py:418
  274.7 1.3 broadcast_select_fusion
  276.1 13.2 %all_to_all.16 = bf16[2,64,4096]{2,1,0:T(8,128)(2,1)S(1)} all-to-all(bf16[2,64,4096]{2,1,0:T(8,128)(2,1)S(1)} %bitcast.40), channel_id=1, replica_groups=mesh['mem'=4,'head'=2,'span'=4] {'head'}, dimensions={0} | all-to-all | bytes 2097152 | tf_op jit(solution)/shard_map/all_to_all | solution.py:420
  289.3 1.1 copy.10
  290.4 1.6 broadcast_in_dim.3
  (1 shorter events, 0.0 us)
Async XLA Ops:
  6.3 12.3 %copy-start.5 = (bf16[1,128,4,128]{3,2,1,0:T(4,128)(2,1)S(1)}, bf16[1,128,4,128]{3,2,1,0:T(4,128)(2,1)}, u32[]{:S(2)}) copy-start(bf16[1,128,4,128]{3,2,1,0:T(4,128)(2,1)} %param.8) | copy-start | bytes 393220
  6.4 12.4 %copy-start.6 = (bf16[1,128,4,128]{3,2,1,0:T(4,128)(2,1)S(1)}, bf16[1,128,4,128]{3,2,1,0:T(4,128)(2,1)}, u32[]{:S(2)}) copy-start(bf16[1,128,4,128]{3,2,1,0:T(4,128)(2,1)} %param.7) | copy-start | bytes 393220
  17.3 61.1 %collective-permute-start.1 = (bf16[16,2,128,128]{3,2,1,0:T(8,128)(2,1)}, bf16[16,2,128,128]{3,2,1,0:T(8,128)(2,1)S(1)}, u32[]{:S(2)}, u32[]{:S(2)}) collective-permute-start(bf16[16,2,128,128]{3,2,1,0:T(8,128)(2,1)} %shard_map.65.refs_2_), channel_id=1, source_target_pairs={{0,8},{24,16},{1,9},{25,17},{2,10},{26,18},{3,11},{27,19},{4,12},{... | collective-permute-start | bytes 3145736 | tf_op jit(solution)/shard_map/ppermute | solution.py:378
  19.6 30.7 %collective-permute-start.7 = (bf16[4,2,128,128]{3,2,1,0:T(8,128)(2,1)}, bf16[4,2,128,128]{3,2,1,0:T(8,128)(2,1)}, u32[]{:S(2)}, u32[]{:S(2)}) collective-permute-start(bf16[4,2,128,128]{3,2,1,0:T(8,128)(2,1)} %get-tuple-element.28), channel_id=1, source_target_pairs={{0,8},{24,16},{1,9},{25,17},{2,10},{26,18},{3,11},{27,19},{4,12},{... | collective-permute-start | bytes 786440 | tf_op jit(solution)/shard_map/ppermute | solution.py:378
  20.8 34.2 %collective-permute-start.8 = (bf16[4,2,128,128]{3,2,1,0:T(8,128)(2,1)}, bf16[4,2,128,128]{3,2,1,0:T(8,128)(2,1)}, u32[]{:S(2)}, u32[]{:S(2)}) collective-permute-start(bf16[4,2,128,128]{3,2,1,0:T(8,128)(2,1)} %get-tuple-element.28), channel_id=1, source_target_pairs={{8,16},{16,8},{9,17},{17,9},{10,18},{18,10},{11,19},{19,11},{12,20... | collective-permute-start | bytes 786440 | tf_op jit(solution)/shard_map/ppermute | solution.py:381
  22.8 33.6 %collective-permute-start.9 = (bf16[4,2,128,128]{3,2,1,0:T(8,128)(2,1)}, bf16[4,2,128,128]{3,2,1,0:T(8,128)(2,1)}, u32[]{:S(2)}, u32[]{:S(2)}) collective-permute-start(bf16[4,2,128,128]{3,2,1,0:T(8,128)(2,1)} %get-tuple-element.28), channel_id=1, source_target_pairs={{0,16},{24,8},{1,17},{25,9},{2,18},{26,10},{3,19},{27,11},{4,20},{... | collective-permute-start | bytes 786440 | tf_op jit(solution)/shard_map/ppermute | solution.py:384
  31.1 36.0 %collective-permute-start.2 = (bf16[8,2,128,128]{3,2,1,0:T(8,128)(2,1)}, bf16[8,2,128,128]{3,2,1,0:T(8,128)(2,1)S(1)}, u32[]{:S(2)}, u32[]{:S(2)}) collective-permute-start(bf16[8,2,128,128]{3,2,1,0:T(8,128)(2,1)} %shard_map.66.refs_0_), channel_id=1, source_target_pairs={{0,8},{24,16},{1,9},{25,17},{2,10},{26,18},{3,11},{27,19},{4,12},{... | collective-permute-start | bytes 1572872 | tf_op jit(solution)/shard_map/ppermute | solution.py:378
  50.3 28.2 %collective-permute-start.3 = (bf16[8,2,128,128]{3,2,1,0:T(8,128)(2,1)}, bf16[8,2,128,128]{3,2,1,0:T(8,128)(2,1)S(1)}, u32[]{:S(2)}, u32[]{:S(2)}) collective-permute-start(bf16[8,2,128,128]{3,2,1,0:T(8,128)(2,1)} %shard_map.67.refs_1_), channel_id=1, source_target_pairs={{0,8},{24,16},{1,9},{25,17},{2,10},{26,18},{3,11},{27,19},{4,12},{... | collective-permute-start | bytes 1572872 | tf_op jit(solution)/shard_map/ppermute | solution.py:378
  55.1 100.3 %collective-permute-start = (bf16[4,128,1024]{2,1,0:T(8,128)(2,1)}, bf16[4,128,1024]{2,1,0:T(8,128)(2,1)}, u32[]{:S(2)}, u32[]{:S(2)}) collective-permute-start(bf16[4,128,1024]{2,1,0:T(8,128)(2,1)} %reshape.13.own_ref), channel_id=1, source_target_pairs={{0,8},{24,16},{1,9},{25,17},{2,10},{26,18},{3,11},{27,19},{4,12},{... | collective-permute-start | bytes 3145736 | tf_op jit(solution)/shard_map/ppermute | solution.py:378
  57.6 97.8 %copy-start.4 = (bf16[4,4,2,128,128]{4,3,2,1,0:T(8,128)(2,1)}, bf16[4,4,2,128,128]{4,3,2,1,0:T(8,128)(2,1)S(1)}, u32[]{:S(2)}) copy-start(bf16[4,4,2,128,128]{4,3,2,1,0:T(8,128)(2,1)S(1)} %pad_maximum_fusion.cur_ref) | copy-start | bytes 3145732
  57.6 97.8 %collective-permute-start.10 = (bf16[4,4,2,128,128]{4,3,2,1,0:T(8,128)(2,1)S(1)}, bf16[4,4,2,128,128]{4,3,2,1,0:T(8,128)(2,1)}, u32[]{:S(2)}, u32[]{:S(2)}) collective-permute-start(bf16[4,4,2,128,128]{4,3,2,1,0:T(8,128)(2,1)S(1)} %pad_maximum_fusion.cur_ref), channel_id=1, source_target_pairs={{0,1},{1,2},{2,3},{4,5},{5,6},{6,7},{8,9},{9,10},{10,11},{12,13},{... | collective-permute-start | bytes 3145736 | tf_op jit(solution)/shard_map/ppermute | solution.py:402
  67.1 11.3 %copy-start.2 = (bf16[8,2,128,128]{3,2,1,0:T(8,128)(2,1)}, bf16[8,2,128,128]{3,2,1,0:T(8,128)(2,1)S(1)}, u32[]{:S(2)}) copy-start(bf16[8,2,128,128]{3,2,1,0:T(8,128)(2,1)S(1)} %collective-permute-done.2.refs_3_.refs_0_) | copy-start | bytes 1572868
  78.5 0.8 copy-start.3
  79.3 1.0 copy-start.1
  98.3 53.7 %copy-start = (bf16[8,2,128,128]{3,2,1,0:T(8,128)(2,1)S(1)}, bf16[8,2,128,128]{3,2,1,0:T(8,128)(2,1)}, u32[]{:S(2)}) copy-start(bf16[8,2,128,128]{3,2,1,0:T(8,128)(2,1)} %shard_map.66.refs_0_) | copy-start | bytes 1572868
  98.3 149.6 %collective-permute-start.4 = (bf16[32,2,128,128]{3,2,1,0:T(8,128)(2,1)}, bf16[32,2,128,128]{3,2,1,0:T(8,128)(2,1)}, u32[]{:S(2)}, u32[]{:S(2)}) collective-permute-start(bf16[32,2,128,128]{3,2,1,0:T(8,128)(2,1)} %shard_map.68), channel_id=1, source_target_pairs={{8,16},{16,8},{9,17},{17,9},{10,18},{18,10},{11,19},{19,11},{12,20... | collective-permute-start | bytes 6291464 | tf_op jit(solution)/shard_map/ppermute | solution.py:381
  150.1 72.9 %collective-permute-start.5 = (bf16[24,2,128,128]{3,2,1,0:T(8,128)(2,1)}, bf16[24,2,128,128]{3,2,1,0:T(8,128)(2,1)S(1)}, u32[]{:S(2)}, u32[]{:S(2)}) collective-permute-start(bf16[24,2,128,128]{3,2,1,0:T(8,128)(2,1)} %shard_map.69), channel_id=1, source_target_pairs={{8,16},{16,8},{9,17},{17,9},{10,18},{18,10},{11,19},{19,11},{12,20... | collective-permute-start | bytes 4718600 | tf_op jit(solution)/shard_map/ppermute | solution.py:381
  152.0 41.6 %collective-permute-start.6 = (bf16[8,2,128,128]{3,2,1,0:T(8,128)(2,1)S(1)}, bf16[8,2,128,128]{3,2,1,0:T(8,128)(2,1)S(1)}, u32[]{:S(2)}, u32[]{:S(2)}) collective-permute-start(bf16[8,2,128,128]{3,2,1,0:T(8,128)(2,1)S(1)} %copy-done), channel_id=1, source_target_pairs={{8,16},{16,8},{9,17},{17,9},{10,18},{18,10},{11,19},{19,11},{12,20... | collective-permute-start | bytes 1572872 | tf_op jit(solution)/shard_map/ppermute | solution.py:381
  193.6 0.8 copy-start.8
  223.0 1.2 copy-start.7
  254.0 20.7 %collective-permute-start.11 = (bf16[128,4096]{1,0:T(8,128)(2,1)}, bf16[128,4096]{1,0:T(8,128)(2,1)S(1)}, u32[]{:S(2)}, u32[]{:S(2)}) collective-permute-start(bf16[128,4096]{1,0:T(8,128)(2,1)} %get-tuple-element.26), channel_id=1, source_target_pairs={{8,0},{16,24},{9,1},{17,25},{10,2},{18,26},{11,3},{19,27},{12,4},{... | collective-permute-start | bytes 3145736 | tf_op jit(solution)/shard_map/ppermute | solution.py:418

commit v2 on v0

--- a/solution.py
+++ b/solution.py
@@ -1,11 +1,598 @@
+import functools
 import math
 
 import jax
 import jax.numpy as jnp
 from jax import lax
+from jax.experimental import pallas as pl
+from jax.experimental.pallas import tpu as pltpu
 from jax.sharding import PartitionSpec as P
 
 NEG = -1e30
+LANES = 128
+VMEM = 56 * 1024 * 1024
+TINY = pl.CostEstimate(flops=1000, bytes_accessed=1000, transcendentals=0)
+AHEAD = 6
+
+PIECES = (16, 16)
+CHUNKS = (16, 16, 16)
+FIRST = 16
+TILE = 4
+
+ME, ENDER, OPPOSITE, FAR, LOW, PRIOR, MIDDLE, GROUP = range(8)
+OWN, END, STREAM, EXTRA = range(4)
+
+
+def smem():
+    return pl.BlockSpec(memory_space=pltpu.SMEM)
+
+
+def vmem():
+    return pl.BlockSpec(memory_space=pltpu.VMEM)
+
+
+def hbm():
+    return pl.BlockSpec(memory_space=pl.ANY)
+
+
+def head_picker(tokens, rows, head):
+    token = lax.broadcasted_iota(jnp.int32, (tokens, rows), 0)
+    row = lax.broadcasted_iota(jnp.int32, (tokens, rows), 1)
+    return (row == token * (rows // tokens) + head).astype(jnp.bfloat16)
+
+
+def pick_pair(pick, keys, values):
+    keys = jnp.dot(pick, keys, preferred_element_type=jnp.float32)
+    values_t = lax.dot_general(
+        values, pick, (((0,), (1,)), ((), ())), preferred_element_type=jnp.float32
+    )
+    return keys.astype(jnp.bfloat16), values_t.astype(jnp.bfloat16)
+
+
+def plan_units(units_dev, who_ref, list_ref, count_ref, table_ref):
+    heads, topk = list_ref.shape
+    me = who_ref[ME]
+
+    def clear(at, _):
+        count_ref[at] = 0
+        return 0
+
+    lax.fori_loop(0, count_ref.shape[0], clear, 0)
+    used = jnp.int32(0)
+    for head in range(heads):
+
+        def note(at, used, head=head):
+            unit = list_ref[head, at]
+            owner = lax.div(unit, jnp.int32(units_dev))
+            entry = owner * heads + head
+            count_ref[entry] = count_ref[entry] + 1
+            table_ref[used] = (unit - owner * units_dev) * heads + head
+            return used + (owner == me).astype(jnp.int32)
+
+        used = lax.fori_loop(0, topk, note, used)
+    table_ref[heads * topk] = used
+
+
+def gather_kernel(units_dev, pieces, first, tile, who_ref, list_ref, keys_ref, values_ref, *refs):
+    refs = list(refs)
+    heads, topk = list_ref.shape
+    if tile:
+        new_keys, new_values, count_ref, table_ref = (refs.pop(0) for _ in range(4))
+        plan_units(units_dev, who_ref, list_ref, count_ref, table_ref)
+    else:
+        table_ref = refs.pop(0)
+    outs = [refs.pop(0) for _ in pieces]
+    key_buf, value_buf, picks, sems = refs
+    rows = keys_ref.shape[1]
+    tokens = rows // heads
+    used = table_ref[heads * topk]
+
+    def copies(at):
+        unit = lax.div(table_ref[at], jnp.int32(heads))
+        slot = lax.rem(at, jnp.int32(AHEAD))
+        return (
+            pltpu.make_async_copy(keys_ref.at[unit], key_buf.at[slot], sems.at[slot, 0]),
+            pltpu.make_async_copy(values_ref.at[unit], value_buf.at[slot], sems.at[slot, 1]),
+        )
+
+    def start(at, _):
+        for copy in copies(at):
+            copy.start()
+        return 0
+
+    stop = jnp.minimum(used, first + sum(pieces))
+    lax.fori_loop(first, jnp.minimum(stop, first + AHEAD), start, 0)
+    for head in range(heads):
+        picks[head] = head_picker(tokens, rows, head)
+    base, place = first, TILE if tile else 0
+    if tile:
+        for head in range(heads):
+            outs[0][head, 0], outs[0][head, 1] = pick_pair(picks[head], new_keys[...], new_values[...])
+    for out_ref, size in zip(outs, pieces):
+
+        def item(slot, _, out_ref=out_ref, base=base, place=place):
+            at = base + slot
+            for copy in copies(at):
+                copy.wait()
+            here = lax.rem(at, jnp.int32(AHEAD))
+            pick = picks[lax.rem(table_ref[at], jnp.int32(heads))]
+            out_ref[place + slot, 0], out_ref[place + slot, 1] = pick_pair(
+                pick, key_buf[here], value_buf[here]
+            )
+
+            @pl.when(at + AHEAD < stop)
+            def _():
+                start(at + AHEAD, 0)
+
+            return 0
+
+        lax.fori_loop(0, jnp.clip(used - base, 0, size), item, 0)
+        base, place = base + size, 0
+
+
+def gather(who, unit_lists, keys, values, pieces, first, tile=None, table=None, n_owner=None):
+    units, rows, width = keys.shape
+    heads, topk = unit_lists.shape
+    tokens = rows // heads
+    extra = [TILE if tile is not None else 0] + [0] * (len(pieces) - 1)
+    tables = [
+        jax.ShapeDtypeStruct((size,), jnp.int32)
+        for size in ([n_owner * heads, heads * topk + 1] if tile is not None else [])
+    ]
+    return pl.pallas_call(
+        functools.partial(gather_kernel, units, pieces, first, tile is not None),
+        out_shape=tuple(
+            tables
+            + [
+                jax.ShapeDtypeStruct((size + more, 2, tokens, width), jnp.bfloat16)
+                for size, more in zip(pieces, extra)
+            ]
+        ),
+        in_specs=[smem(), smem(), hbm(), hbm()] + ([vmem()] * 2 if tile is not None else [smem()]),
+        out_specs=tuple([smem()] * len(tables) + [vmem()] * len(pieces)),
+        scratch_shapes=[
+            pltpu.VMEM((AHEAD, rows, width), jnp.bfloat16),
+            pltpu.VMEM((AHEAD, rows, width), jnp.bfloat16),
+            pltpu.VMEM((heads, tokens, rows), jnp.bfloat16),
+            pltpu.SemaphoreType.DMA((AHEAD, 2)),
+        ],
+        compiler_params=pltpu.CompilerParams(vmem_limit_bytes=VMEM),
+        cost_estimate=TINY,
+    )(who, unit_lists, keys, values, *(tile if tile is not None else (table,)))
+
+
+def head_ranges(count_ref, heads, owner):
+    ranges, at = [], jnp.int32(0)
+    for head in range(heads):
+        after = at + count_ref[owner * heads + head]
+        ranges.append((at, after))
+        at = after
+    return ranges, at
+
+
+def stream_shape(chunks, n_middle, n_end):
+    extra = jnp.maximum(n_middle + n_end - sum(chunks), 0)
+    return extra, jnp.maximum(n_middle - extra, FIRST)
+
+
+def pack_kernel(heads, chunks, first, layout, who_ref, count_ref, *refs):
+    sources = refs[: len(layout)]
+    out_ref, sems = refs[len(layout) :]
+    size = out_ref.shape[0]
+
+    @pl.when(who_ref[MIDDLE] == 1)
+    def _():
+        _, n_own = head_ranges(count_ref, heads, who_ref[ME])
+        _, n_end = head_ranges(count_ref, heads, who_ref[ENDER])
+        extra, base = stream_shape(chunks, n_own, n_end)
+
+        def each(act):
+            for (kind, at, skip), ref in zip(layout, sources):
+                shift, total = (-extra, n_own) if kind == OWN else (base, n_end)
+                count = ref.shape[0] - skip
+                low = jnp.maximum(at + shift, first)
+                high = jnp.minimum(jnp.minimum(at + count, total) + shift, first + size)
+
+                def one(slot, _, ref=ref, shift=shift, at=at, skip=skip):
+                    place = slot - first
+                    act(
+                        pltpu.make_async_copy(
+                            ref.at[slot - shift - at + skip], out_ref.at[place], sems.at[place]
+                        )
+                    )
+                    return 0
+
+                lax.fori_loop(low, jnp.maximum(low, high), one, 0)
+
+        each(lambda copy: copy.start())
+        each(lambda copy: copy.wait())
+
+
+def pack(who, counts, heads, chunks, first, size, sources):
+    layout = tuple(source[:3] for source in sources)
+    arrays = [source[3] for source in sources]
+    return pl.pallas_call(
+        functools.partial(pack_kernel, heads, chunks, first, layout),
+        out_shape=jax.ShapeDtypeStruct((size,) + arrays[0].shape[1:], jnp.bfloat16),
+        in_specs=[smem(), smem()] + [hbm()] * len(arrays),
+        out_specs=vmem(),
+        scratch_shapes=[pltpu.SemaphoreType.DMA((size,))],
+        compiler_params=pltpu.CompilerParams(vmem_limit_bytes=VMEM),
+        cost_estimate=TINY,
+    )(who, counts, *arrays)
+
+
+def attend(scale, keys, values_t, queries_t, mask, state):
+    peak, total, accum = state
+    scores = jnp.dot(keys, queries_t, preferred_element_type=jnp.float32)
+    if mask is not None:
+        scores = jnp.where(mask, scores, NEG)
+    new_peak = jnp.maximum(peak, jnp.max(scores, axis=0, keepdims=True))
+    weights = jnp.exp2((scores - new_peak) * scale)
+    factor = jnp.exp2((peak - new_peak) * scale)
+    total = total * factor + jnp.sum(weights, axis=0, keepdims=True)
+    accum = accum * factor + jnp.dot(
+        values_t, weights.astype(jnp.bfloat16), preferred_element_type=jnp.float32
+    )
+    return new_peak, total, accum
+
+
+def attend_kernel(scale, chunks, layout, n_query, parts, n_state, last, *refs):
+    new = any(part[3] for part in parts)
+    refs = list(refs)
+    who_ref, count_ref = refs.pop(0), refs.pop(0)
+    query_in = [refs.pop(0) for _ in range(n_query)]
+    buffers = [refs.pop(0) for _ in layout]
+    if new:
+        cur_own, cur_rest, prior = (refs.pop(0) for _ in range(3))
+    state_in = [refs.pop(0) for _ in range(n_state)]
+    outs = [refs.pop(0) for _ in range(4 if last else 3)]
+    queries, peak_ref, total_ref, accum_ref, units, unit_sems, state_sems, query_sems = refs
+    state_refs = (peak_ref, total_ref, accum_ref)
+    n_turn, width, rows = queries.shape
+    tokens = units.shape[2]
+    heads = list(count_ref.shape)[0] // 4
+
+    def update(turn, keys, values_t, mask=None):
+        for start in range(0, rows, LANES):
+            lanes = pl.ds(start, LANES)
+            state = tuple(ref[turn, :, lanes] for ref in state_refs)
+            state = attend(scale, keys, values_t, queries[turn, :, lanes], mask, state)
+            for ref, part in zip(state_refs, state):
+                ref[turn, :, lanes] = part
+
+    def new_tiles(turn, head, group):
+        low, has_prior = who_ref[LOW] == 1, who_ref[PRIOR] == 1
+
+        def tile(ref, at=0):
+            return ref[at * TILE + head, 0], ref[at * TILE + head, 1]
+
+        def choose(flag, yes, no):
+            return tuple(jnp.where(flag, a, b) for a, b in zip(yes, no))
+
+        def join(a, b):
+            return jnp.concatenate([a[0], b[0]], axis=0), jnp.concatenate([a[1], b[1]], axis=1)
+
+        key = lax.broadcasted_iota(jnp.int32, (2 * tokens, LANES), 0)
+        position = lax.broadcasted_iota(jnp.int32, (2 * tokens, LANES), 1) % tokens
+        mask = ((key < tokens) & (key <= position)) | (
+            (key >= tokens) & (key - tokens > position) & has_prior
+        )
+
+        def both():
+            pairs = [choose(low, tile(prior, at + 1), tile(cur_rest, at)) for at in (1, 2)]
+            update(turn, *join(*pairs))
+
+        if group == 0:
+            update(turn, *join(tile(cur_own), tile(prior)), mask)
+
+            @pl.when(low | has_prior)
+            def _():
+                update(turn, *choose(low, tile(cur_rest), tile(prior, 1)))
+
+            pl.when(jnp.logical_not(low) | has_prior)(both)
+        else:
+            update(turn, *join(tile(cur_rest), tile(prior, 1)), mask)
+
+            @pl.when(jnp.logical_not(low) | has_prior)
+            def _():
+                update(turn, *choose(low, tile(prior), tile(cur_own)))
+                both()
+
+    @pl.when(who_ref[MIDDLE] == 1)
+    def _():
+        loads = []
+        at = parts[0][0]
+        for number, ref in enumerate(query_in):
+            here = pl.ds(at, ref.shape[0])
+            loads.append(pltpu.make_async_copy(ref, queries.at[here], query_sems.at[number]))
+            at += ref.shape[0]
+        for number, (lowest, highest, _, _, fresh) in enumerate(parts):
+            if not fresh:
+                here = pl.ds(lowest, highest - lowest)
+                loads += [
+                    pltpu.make_async_copy(source.at[here], ref.at[here], state_sems.at[number, at])
+                    for at, (source, ref) in enumerate(zip(state_in, state_refs))
+                ]
+        for load in loads:
+            load.start()
+
+        ranges, totals = zip(
+            *(head_ranges(count_ref, heads, who_ref[role]) for role in (ME, ENDER, OPPOSITE, FAR))
+        )
+        extra, base = stream_shape(chunks, totals[2], totals[3])
+        n_stage = max(entry[3] for entry in layout) + 1
+        place, bounds = jnp.int32(0), []
+        for head in range(heads):
+            stage_at = -1
+            for (kind, first, skip, stage), buffer in zip(layout, buffers):
+                while stage_at < stage:
+                    stage_at += 1
+                    bounds.append(place)
+                if kind == STREAM:
+                    low, high = ranges[2][head]
+                    spans = [
+                        (low, jnp.minimum(high, FIRST)),
+                        (jnp.maximum(low, FIRST + extra) - extra, high - extra),
+                    ]
+                    low, high = ranges[3][head]
+                    spans.append((base + low, base + high))
+                elif kind == EXTRA:
+                    low, high = ranges[2][head]
+                    spans = [(jnp.maximum(low, FIRST), jnp.minimum(high, FIRST + extra))]
+                else:
+                    spans = [ranges[0 if kind == OWN else 1][head]]
+                for low, high in spans:
+                    low = jnp.maximum(low - first, 0)
+                    high = jnp.maximum(jnp.minimum(high - first, buffer.shape[0] - skip), low)
+
+                    def fetch(at, _, buffer=buffer, skip=skip, shift=place - low):
+                        slot = at + shift
+                        pltpu.make_async_copy(
+                            buffer.at[at + skip], units.at[slot], unit_sems.at[slot]
+                        ).start()
+                        return 0
+
+                    lax.fori_loop(low, high, fetch, 0)
+                    place = place + high - low
+            bounds.append(place)
+
+        def arrived(slot, _):
+            pltpu.make_async_copy(buffers[0].at[0], units.at[slot], unit_sems.at[slot]).wait()
+            return 0
+
+        lax.fori_loop(0, place, arrived, 0)
+        for load in loads:
+            load.wait()
+
+        def one_turn(turn, _, group, stage, tiles, fresh):
+            head = lax.rem(turn, jnp.int32(heads))
+            if fresh:
+                peak_ref[turn] = jnp.full((1, rows), NEG, jnp.float32)
+                total_ref[turn] = jnp.zeros((1, rows), jnp.float32)
+                accum_ref[turn] = jnp.zeros((width, rows), jnp.float32)
+            if tiles:
+                new_tiles(turn, head, group)
+            low, high = jnp.int32(0), jnp.int32(0)
+            for at in range(heads):
+                low = jnp.where(head == at, bounds[at * (n_stage + 1) + stage], low)
+                high = jnp.where(head == at, bounds[at * (n_stage + 1) + n_stage], high)
+
+            def several(slot, count):
+                keys = units[pl.ds(slot, count), 0].reshape(count * tokens, width)
+                values_t = jnp.concatenate([units[slot + at, 1] for at in range(count)], axis=1)
+                update(turn, keys, values_t)
+
+            fours = lax.div(high - low, jnp.int32(4))
+
+            def four(at, _):
+                several(low + 4 * at, 4)
+                return 0
+
+            lax.fori_loop(0, fours, four, 0)
+            left = high - low - 4 * fours
+
+            @pl.when(left >= 2)
+            def _():
+                several(high - left, 2)
+
+            @pl.when((left == 1) | (left == 3))
+            def _():
+                several(high - 1, 1)
+
+            if last:
+                keep_own, send_own, keep_end, send_end = outs
+                half = tokens // 2
+                first_group = who_ref[GROUP] == 0
+                for own_rows, keep_ref, send_ref in (
+                    (True, keep_own, send_own),
+                    (False, keep_end, send_end),
+                ):
+
+                    @pl.when((turn < heads) == own_rows)
+                    def _(keep_ref=keep_ref, send_ref=send_ref):
+                        for member in range(rows // tokens):
+                            lanes = pl.ds(member * tokens, tokens)
+                            result = accum_ref[turn, :, lanes] / total_ref[turn, :, lanes]
+                            result = result.T
+                            top, bottom = result[:half], result[half:]
+                            column = pl.ds(
+                                pl.multiple_of((head * (rows // tokens) + member) * width, width), width
+                            )
+                            keep_ref[:, column] = jnp.where(first_group, top, bottom).astype(jnp.bfloat16)
+                            send_ref[:, column] = jnp.where(first_group, bottom, top).astype(jnp.bfloat16)
+
+            return 0
+
+        for lowest, highest, stage, tiles, fresh in parts:
+            body = functools.partial(
+                one_turn, group=0 if lowest < heads else 1, stage=stage, tiles=tiles, fresh=fresh
+            )
+            lax.fori_loop(lowest, highest, body, 0)
+        if not last:
+            stores = []
+            for number, (lowest, highest, _, _, _) in enumerate(parts):
+                here = pl.ds(lowest, highest - lowest)
+                stores += [
+                    pltpu.make_async_copy(ref.at[here], out.at[here], state_sems.at[number, at])
+                    for at, (ref, out) in enumerate(zip(state_refs, outs))
+                ]
+            for store in stores:
+                store.start()
+            for store in stores:
+                store.wait()
+
+
+def attend_call(scale, chunks, who, counts, tokens, parts, queries, buffers, state, tiles=None, last=False):
+    layout = tuple(buffer[:3] + (buffer[4],) for buffer in buffers)
+    arrays = [buffer[3] for buffer in buffers]
+    _, width, rows = queries[0].shape
+    n_turn = 2 * (counts.shape[0] // 4)
+    heads = counts.shape[0] // 4
+    n_units = sum(array.shape[0] - buffer[2] for array, buffer in zip(arrays, buffers))
+    state_shapes = [(n_turn, 1, rows), (n_turn, 1, rows), (n_turn, width, rows)]
+    if last:
+        outs = [jax.ShapeDtypeStruct((tokens // 2, heads * (rows // tokens) * width), jnp.bfloat16)] * 4
+    else:
+        outs = [jax.ShapeDtypeStruct(shape, jnp.float32) for shape in state_shapes]
+    given = [] if state is None else list(state)
+    tile_args = [] if tiles is None else list(tiles)
+    before = 2 + len(queries) + len(arrays) + len(tile_args)
+    aliases = {} if last or state is None else {before + at: at for at in range(3)}
+    return pl.pallas_call(
+        functools.partial(
+            attend_kernel,
+            scale,
+            chunks,
+            layout,
+            len(queries),
+            tuple(parts),
+            len(given),
+            last,
+        ),
+        out_shape=tuple(outs),
+        in_specs=[smem(), smem()]
+        + [hbm()] * (len(queries) + len(arrays))
+        + [vmem()] * len(tile_args)
+        + [hbm()] * len(given),
+        out_specs=tuple([vmem() if last else hbm()] * len(outs)),
+        scratch_shapes=[pltpu.VMEM((n_turn, width, rows), jnp.bfloat16)]
+        + [pltpu.VMEM(shape, jnp.float32) for shape in state_shapes]
+        + [
+            pltpu.VMEM((n_units,) + arrays[0].shape[1:], jnp.bfloat16),
+            pltpu.SemaphoreType.DMA((n_units,)),
+            pltpu.SemaphoreType.DMA((len(parts), 3)),
+            pltpu.SemaphoreType.DMA((len(queries),)),
+        ],
+        input_output_aliases=aliases,
+        compiler_params=pltpu.CompilerParams(vmem_limit_bytes=VMEM),
+        cost_estimate=TINY,
+    )(who, counts, *queries, *arrays, *tile_args, *given)
+
+
+def line_of_four(query, new_keys, new_values, memory_keys, memory_values, retrieved):
+    queries = query[0]
+    tokens, heads, group_size, width = queries.shape
+    units_dev = memory_keys.shape[0]
+    scale = math.log2(math.e) / math.sqrt(width)
+    me = lax.axis_index("mem")
+    span = lax.axis_index("span")
+    group = lax.axis_index("head")
+    low = (me < 2).astype(jnp.int32)
+    middle = (me == 1) | (me == 2)
+    end = jnp.where(low == 1, 0, 3)
+    who = jnp.stack([me, end, 3 - me, 3 - end, low, span > 0, middle, group]).astype(jnp.int32)
+
+    def inward(value):
+        return lax.ppermute(value, "mem", [(0, 1), (3, 2)])
+
+    def across(value):
+        return lax.ppermute(value, "mem", [(1, 2), (2, 1)])
+
+    def far(value):
+        return lax.ppermute(value, "mem", [(0, 2), (3, 1)])
+
+    def onward(value):
+        return lax.ppermute(value, "span", [(at, at + 1) for at in range(lax.axis_size("span") - 1)])
+
+    n_mem = lax.axis_size("mem")
+
+    def after(value, before):
+        return lax.optimization_barrier((value, before))[0]
+
+    own_t = jnp.transpose(queries, (1, 3, 2, 0)).reshape(heads, width, group_size * tokens)
+    end_t = inward(own_t)
+    keys = memory_keys.reshape(units_dev, -1, width)
+    values = memory_values.reshape(units_dev, -1, width)
+    tile_pair = (new_keys[0].reshape(-1, width), new_values[0].reshape(-1, width))
+    unit_lists = after(retrieved[0], own_t)
+    counts, table, own_0 = gather(who, unit_lists, keys, values, PIECES[:1], 0, tile=tile_pair, n_owner=n_mem)
+    stream_0, end_0 = across(own_0), inward(after(own_0, end_t))
+    tile = own_0[:TILE]
+    far_tile = far(after(tile, stream_0))
+    (own_1,) = gather(who, unit_lists, keys, values, PIECES[1:], PIECES[0], table=table)
+    end_1 = inward(after(own_1, end_0))
+
+    places = [sum(PIECES[:at]) for at in range(len(PIECES))]
+    starts = [sum(CHUNKS[:at]) for at in range(len(CHUNKS))]
+    own = [(OWN, places[0], TILE, own_0), (OWN, places[1], 0, own_1)]
+    ends = [(END, places[0], TILE, end_0), (END, places[1], 0, end_1)]
+    streams = [(STREAM, starts[0], TILE, stream_0)]
+    call = functools.partial(attend_call, scale, CHUNKS, who, counts, tokens)
+
+    def send_chunk(at, sources, state):
+        sources = [source[:3] + (after(source[3], state[0]),) for source in sources]
+        packed = pack(who, counts, heads, CHUNKS, starts[at], CHUNKS[at], sources)
+        streams.append((STREAM, starts[at], 0, across(packed)))
+        return [after(state[0], packed), *state[1:]]
+
+    def stage(buffers, before=None):
+        if before is not None:
+            buffers = [buffer[:3] + (after(buffer[3], before[0]),) for buffer in buffers]
+        return [buffer + (0,) for buffer in buffers]
+
+    def parts(tiles, fresh):
+        return [(0, heads, 0, tiles, fresh), (heads, 2 * heads, 0, tiles, fresh)]
+
+    both_t = [own_t, end_t]
+    state = list(call(parts(False, True), both_t, stage(own + streams), None))
+    state = send_chunk(1, own[1:] + ends[:1], state)
+    rest = jnp.concatenate([after(part, state[0])[:TILE] for part in (end_0, stream_0, far_tile)])
+    tiles = (tile, rest, onward(jnp.concatenate([tile, rest])))
+    state = list(call(parts(False, False), both_t, stage(ends[:1], state), state))
+    state = send_chunk(2, own[1:] + ends, state)
+    state = list(call(parts(True, False), both_t, stage(ends[1:] + streams[1:2], state), state, tiles=tiles))
+    last_streams = stage(streams[2:], state)
+    final = functools.partial(call, parts(False, False), both_t, last=True)
+
+    def fits(piece, state):
+        return final(last_streams, state)
+
+    def exceeds(piece, state):
+        return final(last_streams + [(EXTRA, places[-1], 0, across(piece), 0)], state)
+
+    by_owner = counts.reshape(-1, heads).sum(axis=1)
+    over = jnp.maximum(by_owner[0] + by_owner[1], by_owner[2] + by_owner[3]) > sum(CHUNKS)
+    keep_own, send_own, keep_end, send_end = lax.cond(over, exceeds, fits, own_1, tuple(state))
+
+    n_head = lax.axis_size("head")
+
+    def pairs(moves):
+        return [
+            (source * n_head + at, target * n_head + (at + turn) % n_head)
+            for source, target, turn in moves
+            for at in range(n_head)
+        ]
+
+    axes = ("mem", "head")
+    kept = lax.ppermute(keep_end, axes, pairs([(1, 0, 0), (2, 3, 0)]))
+    swapped_end = lax.ppermute(send_end, axes, pairs([(1, 0, 1), (2, 3, 1)]))
+    swapped_own = lax.ppermute(send_own, axes, pairs([(1, 1, 1), (2, 2, 1)]))
+    same = jnp.where(middle, keep_own, kept)
+    other = jnp.where(middle, swapped_own, swapped_end)
+    left = jnp.where(group == 0, same, other)
+    right = jnp.where(group == 0, other, same)
+    return jnp.concatenate([left, right], axis=1)[None]
 
 
 def shifted(value, axis, steps):
@@ -14,7 +601,7 @@
     return lax.ppermute(value, axis, [(source, source + steps) for source in range(first, last)])
 
 
-def local(query, new_keys, new_values, memory_keys, memory_values, retrieved):
+def any_line(query, new_keys, new_values, memory_keys, memory_values, retrieved):
     queries = query[0]
     row_count, head_count, group_size, head_width = queries.shape
     score_scale = 1.0 / math.sqrt(head_width)
@@ -105,6 +692,7 @@
 
 
 def solution(mesh):
+    local = line_of_four if mesh.shape["mem"] == 4 and mesh.shape["head"] == 2 else any_line
     return jax.shard_map(
         local,
         mesh=mesh,

time: 306 us -> 187 us (0.61)
  waiting for transfers between devices: 159 us -> 64.3 us
  Pallas kernels: 0 us -> 81.8 us
  matrix products: 45.2 us -> 0 us
  local copies, waits for them, and re-layouts: 47.1 us -> 6.56 us
  starting transfers between devices: 3.76 us -> 23.3 us
  blocking collectives: 15.4 us -> 0 us
  other arithmetic: 16.6 us -> 5.44 us
  between operations: 13.4 us -> 2.95 us
    psum x1 -> x0, waiting for transfers between devices: 144 us -> none  [local(): lax.psum(slot_terms, 'mem').astype(jnp.float32).astype(jnp.bfloat16)]
    pallas_call x0 -> x8, Pallas kernels: none -> 81.8 us  [the longest x4 68.5 us: attend_call(): pl.pallas_call(functools.partial(attend_kernel, scale, chunks, layout, le...]
    ppermute x1 -> x11, waiting for transfers between devices: 2.91 us -> 64.3 us  [the longest x3 44.6 us: inward(): return lax.ppermute(value, 'mem', [(0, 1), (3, 2)])]
    dot_general x12 -> x0, matrix products: 45.2 us -> none  [the longest x6 27.3 us: update(): jnp.einsum('rhgk,khd->rhgd', weights.astype(jnp.bfloat16), key_pair[1], p...]
    gather x16 -> x0, local copies, waits for them, and re-layouts: 25.5 us -> none  [local(): source_array[local_units[head_at], :, head_at, :]]
    ppermute x1 -> x11, starting transfers between devices: 3.68 us -> 23.3 us  [the longest x3 11.2 us: across(): return lax.ppermute(value, 'mem', [(1, 2), (2, 1)])]
    all_to_all x1 -> x0, blocking collectives: 15.4 us -> none  [local(): lax.all_to_all(attended, 'head', split_axis=0, concat_axis=1, tiled=True)]
    while x12 -> x0, local copies, waits for them, and re-layouts: 12.8 us -> none
  transfers between devices with their start and end apart: 4 -> 11, of which waited for: 3 -> 5; matrix products, arithmetic and copies ran while one was open for 16% -> 4% of each run, Pallas kernels for 0% -> 40%
where the time goes in v2:
time: 187 us; the launch traced here: 184 us
  Pallas kernels  81.8 us (44%)
  waiting for transfers between devices  64.3 us (34%)
  starting transfers between devices  23.3 us (12%)
  local copies, waits for them, and re-layouts  6.56 us (4%)
  other arithmetic  5.44 us (3%)
  between operations  2.95 us (2%)
    pallas_call x4, Pallas kernels, attend_call(): pl.pallas_call(functools.partial(attend_kernel, scale, chunks, layout, le...  68.5 us
    ppermute x3, waiting for transfers between devices, inward(): return lax.ppermute(value, 'mem', [(0, 1), (3, 2)])  44.6 us
    ppermute x3, starting transfers between devices, across(): return lax.ppermute(value, 'mem', [(1, 2), (2, 1)])  11.2 us
    ppermute x1, waiting for transfers between devices, line_of_four(): swapped_own = lax.ppermute(send_own, axes, pairs([(1, 1, 1), (2, 2, 1)]))  9.25 us
    ppermute x1, waiting for transfers between devices, line_of_four(): kept = lax.ppermute(keep_end, axes, pairs([(1, 0, 0), (2, 3, 0)]))  8.98 us
    pallas_call x2, Pallas kernels, gather(): pl.pallas_call(functools.partial(gather_kernel, units, pieces, first, til...  7.34 us
    pallas_call x2, Pallas kernels, pack(): pl.pallas_call(functools.partial(pack_kernel, heads, chunks, first, layou...  5.98 us
    ppermute x3, starting transfers between devices, inward(): return lax.ppermute(value, 'mem', [(0, 1), (3, 2)])  3.85 us
  transfers between devices with their start and end apart: 11, of which 5 were waited for; matrix products, arithmetic and copies ran while one was open for 4% of the time, Pallas kernels for 40%

profile of v2, /device:TPU:17, one launch (start us, length us, event | category | flops | bytes accessed | tf_op | source)
XLA Modules:
  0.0 184.4 jit_solution(14610065437212884014)
XLA Ops:
  0.0 2.2 %copy.13 = bf16[4,128,8,128]{3,2,1,0:T(8,128)(2,1)S(1)} copy(bf16[4,128,8,128]{1,2,0,3:T(8,128)(2,1)} %bitcast.25) | data formatting | bytes 2097152 | tf_op jit(solution)/shard_map/transpose | solution.py:523
  2.2 0.5 reshape.19.refs_2_
  2.7 1.3 collective-permute-start.1
  4.0 0.1 stack.43.who_ref.refs_0_
  4.1 6.4 %shard_map.64 = (s32[16]{0:T(128)S(1)}, s32[65]{0:T(128)}, bf16[20,2,128,128]{3,2,1,0:T(8,128)(2,1)}) custom-call(s32[8]{0:T(128)S(1)} %stack.43.who_ref.refs_0_, s32[4,16]{1,0:T(4,128)} %bitcast.28, bf16[32,512,128]{2,1,0:T(8,128)(2,1)} %bitcast.21, bf16[32,512,128]{2,1,0:T(8,128)(2,1)} %bitcast.23, bf16[512,128]{1,0:T(8,128)(2,1)} %bitcast.26, ...), custom_call_target="tpu_custom_call" | custom-call | flops 1000 | bytes 1000 | tf_op jit(solution)/shard_map/pallas_call | solution.py:142
  10.5 18.1 %collective-permute-done.1.refs_3_ = bf16[4,128,1024]{2,1,0:T(8,128)(2,1)S(1)} collective-permute-done((bf16[4,128,1024]{2,1,0:T(8,128)(2,1)S(1)}, bf16[4,128,1024]{2,1,0:T(8,128)(2,1)S(1)}, u32[]{:S(2)}, u32[]{:S(2)}) %collective-permute-start.1) | collective-permute-done | bytes 1048608 | tf_op jit(solution)/shard_map/ppermute | solution.py:507
  28.6 1.3 collective-permute-start.2
  29.9 2.1 %collective-permute-start.3 = (bf16[20,2,128,128]{3,2,1,0:T(8,128)(2,1)}, bf16[20,2,128,128]{3,2,1,0:T(8,128)(2,1)S(1)}, u32[]{:S(2)}, u32[]{:S(2)}) collective-permute-start(bf16[20,2,128,128]{3,2,1,0:T(8,128)(2,1)} %get-tuple-element.93.refs_4_), channel_id=1, source_target_pairs={{8,16},{16,8},{9,17},{17,9},{10,18},{18,10},{11,19},{19,11},{12,20... | collective-permute-start | bytes 3932168 | tf_op jit(solution)/shard_map/ppermute | solution.py:510
  32.0 0.9 shard_map.65.refs_5_.refs_0_
  32.9 26.5 %collective-permute-done.2.refs_1_.refs_4_ = bf16[20,2,128,128]{3,2,1,0:T(8,128)(2,1)S(1)} collective-permute-done((bf16[20,2,128,128]{3,2,1,0:T(8,128)(2,1)}, bf16[20,2,128,128]{3,2,1,0:T(8,128)(2,1)S(1)}, u32[]{:S(2)}, u32[]{:S(2)}) %collective-permute-start.2) | collective-permute-done | bytes 1310752 | tf_op jit(solution)/shard_map/ppermute | solution.py:507
  59.4 0.0 copy-start.1
  59.4 1.3 collective-permute-start.4
  60.7 1.0 slice.25.refs_6_
  61.7 0.0 copy-start.2
  61.7 0.0 collective-permute-done.3.refs_6_
  61.7 0.0 copy-start.6
  61.7 1.3 collective-permute-start.7
  63.0 0.0 copy-done.1
  63.0 0.0 copy-done.6
  63.1 17.8 %shard_map.66 = (f32[8,1,1024]{2,1,0:T(1,128)S(1)}, f32[8,1,1024]{2,1,0:T(1,128)S(1)}, f32[8,128,1024]{2,1,0:T(8,128)S(1)}) custom-call(s32[8]{0:T(128)S(1)} %stack.43.who_ref.refs_0_, s32[16]{0:T(128)S(1)} %get-tuple-element.90.refs_1_.count_ref, bf16[4,128,1024]{2,1,0:T(8,128)(2,1)S(1)} %reshape.19.refs_2_, ...), custom_call_target="tpu_custom_call" | custom-call | flops 1000 | bytes 1000 | tf_op jit(solution)/shard_map/pallas_call | solution.py:462
  80.9 3.0 %shard_map.67 = bf16[16,2,128,128]{3,2,1,0:T(8,128)(2,1)} custom-call(s32[8]{0:T(128)S(1)} %stack.43.who_ref.refs_0_, s32[16]{0:T(128)S(1)} %get-tuple-element.90.refs_1_.count_ref, bf16[16,2,128,128]{3,2,1,0:T(8,128)(2,1)S(1)} %shard_map.65.refs_5_.refs_0_, bf16[20,2,128,128]{3,2,1,0:T(8,128)(2,1)} %copy-done.1), custom_call_target="tpu_custom_call" | custom-call | flops 1000 | bytes 1000 | tf_op jit(solution)/shard_map/pallas_call | solution.py:214
  83.9 7.2 %collective-permute-start.6 = (bf16[16,2,128,128]{3,2,1,0:T(8,128)(2,1)}, bf16[16,2,128,128]{3,2,1,0:T(8,128)(2,1)}, u32[]{:S(2)}, u32[]{:S(2)}) collective-permute-start(bf16[16,2,128,128]{3,2,1,0:T(8,128)(2,1)} %shard_map.67), channel_id=1, source_target_pairs={{8,16},{16,8},{9,17},{17,9},{10,18},{18,10},{11,19},{19,11},{12,20... | collective-permute-start | bytes 3145736 | tf_op jit(solution)/shard_map/ppermute | solution.py:510
  91.1 1.0 slice.26
  92.0 0.0 copy-start.3
  92.0 1.1 slice.27
  93.1 0.0 copy-start.5
  93.1 0.0 collective-permute-done.7
  93.1 0.0 copy-done.2
  93.1 0.0 copy-start.8
  93.1 1.1 pad_maximum_fusion
  94.3 2.3 %collective-permute-start.8 = (bf16[16,2,128,128]{3,2,1,0:T(8,128)(2,1)}, bf16[16,2,128,128]{3,2,1,0:T(8,128)(2,1)}, u32[]{:S(2)}, u32[]{:S(2)}) collective-permute-start(bf16[16,2,128,128]{3,2,1,0:T(8,128)(2,1)} %pad_maximum_fusion), channel_id=1, source_target_pairs={{0,1},{1,2},{2,3},{4,5},{5,6},{6,7},{8,9},{9,10},{10,11},{12,13},{... | collective-permute-start | bytes 3145736 | tf_op jit(solution)/shard_map/ppermute | solution.py:516
  96.6 0.0 copy-done.5
  96.6 11.6 %shard_map.68 = (f32[8,1,1024]{2,1,0:T(1,128)S(1)}, f32[8,1,1024]{2,1,0:T(1,128)S(1)}, f32[8,128,1024]{2,1,0:T(8,128)S(1)}) custom-call(s32[8]{0:T(128)S(1)} %stack.43.who_ref.refs_0_, s32[16]{0:T(128)S(1)} %get-tuple-element.90.refs_1_.count_ref, ...), custom_call_target="tpu_custom_call", output_to_operand_aliasing={{0}: (5, {}), {1}: (6, {}), {2}: (7, {})} | custom-call | flops 1000 | bytes 1000 | tf_op jit(solution)/shard_map/pallas_call | solution.py:462
  108.2 0.0 copy-done.3
  108.3 0.0 copy-done.8
  108.3 0.0 copy-start
  108.3 0.0 copy-start.4
  108.3 0.0 collective-permute-done.4.refs_2_.refs_4_
  108.3 2.9 %shard_map.69 = bf16[16,2,128,128]{3,2,1,0:T(8,128)(2,1)} custom-call(s32[8]{0:T(128)S(1)} %stack.43.who_ref.refs_0_, s32[16]{0:T(128)S(1)} %get-tuple-element.90.refs_1_.count_ref, bf16[16,2,128,128]{3,2,1,0:T(8,128)(2,1)S(1)} %shard_map.65.refs_5_.refs_0_, bf16[20,2,128,128]{3,2,1,0:T(8,128)(2,1)} %copy-done.1, ...), custom_call_target="tpu_custom_call" | custom-call | flops 1000 | bytes 1000 | tf_op jit(solution)/shard_map/pallas_call | solution.py:214
  111.3 0.0 copy-done
  111.3 2.0 %collective-permute-start.5 = (bf16[16,2,128,128]{3,2,1,0:T(8,128)(2,1)}, bf16[16,2,128,128]{3,2,1,0:T(8,128)(2,1)}, u32[]{:S(2)}, u32[]{:S(2)}) collective-permute-start(bf16[16,2,128,128]{3,2,1,0:T(8,128)(2,1)} %shard_map.69), channel_id=1, source_target_pairs={{8,16},{16,8},{9,17},{17,9},{10,18},{18,10},{11,19},{19,11},{12,20... | collective-permute-start | bytes 3145736 | tf_op jit(solution)/shard_map/ppermute | solution.py:510
  113.3 0.1 reshape.22
  113.4 0.1 reduce_sum.9
  113.5 0.7 fusion
  116.7 0.0 copy-done.4
  116.8 2.0 %pad_maximum_fusion.1.refs_7_ = bf16[12,2,128,128]{3,2,1,0:T(8,128)(2,1)} fusion(bf16[4,2,128,128]{3,2,1,0:T(8,128)(2,1)} %copy-done.8, bf16[4,2,128,128]{3,2,1,0:T(8,128)(2,1)} %copy-done.5, bf16[4,2,128,128]{3,2,1,0:T(8,128)(2,1)S(1)} %copy-done.4), kind=kLoop, calls=%fused_computation.2 | loop fusion | flops 786432 | bytes 1572864 | tf_op jit(solution)/shard_map/concatenate | solution.py:560
  118.7 0.0 collective-permute-done.6.refs_5_
  118.7 0.0 collective-permute-done.8.refs_8_
  118.7 31.0 %shard_map.70 = (f32[8,1,1024]{2,1,0:T(1,128)S(1)}, f32[8,1,1024]{2,1,0:T(1,128)S(1)}, f32[8,128,1024]{2,1,0:T(8,128)}) custom-call(s32[8]{0:T(128)S(1)} %stack.43.who_ref.refs_0_, s32[16]{0:T(128)S(1)} %get-tuple-element.90.refs_1_.count_ref, ...), custom_call_target="tpu_custom_call", output_to_operand_aliasing={{0}: (9, {}), {1}: (10, {}), {2}: (11, {})} | custom-call | flops 1000 | bytes 1000 | tf_op jit(solution)/shard_map/pallas_call | solution.py:462
  149.8 0.0 collective-permute-done.5
  149.8 8.1 %conditional.1 = ((bf16[64,4096]{1,0:T(8,128)(2,1)}, bf16[64,4096]{1,0:T(8,128)(2,1)}, bf16[64,4096]{1,0:T(8,128)(2,1)}, bf16[64,4096]{1,0:T(8,128)(2,1)})) conditional(s32[]{:T(128)} %bitcast.15, (s32[8]{0:T(128)S(1)}, s32[16]{0:T(128)S(1)}, bf16[4,128,1024]{2,1,0:T(8,128)(2,1)S(1)}, bf16[4,128,1024]{2,1,0:T(8,128)(2,1)S(1)}, ...), branch_computations={%region_1.2_spmd, %region_2.3_spmd} | conditional | flops 1000 | bytes 8389684 | solution.py:576
  149.8 8.1 %branch_0_fun.1 = (bf16[64,4096]{1,0:T(8,128)(2,1)}, bf16[64,4096]{1,0:T(8,128)(2,1)}, bf16[64,4096]{1,0:T(8,128)(2,1)}, bf16[64,4096]{1,0:T(8,128)(2,1)}) custom-call(s32[8]{0:T(128)S(1)} %get-tuple-element.39.refs_0_, s32[16]{0:T(128)S(1)} %get-tuple-element.40.refs_1_, bf16[4,128,1024]{2,1,0:T(8,128)(2,1)S(1)} %get-tuple-element.41.refs_2_, ...), custom_call_target="tpu_custom_call" | custom-call | flops 1000 | bytes 1000 | tf_op jit(solution)/shard_map/cond/branch_0_fun/pallas_call | solution.py:462
  157.9 1.9 %collective-permute-start.10 = (bf16[64,4096]{1,0:T(8,128)(2,1)}, bf16[64,4096]{1,0:T(8,128)(2,1)S(1)}, u32[]{:S(2)}, u32[]{:S(2)}) collective-permute-start(bf16[64,4096]{1,0:T(8,128)(2,1)} %get-tuple-element.120), channel_id=1, source_target_pairs={{8,12},{12,8},{16,20},{20,16},{9,13},{13,9},{17,21},{21,17},{10,14... | collective-permute-start | bytes 1572872 | tf_op jit(solution)/shard_map/ppermute | solution.py:590
  159.8 1.3 collective-permute-start.11
  161.2 1.3 collective-permute-start.9
  162.5 9.2 %collective-permute-done.10 = bf16[64,4096]{1,0:T(8,128)(2,1)S(1)} collective-permute-done((bf16[64,4096]{1,0:T(8,128)(2,1)}, bf16[64,4096]{1,0:T(8,128)(2,1)S(1)}, u32[]{:S(2)}, u32[]{:S(2)}) %collective-permute-start.10) | collective-permute-done | bytes 524320 | tf_op jit(solution)/shard_map/ppermute | solution.py:590
  171.8 1.5 collective-permute-done.11
  173.3 9.0 %collective-permute-done.9 = bf16[64,4096]{1,0:T(8,128)(2,1)S(1)} collective-permute-done((bf16[64,4096]{1,0:T(8,128)(2,1)}, bf16[64,4096]{1,0:T(8,128)(2,1)S(1)}, u32[]{:S(2)}, u32[]{:S(2)}) %collective-permute-start.9) | collective-permute-done | bytes 524320 | tf_op jit(solution)/shard_map/ppermute | solution.py:588
  182.2 1.2 broadcast_select_fusion.3
  183.4 1.0 maximum_bitcast_fusion
Async XLA Ops:
  2.7 25.9 %collective-permute-start.1 = (bf16[4,128,1024]{2,1,0:T(8,128)(2,1)S(1)}, bf16[4,128,1024]{2,1,0:T(8,128)(2,1)S(1)}, u32[]{:S(2)}, u32[]{:S(2)}) collective-permute-start(bf16[4,128,1024]{2,1,0:T(8,128)(2,1)S(1)} %reshape.19.refs_2_), channel_id=1, source_target_pairs={{0,8},{24,16},{1,9},{25,17},{2,10},{26,18},{3,11},{27,19},{4,12},{... | collective-permute-start | bytes 3145736 | tf_op jit(solution)/shard_map/ppermute | solution.py:507
  28.6 30.8 %collective-permute-start.2 = (bf16[20,2,128,128]{3,2,1,0:T(8,128)(2,1)}, bf16[20,2,128,128]{3,2,1,0:T(8,128)(2,1)S(1)}, u32[]{:S(2)}, u32[]{:S(2)}) collective-permute-start(bf16[20,2,128,128]{3,2,1,0:T(8,128)(2,1)} %get-tuple-element.93.refs_4_), channel_id=1, source_target_pairs={{0,8},{24,16},{1,9},{25,17},{2,10},{26,18},{3,11},{27,19},{4,12},{... | collective-permute-start | bytes 3932168 | tf_op jit(solution)/shard_map/ppermute | solution.py:507
  29.9 31.8 %collective-permute-start.3 = (bf16[20,2,128,128]{3,2,1,0:T(8,128)(2,1)}, bf16[20,2,128,128]{3,2,1,0:T(8,128)(2,1)S(1)}, u32[]{:S(2)}, u32[]{:S(2)}) collective-permute-start(bf16[20,2,128,128]{3,2,1,0:T(8,128)(2,1)} %get-tuple-element.93.refs_4_), channel_id=1, source_target_pairs={{8,16},{16,8},{9,17},{17,9},{10,18},{18,10},{11,19},{19,11},{12,20... | collective-permute-start | bytes 3932168 | tf_op jit(solution)/shard_map/ppermute | solution.py:510
  59.4 3.6 %copy-start.1 = (bf16[20,2,128,128]{3,2,1,0:T(8,128)(2,1)}, bf16[20,2,128,128]{3,2,1,0:T(8,128)(2,1)S(1)}, u32[]{:S(2)}) copy-start(bf16[20,2,128,128]{3,2,1,0:T(8,128)(2,1)S(1)} %collective-permute-done.2.refs_1_.refs_4_) | copy-start | bytes 3932164
  59.4 48.8 %collective-permute-start.4 = (bf16[16,2,128,128]{3,2,1,0:T(8,128)(2,1)S(1)}, bf16[16,2,128,128]{3,2,1,0:T(8,128)(2,1)}, u32[]{:S(2)}, u32[]{:S(2)}) collective-permute-start(bf16[16,2,128,128]{3,2,1,0:T(8,128)(2,1)S(1)} %shard_map.65.refs_5_.refs_0_), channel_id=1, source_target_pairs={{0,8},{24,16},{1,9},{25,17},{2,10},{26,18},{3,11},{27,19},{4,12},{... | collective-permute-start | bytes 3145736 | tf_op jit(solution)/shard_map/ppermute | solution.py:507
  61.7 31.4 %copy-start.2 = (bf16[4,2,128,128]{3,2,1,0:T(8,128)(2,1)}, bf16[4,2,128,128]{3,2,1,0:T(8,128)(2,1)S(1)}, u32[]{:S(2)}) copy-start(bf16[4,2,128,128]{3,2,1,0:T(8,128)(2,1)S(1)} %slice.25.refs_6_) | copy-start | bytes 786436
  61.7 1.3 copy-start.6
  61.7 31.4 %collective-permute-start.7 = (bf16[4,2,128,128]{3,2,1,0:T(8,128)(2,1)S(1)}, bf16[4,2,128,128]{3,2,1,0:T(8,128)(2,1)S(1)}, u32[]{:S(2)}, u32[]{:S(2)}) collective-permute-start(bf16[4,2,128,128]{3,2,1,0:T(8,128)(2,1)S(1)} %slice.25.refs_6_), channel_id=1, source_target_pairs={{0,16},{24,8},{1,17},{25,9},{2,18},{26,10},{3,19},{27,11},{4,20},{... | collective-permute-start | bytes 786440 | tf_op jit(solution)/shard_map/ppermute | solution.py:513
  83.9 34.8 %collective-permute-start.6 = (bf16[16,2,128,128]{3,2,1,0:T(8,128)(2,1)}, bf16[16,2,128,128]{3,2,1,0:T(8,128)(2,1)}, u32[]{:S(2)}, u32[]{:S(2)}) collective-permute-start(bf16[16,2,128,128]{3,2,1,0:T(8,128)(2,1)} %shard_map.67), channel_id=1, source_target_pairs={{8,16},{16,8},{9,17},{17,9},{10,18},{18,10},{11,19},{19,11},{12,20... | collective-permute-start | bytes 3145736 | tf_op jit(solution)/shard_map/ppermute | solution.py:510
  92.0 16.2 %copy-start.3 = (bf16[4,2,128,128]{3,2,1,0:T(8,128)(2,1)}, bf16[4,2,128,128]{3,2,1,0:T(8,128)(2,1)S(1)}, u32[]{:S(2)}) copy-start(bf16[4,2,128,128]{3,2,1,0:T(8,128)(2,1)S(1)} %slice.26) | copy-start | bytes 786436
  93.1 3.5 %copy-start.5 = (bf16[4,2,128,128]{3,2,1,0:T(8,128)(2,1)}, bf16[4,2,128,128]{3,2,1,0:T(8,128)(2,1)S(1)}, u32[]{:S(2)}) copy-start(bf16[4,2,128,128]{3,2,1,0:T(8,128)(2,1)S(1)} %slice.27) | copy-start | bytes 786436
  93.1 15.1 %copy-start.8 = (bf16[4,2,128,128]{3,2,1,0:T(8,128)(2,1)}, bf16[4,2,128,128]{3,2,1,0:T(8,128)(2,1)S(1)}, u32[]{:S(2)}) copy-start(bf16[4,2,128,128]{3,2,1,0:T(8,128)(2,1)S(1)} %collective-permute-done.7) | copy-start | bytes 786436
  94.3 24.5 %collective-permute-start.8 = (bf16[16,2,128,128]{3,2,1,0:T(8,128)(2,1)}, bf16[16,2,128,128]{3,2,1,0:T(8,128)(2,1)}, u32[]{:S(2)}, u32[]{:S(2)}) collective-permute-start(bf16[16,2,128,128]{3,2,1,0:T(8,128)(2,1)} %pad_maximum_fusion), channel_id=1, source_target_pairs={{0,1},{1,2},{2,3},{4,5},{5,6},{6,7},{8,9},{9,10},{10,11},{12,13},{... | collective-permute-start | bytes 3145736 | tf_op jit(solution)/shard_map/ppermute | solution.py:516
  108.3 3.0 %copy-start = (f32[8,128,1024]{2,1,0:T(8,128)}, f32[8,128,1024]{2,1,0:T(8,128)S(1)}, u32[]{:S(2)}) copy-start(f32[8,128,1024]{2,1,0:T(8,128)S(1)} %get-tuple-element.113.refs_11_) | copy-start | bytes 12582916
  108.3 8.5 %copy-start.4 = (bf16[4,2,128,128]{3,2,1,0:T(8,128)(2,1)S(1)}, bf16[4,2,128,128]{3,2,1,0:T(8,128)(2,1)}, u32[]{:S(2)}) copy-start(bf16[4,2,128,128]{3,2,1,0:T(8,128)(2,1)} %copy-done.3) | copy-start | bytes 786436
  111.3 38.5 %collective-permute-start.5 = (bf16[16,2,128,128]{3,2,1,0:T(8,128)(2,1)}, bf16[16,2,128,128]{3,2,1,0:T(8,128)(2,1)}, u32[]{:S(2)}, u32[]{:S(2)}) collective-permute-start(bf16[16,2,128,128]{3,2,1,0:T(8,128)(2,1)} %shard_map.69), channel_id=1, source_target_pairs={{8,16},{16,8},{9,17},{17,9},{10,18},{18,10},{11,19},{19,11},{12,20... | collective-permute-start | bytes 3145736 | tf_op jit(solution)/shard_map/ppermute | solution.py:510
  157.9 13.8 %collective-permute-start.10 = (bf16[64,4096]{1,0:T(8,128)(2,1)}, bf16[64,4096]{1,0:T(8,128)(2,1)S(1)}, u32[]{:S(2)}, u32[]{:S(2)}) collective-permute-start(bf16[64,4096]{1,0:T(8,128)(2,1)} %get-tuple-element.120), channel_id=1, source_target_pairs={{8,12},{12,8},{16,20},{20,16},{9,13},{13,9},{17,21},{21,17},{10,14... | collective-permute-start | bytes 1572872 | tf_op jit(solution)/shard_map/ppermute | solution.py:590
  159.8 13.4 %collective-permute-start.11 = (bf16[64,4096]{1,0:T(8,128)(2,1)}, bf16[64,4096]{1,0:T(8,128)(2,1)S(1)}, u32[]{:S(2)}, u32[]{:S(2)}) collective-permute-start(bf16[64,4096]{1,0:T(8,128)(2,1)} %get-tuple-element.121), channel_id=1, source_target_pairs={{8,4},{12,0},{16,28},{20,24},{9,5},{13,1},{17,29},{21,25},{10,6},{... | collective-permute-start | bytes 1572872 | tf_op jit(solution)/shard_map/ppermute | solution.py:589
  161.2 21.1 %collective-permute-start.9 = (bf16[64,4096]{1,0:T(8,128)(2,1)}, bf16[64,4096]{1,0:T(8,128)(2,1)S(1)}, u32[]{:S(2)}, u32[]{:S(2)}) collective-permute-start(bf16[64,4096]{1,0:T(8,128)(2,1)} %get-tuple-element.119), channel_id=1, source_target_pairs={{8,0},{12,4},{16,24},{20,28},{9,1},{13,5},{17,25},{21,29},{10,2},{... | collective-permute-start | bytes 1572872 | tf_op jit(solution)/shard_map/ppermute | solution.py:588

commit v3 on v2

--- a/solution.py
+++ b/solution.py
@@ -520,18 +520,25 @@
     def after(value, before):
         return lax.optimization_barrier((value, before))[0]
 
-    own_t = jnp.transpose(queries, (1, 3, 2, 0)).reshape(heads, width, group_size * tokens)
-    end_t = inward(own_t)
+    half = heads // 2
+
+    def query_t(value):
+        return jnp.transpose(value, (1, 3, 2, 0)).reshape(-1, width, group_size * tokens)
+
+    own_t = [query_t(queries[:, :half])]
+    early = inward(own_t[0])
     keys = memory_keys.reshape(units_dev, -1, width)
     values = memory_values.reshape(units_dev, -1, width)
     tile_pair = (new_keys[0].reshape(-1, width), new_values[0].reshape(-1, width))
-    unit_lists = after(retrieved[0], own_t)
+    unit_lists = after(retrieved[0], own_t[0])
     counts, table, own_0 = gather(who, unit_lists, keys, values, PIECES[:1], 0, tile=tile_pair, n_owner=n_mem)
-    stream_0, end_0 = across(own_0), inward(after(own_0, end_t))
+    stream_0, end_0 = across(own_0), inward(after(own_0, early))
     tile = own_0[:TILE]
-    far_tile = far(after(tile, stream_0))
+    far_tile = far(tile)
     (own_1,) = gather(who, unit_lists, keys, values, PIECES[1:], PIECES[0], table=table)
-    end_1 = inward(after(own_1, end_0))
+    end_1 = inward(own_1)
+    own_t.append(query_t(after(queries[:, half:], own_1)))
+    late = inward(after(own_t[1], end_0))
 
     places = [sum(PIECES[:at]) for at in range(len(PIECES))]
     starts = [sum(CHUNKS[:at]) for at in range(len(CHUNKS))]
@@ -554,16 +561,38 @@
     def parts(tiles, fresh):
         return [(0, heads, 0, tiles, fresh), (heads, 2 * heads, 0, tiles, fresh)]
 
-    both_t = [own_t, end_t]
-    state = list(call(parts(False, True), both_t, stage(own + streams), None))
+    mine, first, second = (0, heads), (heads, heads + half), (heads + half, 2 * heads)
+    def pinned(buffers, before):
+        return [buffer[:3] + (after(buffer[3], before[0]),) for buffer in buffers]
+
+    state = list(call([mine + (0, False, True), first + (0, False, True)], own_t + [early], stage(own), None))
+    rest = jnp.concatenate([part[:TILE] for part in (end_0, stream_0, far_tile)])
+    tiles = (tile, rest, onward(jnp.concatenate([tile, rest])))
     state = send_chunk(1, own[1:] + ends[:1], state)
-    rest = jnp.concatenate([after(part, state[0])[:TILE] for part in (end_0, stream_0, far_tile)])
-    tiles = (tile, rest, onward(jnp.concatenate([tile, rest])))
-    state = list(call(parts(False, False), both_t, stage(ends[:1], state), state))
+    state = list(
+        call(
+            [mine + (0, False, False), first + (0, False, False)],
+            own_t + [early],
+            stage(streams[:1] + ends[:1], state),
+            state,
+        )
+    )
     state = send_chunk(2, own[1:] + ends, state)
-    state = list(call(parts(True, False), both_t, stage(ends[1:] + streams[1:2], state), state, tiles=tiles))
+    late = after(late, state[0])
+    both_t = own_t + [early, late]
+    state = list(
+        call(
+            [mine + (1, True, False), first + (1, True, False), second + (0, True, True)],
+            both_t,
+            stage(own + streams[:1] + ends[:1]) + [buffer + (1,) for buffer in pinned(ends[1:] + streams[1:2], state)],
+            state,
+            tiles=tiles,
+        )
+    )
     last_streams = stage(streams[2:], state)
-    final = functools.partial(call, parts(False, False), both_t, last=True)
+    final = functools.partial(
+        call, [mine + (0, False, False), (heads, 2 * heads, 0, False, False)], both_t, last=True
+    )
 
     def fits(piece, state):
         return final(last_streams, state)

time: 187 us -> 176 us (0.941)
  waiting for transfers between devices: 64.3 us -> 42.4 us
  local copies, waits for them, and re-layouts: 6.56 us -> 13.1 us
  starting transfers between devices: 23.3 us -> 26.2 us
    ppermute x3 -> x4, waiting for transfers between devices: 44.6 us -> 15.2 us  [inward(): return lax.ppermute(value, 'mem', [(0, 1), (3, 2)])]
    ppermute x1, waiting for transfers between devices: 9.25 us -> 1.06 us  [line_of_four(): swapped_own = lax.ppermute(send_own, axes, pairs([(1, 1, 1), (2, 2, 1)]))]
    ppermute x1, waiting for transfers between devices: 0.01 us -> 6.07 us  [far(): return lax.ppermute(value, 'mem', [(0, 2), (3, 1)])]
    ppermute x3, waiting for transfers between devices: 0.01 us -> 5.5 us  [across(): return lax.ppermute(value, 'mem', [(1, 2), (2, 1)])]
    ppermute x1, waiting for transfers between devices: 1.49 us -> 6.48 us  [line_of_four(): swapped_end = lax.ppermute(send_end, axes, pairs([(1, 0, 1), (2, 3, 1)]))]
    ppermute x1, starting transfers between devices: 2.33 us -> 5.66 us  [onward(): lax.ppermute(value, 'span', [(at, at + 1) for at in range(lax.axis_size('...]
    slice x2 -> x3, local copies, waits for them, and re-layouts: 2.03 us -> 5 us  [the longest x2 2.83 us: line_of_four(): part[:TILE]]
    ppermute x3, starting transfers between devices: 11.2 us -> 8.79 us  [across(): return lax.ppermute(value, 'mem', [(1, 2), (2, 1)])]
  transfers between devices with their start and end apart: 11 -> 12, of which waited for: 5 -> 8; matrix products, arithmetic and copies ran while one was open for 4% -> 8% of each run, Pallas kernels for 40% -> 42%
where the time goes in v3:
time: 176 us; the launch traced here: 173 us
  Pallas kernels  81.5 us (46%)
  waiting for transfers between devices  42.4 us (24%)
  starting transfers between devices  26.2 us (15%)
  local copies, waits for them, and re-layouts  13.1 us (7%)
  other arithmetic  6.48 us (4%)
  between operations  2.86 us (2%)
    pallas_call x4, Pallas kernels, attend_call(): pl.pallas_call(functools.partial(attend_kernel, scale, chunks, layout, le...  68.3 us
    ppermute x4, waiting for transfers between devices, inward(): return lax.ppermute(value, 'mem', [(0, 1), (3, 2)])  15.2 us
    ppermute x3, starting transfers between devices, across(): return lax.ppermute(value, 'mem', [(1, 2), (2, 1)])  8.79 us
    pallas_call x2, Pallas kernels, gather(): pl.pallas_call(functools.partial(gather_kernel, units, pieces, first, til...  8.37 us
    ppermute x1, waiting for transfers between devices, line_of_four(): kept = lax.ppermute(keep_end, axes, pairs([(1, 0, 0), (2, 3, 0)]))  8.05 us
    ppermute x1, waiting for transfers between devices, line_of_four(): swapped_end = lax.ppermute(send_end, axes, pairs([(1, 0, 1), (2, 3, 1)]))  6.48 us
    ppermute x1, waiting for transfers between devices, far(): return lax.ppermute(value, 'mem', [(0, 2), (3, 1)])  6.07 us
    ppermute x1, starting transfers between devices, onward(): lax.ppermute(value, 'span', [(at, at + 1) for at in range(lax.axis_size('...  5.66 us
  transfers between devices with their start and end apart: 12, of which 8 were waited for; matrix products, arithmetic and copies ran while one was open for 8% of the time, Pallas kernels for 42%

profile of v3, /device:TPU:17, one launch (start us, length us, event | category | flops | bytes accessed | tf_op | source)
XLA Modules:
  0.0 172.8 jit_solution(1119469046754849816)
XLA Ops:
  0.0 2.2 %fusion = (bf16[128,2,8,128]{3,2,1,0:T(8,128)(2,1)}, bf16[2,128,8,128]{1,2,0,3:T(8,128)(2,1)S(1)}) fusion(bf16[128,4,8,128]{3,2,1,0:T(8,128)(2,1)} %bitcast.29), kind=kLoop, calls=%fused_computation.8 | loop fusion | bytes 2097152 | tf_op jit(solution)/shard_map/slice | solution.py:540
  2.2 0.6 copy.13
  2.8 0.2 reshape.22.refs_2_
  3.0 1.3 collective-permute-start.1
  4.3 0.1 stack.43.who_ref.refs_0_
  4.4 7.4 %shard_map.64 = (s32[16]{0:T(128)S(1)}, s32[65]{0:T(128)}, bf16[20,2,128,128]{3,2,1,0:T(8,128)(2,1)}) custom-call(s32[8]{0:T(128)S(1)} %stack.43.who_ref.refs_0_, s32[4,16]{1,0:T(4,128)} %bitcast.32, bf16[32,512,128]{2,1,0:T(8,128)(2,1)} %bitcast.24, bf16[32,512,128]{2,1,0:T(8,128)(2,1)} %bitcast.26, bf16[512,128]{1,0:T(8,128)(2,1)} %bitcast.30, ...), custom_call_target="tpu_custom_call" | custom-call | flops 1000 | bytes 1000 | tf_op jit(solution)/shard_map/pallas_call | solution.py:142
  11.9 2.6 %collective-permute-start.4 = (bf16[20,2,128,128]{3,2,1,0:T(8,128)(2,1)}, bf16[20,2,128,128]{3,2,1,0:T(8,128)(2,1)}, u32[]{:S(2)}, u32[]{:S(2)}) collective-permute-start(bf16[20,2,128,128]{3,2,1,0:T(8,128)(2,1)} %get-tuple-element.106.refs_5_.refs_6_), channel_id=1, source_target_pairs={{8,16},{16,8},{9,17},{17,9},{10,18},{18,10},{11,19},{19,11},{12,20... | collective-permute-start | bytes 3932168 | tf_op jit(solution)/shard_map/ppermute | solution.py:510
  14.4 3.2 %collective-permute-done.1.refs_4_ = bf16[2,128,1024]{2,1,0:T(8,128)(2,1)S(1)} collective-permute-done((bf16[2,128,1024]{2,1,0:T(8,128)(2,1)S(1)}, bf16[2,128,1024]{2,1,0:T(8,128)(2,1)S(1)}, u32[]{:S(2)}, u32[]{:S(2)}) %collective-permute-start.1) | collective-permute-done | bytes 524320 | tf_op jit(solution)/shard_map/ppermute | solution.py:507
  17.7 0.0 copy-start.2
  17.7 1.3 collective-permute-start.2
  19.0 0.9 shard_map.65.refs_6_.refs_0_.refs_7_
  19.9 1.3 collective-permute-start.5
  21.2 1.7 slice.33.refs_12_
  22.9 1.3 collective-permute-start.8
  24.2 0.0 copy-done.2
  24.2 2.4 %copy.14 = bf16[2,128,8,128]{3,2,1,0:T(8,128)(2,1)} copy(bf16[2,128,8,128]{1,2,0,3:T(8,128)(2,1)} %bitcast.28) | data formatting | bytes 1048576 | tf_op jit(solution)/shard_map/transpose | solution.py:526
  26.6 1.3 reshape.26.refs_3_
  27.8 9.8 %shard_map.66 = (f32[8,1,1024]{2,1,0:T(1,128)S(1)}, f32[8,1,1024]{2,1,0:T(1,128)S(1)}, f32[8,128,1024]{2,1,0:T(8,128)S(1)}) custom-call(s32[8]{0:T(128)S(1)} %stack.43.who_ref.refs_0_, s32[16]{0:T(128)S(1)} %get-tuple-element.102.refs_1_.count_ref, bf16[2,128,1024]{2,1,0:T(8,128)(2,1)S(1)} %reshape.22.refs_2_, bf16[2,128,1024]{2,1,0:T(8,128)(2,1)S(1)} %reshape.26.refs_3_, ...), custom_call_target="tpu_custom_call" | custom-call | flops 1000 | bytes 1000 | tf_op jit(solution)/shard_map/pallas_call | solution.py:462
  37.6 0.0 copy-start.3
  37.7 5.5 %collective-permute-done.4.refs_5_.refs_8_ = bf16[20,2,128,128]{3,2,1,0:T(8,128)(2,1)} collective-permute-done((bf16[20,2,128,128]{3,2,1,0:T(8,128)(2,1)}, bf16[20,2,128,128]{3,2,1,0:T(8,128)(2,1)}, u32[]{:S(2)}, u32[]{:S(2)}) %collective-permute-start.4) | collective-permute-done | bytes 1310752 | tf_op jit(solution)/shard_map/ppermute | solution.py:510
  43.2 1.7 slice.39
  44.8 3.7 %collective-permute-done.2.refs_1_.refs_6_.refs_9_ = bf16[20,2,128,128]{3,2,1,0:T(8,128)(2,1)S(1)} collective-permute-done((bf16[20,2,128,128]{3,2,1,0:T(8,128)(2,1)}, bf16[20,2,128,128]{3,2,1,0:T(8,128)(2,1)S(1)}, u32[]{:S(2)}, u32[]{:S(2)}) %collective-permute-start.2) | collective-permute-done | bytes 1310752 | tf_op jit(solution)/shard_map/ppermute | solution.py:507
  48.5 0.0 copy-start.1
  48.5 1.1 copy-done.1
  49.6 3.0 %shard_map.67 = bf16[16,2,128,128]{3,2,1,0:T(8,128)(2,1)} custom-call(s32[8]{0:T(128)S(1)} %stack.43.who_ref.refs_0_, s32[16]{0:T(128)S(1)} %get-tuple-element.102.refs_1_.count_ref, bf16[16,2,128,128]{3,2,1,0:T(8,128)(2,1)S(1)} %shard_map.65.refs_6_.refs_0_.refs_7_, bf16[20,2,128,128]{3,2,1,0:T(8,128)(2,1)} %copy-done.1), custom_call_target="tpu_custom_call" | custom-call | flops 1000 | bytes 1000 | tf_op jit(solution)/shard_map/pallas_call | solution.py:214
  52.6 2.1 %collective-permute-start.7 = (bf16[16,2,128,128]{3,2,1,0:T(8,128)(2,1)}, bf16[16,2,128,128]{3,2,1,0:T(8,128)(2,1)}, u32[]{:S(2)}, u32[]{:S(2)}) collective-permute-start(bf16[16,2,128,128]{3,2,1,0:T(8,128)(2,1)} %shard_map.67), channel_id=1, source_target_pairs={{8,16},{16,8},{9,17},{17,9},{10,18},{18,10},{11,19},{19,11},{12,20... | collective-permute-start | bytes 3145736 | tf_op jit(solution)/shard_map/ppermute | solution.py:510
  54.7 0.0 copy-done.3
  54.7 0.0 copy-start.5
  54.8 14.6 %shard_map.68 = (f32[8,1,1024]{2,1,0:T(1,128)S(1)}, f32[8,1,1024]{2,1,0:T(1,128)S(1)}, f32[8,128,1024]{2,1,0:T(8,128)S(1)}) custom-call(s32[8]{0:T(128)S(1)} %stack.43.who_ref.refs_0_, s32[16]{0:T(128)S(1)} %get-tuple-element.102.refs_1_.count_ref, ...), custom_call_target="tpu_custom_call", output_to_operand_aliasing={{0}: (7, {}), {1}: (8, {}), {2}: (9, {})} | custom-call | flops 1000 | bytes 1000 | tf_op jit(solution)/shard_map/pallas_call | solution.py:462
  69.4 0.0 copy-start
  69.4 1.2 slice.38
  70.5 0.0 copy-start.6
  70.6 6.1 %collective-permute-done.8 = bf16[4,2,128,128]{3,2,1,0:T(8,128)(2,1)} collective-permute-done((bf16[4,2,128,128]{3,2,1,0:T(8,128)(2,1)}, bf16[4,2,128,128]{3,2,1,0:T(8,128)(2,1)}, u32[]{:S(2)}, u32[]{:S(2)}) %collective-permute-start.8) | collective-permute-done | bytes 262176 | tf_op jit(solution)/shard_map/ppermute | solution.py:513
  76.6 0.0 copy-done.5
  76.6 2.1 %pad_maximum_fusion = bf16[16,2,128,128]{3,2,1,0:T(8,128)(2,1)} fusion(bf16[4,2,128,128]{3,2,1,0:T(8,128)(2,1)} %collective-permute-done.8, bf16[4,2,128,128]{3,2,1,0:T(8,128)(2,1)S(1)} %copy-done.5, bf16[4,2,128,128]{3,2,1,0:T(8,128)(2,1)S(1)} %slice.38, bf16[4,2,128,128]{3,2,1,0:T(8,128)(2,1)} %slice.33.refs_12_), kind=kLoop, calls=%fused_computation | loop fusion | flops 1572864 | bytes 2097152 | tf_op jit(solution)/shard_map/concatenate | solution.py:570
  78.8 0.0 copy-start.4
  78.8 0.0 collective-permute-done.5.refs_2_.refs_10_
  78.8 5.7 %collective-permute-start.9 = (bf16[16,2,128,128]{3,2,1,0:T(8,128)(2,1)}, bf16[16,2,128,128]{3,2,1,0:T(8,128)(2,1)}, u32[]{:S(2)}, u32[]{:S(2)}) collective-permute-start(bf16[16,2,128,128]{3,2,1,0:T(8,128)(2,1)} %pad_maximum_fusion), channel_id=1, source_target_pairs={{0,1},{1,2},{2,3},{4,5},{5,6},{6,7},{8,9},{9,10},{10,11},{12,13},{... | collective-permute-start | bytes 3145736 | tf_op jit(solution)/shard_map/ppermute | solution.py:516
  84.4 1.7 shard_map.69
  86.2 0.0 copy-done
  86.2 0.0 copy-done.6
  86.2 4.1 %collective-permute-start.6 = (bf16[16,2,128,128]{3,2,1,0:T(8,128)(2,1)}, bf16[16,2,128,128]{3,2,1,0:T(8,128)(2,1)}, u32[]{:S(2)}, u32[]{:S(2)}) collective-permute-start(bf16[16,2,128,128]{3,2,1,0:T(8,128)(2,1)} %shard_map.69), channel_id=1, source_target_pairs={{8,16},{16,8},{9,17},{17,9},{10,18},{18,10},{11,19},{19,11},{12,20... | collective-permute-start | bytes 3145736 | tf_op jit(solution)/shard_map/ppermute | solution.py:510
  90.3 1.3 collective-permute-start.3
  91.6 0.1 reshape.25
  91.7 0.1 reduce_sum.9
  91.8 0.7 fusion.1
  95.1 2.0 %pad_maximum_fusion.1.refs_13_ = bf16[12,2,128,128]{3,2,1,0:T(8,128)(2,1)} fusion(bf16[4,2,128,128]{3,2,1,0:T(8,128)(2,1)} %collective-permute-done.8, bf16[4,2,128,128]{3,2,1,0:T(8,128)(2,1)S(1)} %copy-done.5, bf16[4,2,128,128]{3,2,1,0:T(8,128)(2,1)} %copy-done.6), kind=kLoop, calls=%fused_computation.2 | loop fusion | flops 786432 | bytes 1572864 | tf_op jit(solution)/shard_map/concatenate | solution.py:569
  97.1 8.3 %collective-permute-done.3.refs_5_ = bf16[2,128,1024]{2,1,0:T(8,128)(2,1)S(1)} collective-permute-done((bf16[2,128,1024]{2,1,0:T(8,128)(2,1)S(1)}, bf16[2,128,1024]{2,1,0:T(8,128)(2,1)S(1)}, u32[]{:S(2)}, u32[]{:S(2)}) %collective-permute-start.3) | collective-permute-done | bytes 524320 | tf_op jit(solution)/shard_map/ppermute | solution.py:507
  105.4 0.0 collective-permute-done.7.refs_11_
  105.4 0.0 collective-permute-done.9.refs_14_
  105.4 0.0 copy-done.4
  105.4 35.6 %shard_map.70 = (f32[8,1,1024]{2,1,0:T(1,128)S(1)}, f32[8,1,1024]{2,1,0:T(1,128)S(1)}, f32[8,128,1024]{2,1,0:T(8,128)}) custom-call(s32[8]{0:T(128)S(1)} %stack.43.who_ref.refs_0_, s32[16]{0:T(128)S(1)} %get-tuple-element.102.refs_1_.count_ref, ...), custom_call_target="tpu_custom_call", output_to_operand_aliasing={{0}: (15, {}), {1}: (16, {}), {2}: (17, {})} | custom-call | flops 1000 | bytes 1000 | tf_op jit(solution)/shard_map/pallas_call | solution.py:462
  141.0 0.0 collective-permute-done.6
  141.0 8.6 %conditional.1 = ((bf16[64,4096]{1,0:T(8,128)(2,1)}, bf16[64,4096]{1,0:T(8,128)(2,1)}, bf16[64,4096]{1,0:T(8,128)(2,1)}, bf16[64,4096]{1,0:T(8,128)(2,1)})) conditional(s32[]{:T(128)} %bitcast.15, (s32[8]{0:T(128)S(1)}, s32[16]{0:T(128)S(1)}, bf16[2,128,1024]{2,1,0:T(8,128)(2,1)S(1)}, bf16[2,128,1024]{2,1,0:T(8,128)(2,1)S(1)}, ...), branch_computations={%region_1.2_spmd, %region_2.3_spmd} | conditional | flops 1000 | bytes 8389684 | solution.py:605
  141.0 8.3 %branch_0_fun.1 = (bf16[64,4096]{1,0:T(8,128)(2,1)}, bf16[64,4096]{1,0:T(8,128)(2,1)}, bf16[64,4096]{1,0:T(8,128)(2,1)}, bf16[64,4096]{1,0:T(8,128)(2,1)}) custom-call(s32[8]{0:T(128)S(1)} %get-tuple-element.47.refs_0_, s32[16]{0:T(128)S(1)} %get-tuple-element.48.refs_1_, bf16[2,128,1024]{2,1,0:T(8,128)(2,1)S(1)} %get-tuple-element.49.refs_2_, ...), custom_call_target="tpu_custom_call" | custom-call | flops 1000 | bytes 1000 | tf_op jit(solution)/shard_map/cond/branch_0_fun/pallas_call | solution.py:462
  149.6 1.3 collective-permute-start.10
  151.0 2.7 %collective-permute-start.11 = (bf16[64,4096]{1,0:T(8,128)(2,1)}, bf16[64,4096]{1,0:T(8,128)(2,1)S(1)}, u32[]{:S(2)}, u32[]{:S(2)}) collective-permute-start(bf16[64,4096]{1,0:T(8,128)(2,1)} %get-tuple-element.132), channel_id=1, source_target_pairs={{8,12},{12,8},{16,20},{20,16},{9,13},{13,9},{17,21},{21,17},{10,14... | collective-permute-start | bytes 1572872 | tf_op jit(solution)/shard_map/ppermute | solution.py:619
  153.7 1.3 collective-permute-start.12
  155.0 8.0 %collective-permute-done.10 = bf16[64,4096]{1,0:T(8,128)(2,1)S(1)} collective-permute-done((bf16[64,4096]{1,0:T(8,128)(2,1)}, bf16[64,4096]{1,0:T(8,128)(2,1)S(1)}, u32[]{:S(2)}, u32[]{:S(2)}) %collective-permute-start.10) | collective-permute-done | bytes 524320 | tf_op jit(solution)/shard_map/ppermute | solution.py:617
  163.0 1.1 collective-permute-done.11
  164.1 6.5 %collective-permute-done.12 = bf16[64,4096]{1,0:T(8,128)(2,1)S(1)} collective-permute-done((bf16[64,4096]{1,0:T(8,128)(2,1)}, bf16[64,4096]{1,0:T(8,128)(2,1)S(1)}, u32[]{:S(2)}, u32[]{:S(2)}) %collective-permute-start.12) | collective-permute-done | bytes 524320 | tf_op jit(solution)/shard_map/ppermute | solution.py:618
  170.6 1.2 broadcast_select_fusion.3
  171.7 1.0 maximum_bitcast_fusion
Async XLA Ops:
  3.0 14.7 %collective-permute-start.1 = (bf16[2,128,1024]{2,1,0:T(8,128)(2,1)S(1)}, bf16[2,128,1024]{2,1,0:T(8,128)(2,1)S(1)}, u32[]{:S(2)}, u32[]{:S(2)}) collective-permute-start(bf16[2,128,1024]{2,1,0:T(8,128)(2,1)S(1)} %reshape.22.refs_2_), channel_id=1, source_target_pairs={{0,8},{24,16},{1,9},{25,17},{2,10},{26,18},{3,11},{27,19},{4,12},{... | collective-permute-start | bytes 1572872 | tf_op jit(solution)/shard_map/ppermute | solution.py:507
  11.9 31.3 %collective-permute-start.4 = (bf16[20,2,128,128]{3,2,1,0:T(8,128)(2,1)}, bf16[20,2,128,128]{3,2,1,0:T(8,128)(2,1)}, u32[]{:S(2)}, u32[]{:S(2)}) collective-permute-start(bf16[20,2,128,128]{3,2,1,0:T(8,128)(2,1)} %get-tuple-element.106.refs_5_.refs_6_), channel_id=1, source_target_pairs={{8,16},{16,8},{9,17},{17,9},{10,18},{18,10},{11,19},{19,11},{12,20... | collective-permute-start | bytes 3932168 | tf_op jit(solution)/shard_map/ppermute | solution.py:510
  17.7 6.5 %copy-start.2 = (bf16[2,128,1024]{2,1,0:T(8,128)(2,1)}, bf16[2,128,1024]{2,1,0:T(8,128)(2,1)S(1)}, u32[]{:S(2)}) copy-start(bf16[2,128,1024]{2,1,0:T(8,128)(2,1)S(1)} %collective-permute-done.1.refs_4_) | copy-start | bytes 1572868
  17.7 30.8 %collective-permute-start.2 = (bf16[20,2,128,128]{3,2,1,0:T(8,128)(2,1)}, bf16[20,2,128,128]{3,2,1,0:T(8,128)(2,1)S(1)}, u32[]{:S(2)}, u32[]{:S(2)}) collective-permute-start(bf16[20,2,128,128]{3,2,1,0:T(8,128)(2,1)} %get-tuple-element.106.refs_5_.refs_6_), channel_id=1, source_target_pairs={{0,8},{24,16},{1,9},{25,17},{2,10},{26,18},{3,11},{27,19},{4,12},{... | collective-permute-start | bytes 3932168 | tf_op jit(solution)/shard_map/ppermute | solution.py:507
  19.9 58.9 %collective-permute-start.5 = (bf16[16,2,128,128]{3,2,1,0:T(8,128)(2,1)S(1)}, bf16[16,2,128,128]{3,2,1,0:T(8,128)(2,1)}, u32[]{:S(2)}, u32[]{:S(2)}) collective-permute-start(bf16[16,2,128,128]{3,2,1,0:T(8,128)(2,1)S(1)} %shard_map.65.refs_6_.refs_0_.refs_7_), channel_id=1, source_target_pairs={{0,8},{24,16},{1,9},{25,17},{2,10},{26,18},{3,11},{27,19},{4,12},{... | collective-permute-start | bytes 3145736 | tf_op jit(solution)/shard_map/ppermute | solution.py:507
  22.9 53.7 %collective-permute-start.8 = (bf16[4,2,128,128]{3,2,1,0:T(8,128)(2,1)}, bf16[4,2,128,128]{3,2,1,0:T(8,128)(2,1)}, u32[]{:S(2)}, u32[]{:S(2)}) collective-permute-start(bf16[4,2,128,128]{3,2,1,0:T(8,128)(2,1)} %slice.33.refs_12_), channel_id=1, source_target_pairs={{0,16},{24,8},{1,17},{25,9},{2,18},{26,10},{3,19},{27,11},{4,20},{... | collective-permute-start | bytes 786440 | tf_op jit(solution)/shard_map/ppermute | solution.py:513
  37.6 17.1 %copy-start.3 = (bf16[2,128,1024]{2,1,0:T(8,128)(2,1)S(1)}, bf16[2,128,1024]{2,1,0:T(8,128)(2,1)}, u32[]{:S(2)}) copy-start(bf16[2,128,1024]{2,1,0:T(8,128)(2,1)} %copy-done.2) | copy-start | bytes 1572868
  48.5 1.1 copy-start.1
  52.6 52.7 %collective-permute-start.7 = (bf16[16,2,128,128]{3,2,1,0:T(8,128)(2,1)}, bf16[16,2,128,128]{3,2,1,0:T(8,128)(2,1)}, u32[]{:S(2)}, u32[]{:S(2)}) collective-permute-start(bf16[16,2,128,128]{3,2,1,0:T(8,128)(2,1)} %shard_map.67), channel_id=1, source_target_pairs={{8,16},{16,8},{9,17},{17,9},{10,18},{18,10},{11,19},{19,11},{12,20... | collective-permute-start | bytes 3145736 | tf_op jit(solution)/shard_map/ppermute | solution.py:510
  54.7 21.9 %copy-start.5 = (bf16[4,2,128,128]{3,2,1,0:T(8,128)(2,1)S(1)}, bf16[4,2,128,128]{3,2,1,0:T(8,128)(2,1)}, u32[]{:S(2)}) copy-start(bf16[4,2,128,128]{3,2,1,0:T(8,128)(2,1)} %slice.39) | copy-start | bytes 786436
  69.4 16.8 %copy-start = (f32[8,128,1024]{2,1,0:T(8,128)}, f32[8,128,1024]{2,1,0:T(8,128)S(1)}, u32[]{:S(2)}) copy-start(f32[8,128,1024]{2,1,0:T(8,128)S(1)} %get-tuple-element.125.refs_17_) | copy-start | bytes 12582916
  70.5 15.6 %copy-start.6 = (bf16[4,2,128,128]{3,2,1,0:T(8,128)(2,1)}, bf16[4,2,128,128]{3,2,1,0:T(8,128)(2,1)S(1)}, u32[]{:S(2)}) copy-start(bf16[4,2,128,128]{3,2,1,0:T(8,128)(2,1)S(1)} %slice.38) | copy-start | bytes 786436
  78.8 26.6 %copy-start.4 = (bf16[2,128,1024]{2,1,0:T(8,128)(2,1)S(1)}, bf16[2,128,1024]{2,1,0:T(8,128)(2,1)}, u32[]{:S(2)}) copy-start(bf16[2,128,1024]{2,1,0:T(8,128)(2,1)} %copy-done.2) | copy-start | bytes 1572868
  78.8 26.6 %collective-permute-start.9 = (bf16[16,2,128,128]{3,2,1,0:T(8,128)(2,1)}, bf16[16,2,128,128]{3,2,1,0:T(8,128)(2,1)}, u32[]{:S(2)}, u32[]{:S(2)}) collective-permute-start(bf16[16,2,128,128]{3,2,1,0:T(8,128)(2,1)} %pad_maximum_fusion), channel_id=1, source_target_pairs={{0,1},{1,2},{2,3},{4,5},{5,6},{6,7},{8,9},{9,10},{10,11},{12,13},{... | collective-permute-start | bytes 3145736 | tf_op jit(solution)/shard_map/ppermute | solution.py:516
  86.2 54.8 %collective-permute-start.6 = (bf16[16,2,128,128]{3,2,1,0:T(8,128)(2,1)}, bf16[16,2,128,128]{3,2,1,0:T(8,128)(2,1)}, u32[]{:S(2)}, u32[]{:S(2)}) collective-permute-start(bf16[16,2,128,128]{3,2,1,0:T(8,128)(2,1)} %shard_map.69), channel_id=1, source_target_pairs={{8,16},{16,8},{9,17},{17,9},{10,18},{18,10},{11,19},{19,11},{12,20... | collective-permute-start | bytes 3145736 | tf_op jit(solution)/shard_map/ppermute | solution.py:510
  90.3 15.1 %collective-permute-start.3 = (bf16[2,128,1024]{2,1,0:T(8,128)(2,1)S(1)}, bf16[2,128,1024]{2,1,0:T(8,128)(2,1)S(1)}, u32[]{:S(2)}, u32[]{:S(2)}) collective-permute-start(bf16[2,128,1024]{2,1,0:T(8,128)(2,1)S(1)} %reshape.26.refs_3_), channel_id=1, source_target_pairs={{0,8},{24,16},{1,9},{25,17},{2,10},{26,18},{3,11},{27,19},{4,12},{... | collective-permute-start | bytes 1572872 | tf_op jit(solution)/shard_map/ppermute | solution.py:507
  149.6 13.4 %collective-permute-start.10 = (bf16[64,4096]{1,0:T(8,128)(2,1)}, bf16[64,4096]{1,0:T(8,128)(2,1)S(1)}, u32[]{:S(2)}, u32[]{:S(2)}) collective-permute-start(bf16[64,4096]{1,0:T(8,128)(2,1)} %get-tuple-element.131), channel_id=1, source_target_pairs={{8,0},{12,4},{16,24},{20,28},{9,1},{13,5},{17,25},{21,29},{10,2},{... | collective-permute-start | bytes 1572872 | tf_op jit(solution)/shard_map/ppermute | solution.py:617
  151.0 13.1 %collective-permute-start.11 = (bf16[64,4096]{1,0:T(8,128)(2,1)}, bf16[64,4096]{1,0:T(8,128)(2,1)S(1)}, u32[]{:S(2)}, u32[]{:S(2)}) collective-permute-start(bf16[64,4096]{1,0:T(8,128)(2,1)} %get-tuple-element.132), channel_id=1, source_target_pairs={{8,12},{12,8},{16,20},{20,16},{9,13},{13,9},{17,21},{21,17},{10,14... | collective-permute-start | bytes 1572872 | tf_op jit(solution)/shard_map/ppermute | solution.py:619
  153.7 16.9 %collective-permute-start.12 = (bf16[64,4096]{1,0:T(8,128)(2,1)}, bf16[64,4096]{1,0:T(8,128)(2,1)S(1)}, u32[]{:S(2)}, u32[]{:S(2)}) collective-permute-start(bf16[64,4096]{1,0:T(8,128)(2,1)} %get-tuple-element.133), channel_id=1, source_target_pairs={{8,4},{12,0},{16,28},{20,24},{9,5},{13,1},{17,29},{21,25},{10,6},{... | collective-permute-start | bytes 1572872 | tf_op jit(solution)/shard_map/ppermute | solution.py:618

commit v4 on v3

--- a/solution.py
+++ b/solution.py
@@ -244,7 +244,7 @@
     query_in = [refs.pop(0) for _ in range(n_query)]
     buffers = [refs.pop(0) for _ in layout]
     if new:
-        cur_own, cur_rest, prior = (refs.pop(0) for _ in range(3))
+        cur, prior = refs.pop(0), refs.pop(0)
     state_in = [refs.pop(0) for _ in range(n_state)]
     outs = [refs.pop(0) for _ in range(4 if last else 3)]
     queries, peak_ref, total_ref, accum_ref, units, unit_sems, state_sems, query_sems = refs
@@ -280,23 +280,23 @@
         )
 
         def both():
-            pairs = [choose(low, tile(prior, at + 1), tile(cur_rest, at)) for at in (1, 2)]
+            pairs = [choose(low, tile(prior, at), tile(cur, at)) for at in (2, 3)]
             update(turn, *join(*pairs))
 
         if group == 0:
-            update(turn, *join(tile(cur_own), tile(prior)), mask)
+            update(turn, *join(tile(cur), tile(prior)), mask)
 
             @pl.when(low | has_prior)
             def _():
-                update(turn, *choose(low, tile(cur_rest), tile(prior, 1)))
+                update(turn, *choose(low, tile(cur, 1), tile(prior, 1)))
 
             pl.when(jnp.logical_not(low) | has_prior)(both)
         else:
-            update(turn, *join(tile(cur_rest), tile(prior, 1)), mask)
+            update(turn, *join(tile(cur, 1), tile(prior, 1)), mask)
 
             @pl.when(jnp.logical_not(low) | has_prior)
             def _():
-                update(turn, *choose(low, tile(prior), tile(cur_own)))
+                update(turn, *choose(low, tile(prior), tile(cur)))
                 both()
 
     @pl.when(who_ref[MIDDLE] == 1)
@@ -565,9 +565,10 @@
     def pinned(buffers, before):
         return [buffer[:3] + (after(buffer[3], before[0]),) for buffer in buffers]
 
+    by_owner = counts.reshape(-1, heads).sum(axis=1)
+    over = jnp.maximum(by_owner[0] + by_owner[1], by_owner[2] + by_owner[3]) > sum(CHUNKS)
+    own_t[0] = after(own_t[0], over)
     state = list(call([mine + (0, False, True), first + (0, False, True)], own_t + [early], stage(own), None))
-    rest = jnp.concatenate([part[:TILE] for part in (end_0, stream_0, far_tile)])
-    tiles = (tile, rest, onward(jnp.concatenate([tile, rest])))
     state = send_chunk(1, own[1:] + ends[:1], state)
     state = list(
         call(
@@ -577,14 +578,24 @@
             state,
         )
     )
+    tiles = jnp.concatenate([own_0[:TILE], end_0[:TILE], stream_0[:TILE], after(far_tile, state[0])])
+    tiles = (tiles, onward(tiles))
     state = send_chunk(2, own[1:] + ends, state)
+    state = list(
+        call(
+            [mine + (0, True, False), first + (0, True, False)],
+            own_t + [early],
+            stage(ends[1:] + streams[1:2], state),
+            state, tiles=tiles,
+        )
+    )
     late = after(late, state[0])
     both_t = own_t + [early, late]
     state = list(
         call(
-            [mine + (1, True, False), first + (1, True, False), second + (0, True, True)],
-            both_t,
-            stage(own + streams[:1] + ends[:1]) + [buffer + (1,) for buffer in pinned(ends[1:] + streams[1:2], state)],
+            [second + (0, True, True)],
+            [late],
+            stage(own + streams[:1] + ends + streams[1:2], state),
             state,
             tiles=tiles,
         )
@@ -600,8 +611,6 @@
     def exceeds(piece, state):
         return final(last_streams + [(EXTRA, places[-1], 0, across(piece), 0)], state)
 
-    by_owner = counts.reshape(-1, heads).sum(axis=1)
-    over = jnp.maximum(by_owner[0] + by_owner[1], by_owner[2] + by_owner[3]) > sum(CHUNKS)
     keep_own, send_own, keep_end, send_end = lax.cond(over, exceeds, fits, own_1, tuple(state))
 
     n_head = lax.axis_size("head")

time: 176 us -> 167 us (0.949); the launches traced: 173 us -> 166 us
  waiting for transfers between devices: 42.4 us -> 33.3 us
  Pallas kernels: 81.5 us -> 88 us
  local copies, waits for them, and re-layouts: 13.1 us -> 9.38 us
  other arithmetic: 6.48 us -> 4.5 us
    ppermute x4, waiting for transfers between devices: 15.2 us -> 5.77 us  [inward(): return lax.ppermute(value, 'mem', [(0, 1), (3, 2)])]
    pallas_call x4 -> x5, Pallas kernels: 68.3 us -> 74.3 us  [attend_call(): pl.pallas_call(functools.partial(attend_kernel, scale, chunks, layout, le...]
    ppermute x1, waiting for transfers between devices: 0.01 us -> 4.72 us  [onward(): lax.ppermute(value, 'span', [(at, at + 1) for at in range(lax.axis_size('...]
    concatenate x2 -> x1, other arithmetic: 4.15 us -> 2.17 us  [line_of_four(): jnp.concatenate([own_0[:TILE], end_0[:TILE], stream_0[:TILE], after(far_t...]
    ppermute x3, waiting for transfers between devices: 5.5 us -> 3.56 us  [across(): return lax.ppermute(value, 'mem', [(1, 2), (2, 1)])]
    slice x3 -> x4, local copies, waits for them, and re-layouts: 4.52 us -> 2.67 us  [the longest x1 1.7 us: line_of_four(): own_0[:TILE]]
  transfers between devices with their start and end apart: 12 -> 12, of which waited for: 8 -> 7; matrix products, arithmetic and copies ran while one was open for 8% -> 5% of each run, Pallas kernels for 42% -> 47%
where the time goes in v4:
time: 167 us; the launch traced here: 166 us
  Pallas kernels  88 us (53%)
  waiting for transfers between devices  33.3 us (20%)
  starting transfers between devices  27.8 us (17%)
  local copies, waits for them, and re-layouts  9.38 us (6%)
  other arithmetic  4.5 us (3%)
  between operations  2.69 us (2%)
    pallas_call x5, Pallas kernels, attend_call(): pl.pallas_call(functools.partial(attend_kernel, scale, chunks, layout, le...  74.3 us
    pallas_call x2, Pallas kernels, gather(): pl.pallas_call(functools.partial(gather_kernel, units, pieces, first, til...  9.13 us
    ppermute x3, starting transfers between devices, across(): return lax.ppermute(value, 'mem', [(1, 2), (2, 1)])  9.02 us
    ppermute x1, waiting for transfers between devices, line_of_four(): swapped_end = lax.ppermute(send_end, axes, pairs([(1, 0, 1), (2, 3, 1)]))  7.21 us
    ppermute x1, waiting for transfers between devices, line_of_four(): kept = lax.ppermute(keep_end, axes, pairs([(1, 0, 0), (2, 3, 0)]))  6.64 us
    ppermute x4, waiting for transfers between devices, inward(): return lax.ppermute(value, 'mem', [(0, 1), (3, 2)])  5.77 us
    ppermute x1, starting transfers between devices, onward(): lax.ppermute(value, 'span', [(at, at + 1) for at in range(lax.axis_size('...  5.63 us
    ppermute x1, waiting for transfers between devices, far(): return lax.ppermute(value, 'mem', [(0, 2), (3, 1)])  5.37 us
  transfers between devices with their start and end apart: 12, of which 7 were waited for; matrix products, arithmetic and copies ran while one was open for 5% of the time, Pallas kernels for 47%

profile of v4, /device:TPU:17, one launch (start us, length us, event | category | flops | bytes accessed | tf_op | source)
XLA Modules:
  0.0 166.0 jit_solution(7167296619735444866)
XLA Ops:
  0.0 1.4 fusion
  1.4 0.6 copy.16
  2.0 0.2 reshape.20.refs_2_
  2.2 1.3 collective-permute-start.1
  3.5 0.1 stack.43.who_ref.refs_0_
  3.6 8.2 %shard_map.64 = (s32[16]{0:T(128)S(1)}, s32[65]{0:T(128)}, bf16[20,2,128,128]{3,2,1,0:T(8,128)(2,1)}) custom-call(s32[8]{0:T(128)S(1)} %stack.43.who_ref.refs_0_, s32[4,16]{1,0:T(4,128)} %bitcast.32, bf16[32,512,128]{2,1,0:T(8,128)(2,1)} %bitcast.24, bf16[32,512,128]{2,1,0:T(8,128)(2,1)} %bitcast.26, bf16[512,128]{1,0:T(8,128)(2,1)} %bitcast.30, ...), custom_call_target="tpu_custom_call" | custom-call | flops 1000 | bytes 1000 | tf_op jit(solution)/shard_map/pallas_call | solution.py:142
  11.8 2.1 %collective-permute-start.5 = (bf16[20,2,128,128]{3,2,1,0:T(8,128)(2,1)}, bf16[20,2,128,128]{3,2,1,0:T(8,128)(2,1)}, u32[]{:S(2)}, u32[]{:S(2)}) collective-permute-start(bf16[20,2,128,128]{3,2,1,0:T(8,128)(2,1)} %get-tuple-element.140.refs_5_.refs_3_), channel_id=1, source_target_pairs={{8,16},{16,8},{9,17},{17,9},{10,18},{18,10},{11,19},{19,11},{12,20... | collective-permute-start | bytes 3932168 | tf_op jit(solution)/shard_map/ppermute | solution.py:510
  13.9 3.0 %collective-permute-done.1.refs_4_ = bf16[2,128,1024]{2,1,0:T(8,128)(2,1)S(1)} collective-permute-done((bf16[2,128,1024]{2,1,0:T(8,128)(2,1)S(1)}, bf16[2,128,1024]{2,1,0:T(8,128)(2,1)S(1)}, u32[]{:S(2)}, u32[]{:S(2)}) %collective-permute-start.1) | collective-permute-done | bytes 524320 | tf_op jit(solution)/shard_map/ppermute | solution.py:507
  16.9 0.0 copy-start.1
  16.9 1.3 collective-permute-start.2
  18.2 0.0 copy-done.1
  18.2 0.9 shard_map.65.refs_6_.refs_0_.refs_4_
  19.1 1.3 collective-permute-start.4
  20.4 1.7 %slice.34 = bf16[4,2,128,128]{3,2,1,0:T(8,128)(2,1)} slice(bf16[20,2,128,128]{3,2,1,0:T(8,128)(2,1)} %get-tuple-element.140.refs_5_.refs_3_), slice={[0:4], [0:2], [0:128], [0:128]} | slice | bytes 524288 | tf_op jit(solution)/shard_map/slice | solution.py:581
  22.1 1.3 collective-permute-start.7
  23.4 0.1 reshape.23
  23.5 0.1 reduce_sum.9
  23.6 0.6 fusion.1
  26.6 1.4 copy.17
  28.0 1.3 reshape.24.refs_3_
  29.3 0.0 copy-start.2
  29.3 11.1 %shard_map.66 = (f32[8,1,1024]{2,1,0:T(1,128)S(1)}, f32[8,1,1024]{2,1,0:T(1,128)S(1)}, f32[8,128,1024]{2,1,0:T(8,128)}) custom-call(s32[8]{0:T(128)S(1)} %stack.43.who_ref.refs_0_, s32[16]{0:T(128)S(1)} %get-tuple-element.113.refs_1_.count_ref, bf16[2,128,1024]{2,1,0:T(8,128)(2,1)S(1)} %reshape.20.refs_2_, bf16[2,128,1024]{2,1,0:T(8,128)(2,1)S(1)} %reshape.24.refs_3_, ...), custom_call_target="tpu_custom_call" | custom-call | flops 1000 | bytes 1000 | tf_op jit(solution)/shard_map/pallas_call | solution.py:462
  40.4 3.6 %collective-permute-done.5.refs_5_ = bf16[20,2,128,128]{3,2,1,0:T(8,128)(2,1)} collective-permute-done((bf16[20,2,128,128]{3,2,1,0:T(8,128)(2,1)}, bf16[20,2,128,128]{3,2,1,0:T(8,128)(2,1)}, u32[]{:S(2)}, u32[]{:S(2)}) %collective-permute-start.5) | collective-permute-done | bytes 1310752 | tf_op jit(solution)/shard_map/ppermute | solution.py:510
  44.0 1.0 slice.40
  44.9 2.8 %collective-permute-done.2.refs_1_.refs_6_ = bf16[20,2,128,128]{3,2,1,0:T(8,128)(2,1)S(1)} collective-permute-done((bf16[20,2,128,128]{3,2,1,0:T(8,128)(2,1)}, bf16[20,2,128,128]{3,2,1,0:T(8,128)(2,1)S(1)}, u32[]{:S(2)}, u32[]{:S(2)}) %collective-permute-start.2) | collective-permute-done | bytes 1310752 | tf_op jit(solution)/shard_map/ppermute | solution.py:507
  47.7 0.0 copy-start
  47.7 1.1 copy-done
  48.8 2.8 %shard_map.67 = bf16[16,2,128,128]{3,2,1,0:T(8,128)(2,1)} custom-call(s32[8]{0:T(128)S(1)} %stack.43.who_ref.refs_0_, s32[16]{0:T(128)S(1)} %get-tuple-element.113.refs_1_.count_ref, bf16[16,2,128,128]{3,2,1,0:T(8,128)(2,1)S(1)} %shard_map.65.refs_6_.refs_0_.refs_4_, bf16[20,2,128,128]{3,2,1,0:T(8,128)(2,1)} %copy-done), custom_call_target="tpu_custom_call" | custom-call | flops 1000 | bytes 1000 | tf_op jit(solution)/shard_map/pallas_call | solution.py:214
  51.6 2.7 %collective-permute-start.6 = (bf16[16,2,128,128]{3,2,1,0:T(8,128)(2,1)}, bf16[16,2,128,128]{3,2,1,0:T(8,128)(2,1)}, u32[]{:S(2)}, u32[]{:S(2)}) collective-permute-start(bf16[16,2,128,128]{3,2,1,0:T(8,128)(2,1)} %shard_map.67), channel_id=1, source_target_pairs={{8,16},{16,8},{9,17},{17,9},{10,18},{18,10},{11,19},{19,11},{12,20... | collective-permute-start | bytes 3145736 | tf_op jit(solution)/shard_map/ppermute | solution.py:510
  54.3 0.0 copy-done.2
  54.3 0.0 slice-start
  54.3 16.2 %shard_map.68 = (f32[8,1,1024]{2,1,0:T(1,128)S(1)}, f32[8,1,1024]{2,1,0:T(1,128)S(1)}, f32[8,128,1024]{2,1,0:T(8,128)}) custom-call(s32[8]{0:T(128)S(1)} %stack.43.who_ref.refs_0_, s32[16]{0:T(128)S(1)} %get-tuple-element.113.refs_1_.count_ref, ...), custom_call_target="tpu_custom_call", output_to_operand_aliasing={{0}: (7, {}), {1}: (8, {}), {2}: (9, {})} | custom-call | flops 1000 | bytes 1000 | tf_op jit(solution)/shard_map/pallas_call | solution.py:462
  70.5 0.0 copy-start.3
  70.5 5.4 %collective-permute-done.7 = bf16[4,2,128,128]{3,2,1,0:T(8,128)(2,1)} collective-permute-done((bf16[4,2,128,128]{3,2,1,0:T(8,128)(2,1)}, bf16[4,2,128,128]{3,2,1,0:T(8,128)(2,1)}, u32[]{:S(2)}, u32[]{:S(2)}) %collective-permute-start.7) | collective-permute-done | bytes 262176 | tf_op jit(solution)/shard_map/ppermute | solution.py:513
  75.8 0.0 slice-done
  75.8 2.2 %pad_maximum_fusion.refs_7_.refs_9_ = bf16[16,2,128,128]{3,2,1,0:T(8,128)(2,1)} fusion(bf16[4,2,128,128]{3,2,1,0:T(8,128)(2,1)} %collective-permute-done.7, bf16[4,2,128,128]{3,2,1,0:T(8,128)(2,1)S(1)} %slice.40, bf16[4,2,128,128]{3,2,1,0:T(8,128)(2,1)S(1)} %slice-done, bf16[4,2,128,128]{3,2,1,0:T(8,128)(2,1)} %slice.34), kind=kLoop, calls=%fused_computation | loop fusion | flops 1572864 | bytes 2097152 | tf_op jit(solution)/shard_map/concatenate | solution.py:581
  78.0 5.6 %collective-permute-start.8 = (bf16[16,2,128,128]{3,2,1,0:T(8,128)(2,1)}, bf16[16,2,128,128]{3,2,1,0:T(8,128)(2,1)}, u32[]{:S(2)}, u32[]{:S(2)}) collective-permute-start(bf16[16,2,128,128]{3,2,1,0:T(8,128)(2,1)} %pad_maximum_fusion.refs_7_.refs_9_), channel_id=1, source_target_pairs={{0,1},{1,2},{2,3},{4,5},{5,6},{6,7},{8,9},{9,10},{10,11},{12,13},{... | collective-permute-start | bytes 3145736 | tf_op jit(solution)/shard_map/ppermute | solution.py:516
  83.6 0.0 collective-permute-done.4.refs_2_.refs_5_.refs_7_
  83.7 1.7 %shard_map.69 = bf16[16,2,128,128]{3,2,1,0:T(8,128)(2,1)} custom-call(s32[8]{0:T(128)S(1)} %stack.43.who_ref.refs_0_, s32[16]{0:T(128)S(1)} %get-tuple-element.113.refs_1_.count_ref, bf16[16,2,128,128]{3,2,1,0:T(8,128)(2,1)S(1)} %shard_map.65.refs_6_.refs_0_.refs_4_, bf16[20,2,128,128]{3,2,1,0:T(8,128)(2,1)} %copy-done, ...), custom_call_target="tpu_custom_call" | custom-call | flops 1000 | bytes 1000 | tf_op jit(solution)/shard_map/pallas_call | solution.py:214
  85.4 4.3 %collective-permute-start.9 = (bf16[16,2,128,128]{3,2,1,0:T(8,128)(2,1)}, bf16[16,2,128,128]{3,2,1,0:T(8,128)(2,1)}, u32[]{:S(2)}, u32[]{:S(2)}) collective-permute-start(bf16[16,2,128,128]{3,2,1,0:T(8,128)(2,1)} %shard_map.69), channel_id=1, source_target_pairs={{8,16},{16,8},{9,17},{17,9},{10,18},{18,10},{11,19},{19,11},{12,20... | collective-permute-start | bytes 3145736 | tf_op jit(solution)/shard_map/ppermute | solution.py:510
  89.7 1.3 collective-permute-start.3
  91.0 0.0 collective-permute-done.6.refs_6_.refs_8_
  91.0 4.7 %collective-permute-done.8.refs_8_.refs_10_ = bf16[16,2,128,128]{3,2,1,0:T(8,128)(2,1)} collective-permute-done((bf16[16,2,128,128]{3,2,1,0:T(8,128)(2,1)}, bf16[16,2,128,128]{3,2,1,0:T(8,128)(2,1)}, u32[]{:S(2)}, u32[]{:S(2)}) %collective-permute-start.8) | collective-permute-done | bytes 1048608 | tf_op jit(solution)/shard_map/ppermute | solution.py:516
  95.7 0.0 copy-done.3
  95.7 22.0 %shard_map.70 = (f32[8,1,1024]{2,1,0:T(1,128)S(1)}, f32[8,1,1024]{2,1,0:T(1,128)S(1)}, f32[8,128,1024]{2,1,0:T(8,128)}) custom-call(s32[8]{0:T(128)S(1)} %stack.43.who_ref.refs_0_, s32[16]{0:T(128)S(1)} %get-tuple-element.113.refs_1_.count_ref, ...), custom_call_target="tpu_custom_call", output_to_operand_aliasing={{0}: (9, {}), {1}: (10, {}), {2}: (11, {})} | custom-call | flops 1000 | bytes 1000 | tf_op jit(solution)/shard_map/pallas_call | solution.py:462
  117.7 0.0 collective-permute-done.3.refs_2_
  117.7 14.6 %shard_map.71 = (f32[8,1,1024]{2,1,0:T(1,128)S(1)}, f32[8,1,1024]{2,1,0:T(1,128)S(1)}, f32[8,128,1024]{2,1,0:T(8,128)}) custom-call(s32[8]{0:T(128)S(1)} %stack.43.who_ref.refs_0_, s32[16]{0:T(128)S(1)} %get-tuple-element.113.refs_1_.count_ref, ...), custom_call_target="tpu_custom_call", output_to_operand_aliasing={{0}: (11, {}), {1}: (12, {}), {2}: (13, {})} | custom-call | flops 1000 | bytes 1000 | tf_op jit(solution)/shard_map/pallas_call | solution.py:462
  132.4 0.0 collective-permute-done.9
  132.4 10.7 %conditional.1 = ((bf16[64,4096]{1,0:T(8,128)(2,1)}, bf16[64,4096]{1,0:T(8,128)(2,1)}, bf16[64,4096]{1,0:T(8,128)(2,1)}, bf16[64,4096]{1,0:T(8,128)(2,1)})) conditional(s32[]{:T(128)} %convert_element_type.9, (s32[8]{0:T(128)S(1)}, s32[16]{0:T(128)S(1)}, bf16[2,128,1024]{2,1,0:T(8,128)(2,1)S(1)}, bf16[2,128,1024]{2,1,0:T(8,128)(2,1)S(1)}, ...), branch_computations={%region_1.2_spmd, %region_2.3_spmd} | conditional | flops 1000 | bytes 8389684 | solution.py:614
  132.4 10.4 %branch_0_fun.1 = (bf16[64,4096]{1,0:T(8,128)(2,1)}, bf16[64,4096]{1,0:T(8,128)(2,1)}, bf16[64,4096]{1,0:T(8,128)(2,1)}, bf16[64,4096]{1,0:T(8,128)(2,1)}) custom-call(s32[8]{0:T(128)S(1)} %get-tuple-element.47.refs_0_, s32[16]{0:T(128)S(1)} %get-tuple-element.48.refs_1_, bf16[2,128,1024]{2,1,0:T(8,128)(2,1)S(1)} %get-tuple-element.49.refs_2_, ...), custom_call_target="tpu_custom_call" | custom-call | flops 1000 | bytes 1000 | tf_op jit(solution)/shard_map/cond/branch_0_fun/pallas_call | solution.py:462
  143.1 1.3 collective-permute-start.10
  144.4 4.1 %collective-permute-start.11 = (bf16[64,4096]{1,0:T(8,128)(2,1)}, bf16[64,4096]{1,0:T(8,128)(2,1)S(1)}, u32[]{:S(2)}, u32[]{:S(2)}) collective-permute-start(bf16[64,4096]{1,0:T(8,128)(2,1)} %get-tuple-element.154), channel_id=1, source_target_pairs={{8,12},{12,8},{16,20},{20,16},{9,13},{13,9},{17,21},{21,17},{10,14... | collective-permute-start | bytes 1572872 | tf_op jit(solution)/shard_map/ppermute | solution.py:628
  148.5 1.3 collective-permute-start.12
  149.9 6.6 %collective-permute-done.10 = bf16[64,4096]{1,0:T(8,128)(2,1)S(1)} collective-permute-done((bf16[64,4096]{1,0:T(8,128)(2,1)}, bf16[64,4096]{1,0:T(8,128)(2,1)S(1)}, u32[]{:S(2)}, u32[]{:S(2)}) %collective-permute-start.10) | collective-permute-done | bytes 524320 | tf_op jit(solution)/shard_map/ppermute | solution.py:626
  156.5 0.0 collective-permute-done.11
  156.6 7.2 %collective-permute-done.12 = bf16[64,4096]{1,0:T(8,128)(2,1)S(1)} collective-permute-done((bf16[64,4096]{1,0:T(8,128)(2,1)}, bf16[64,4096]{1,0:T(8,128)(2,1)S(1)}, u32[]{:S(2)}, u32[]{:S(2)}) %collective-permute-start.12) | collective-permute-done | bytes 524320 | tf_op jit(solution)/shard_map/ppermute | solution.py:627
  163.8 1.2 broadcast_select_fusion.3
  164.9 1.0 maximum_bitcast_fusion
Async XLA Ops:
  2.2 14.7 %collective-permute-start.1 = (bf16[2,128,1024]{2,1,0:T(8,128)(2,1)S(1)}, bf16[2,128,1024]{2,1,0:T(8,128)(2,1)S(1)}, u32[]{:S(2)}, u32[]{:S(2)}) collective-permute-start(bf16[2,128,1024]{2,1,0:T(8,128)(2,1)S(1)} %reshape.20.refs_2_), channel_id=1, source_target_pairs={{0,8},{24,16},{1,9},{25,17},{2,10},{26,18},{3,11},{27,19},{4,12},{... | collective-permute-start | bytes 1572872 | tf_op jit(solution)/shard_map/ppermute | solution.py:507
  11.8 32.1 %collective-permute-start.5 = (bf16[20,2,128,128]{3,2,1,0:T(8,128)(2,1)}, bf16[20,2,128,128]{3,2,1,0:T(8,128)(2,1)}, u32[]{:S(2)}, u32[]{:S(2)}) collective-permute-start(bf16[20,2,128,128]{3,2,1,0:T(8,128)(2,1)} %get-tuple-element.140.refs_5_.refs_3_), channel_id=1, source_target_pairs={{8,16},{16,8},{9,17},{17,9},{10,18},{18,10},{11,19},{19,11},{12,20... | collective-permute-start | bytes 3932168 | tf_op jit(solution)/shard_map/ppermute | solution.py:510
  16.9 1.3 copy-start.1
  16.9 30.8 %collective-permute-start.2 = (bf16[20,2,128,128]{3,2,1,0:T(8,128)(2,1)}, bf16[20,2,128,128]{3,2,1,0:T(8,128)(2,1)S(1)}, u32[]{:S(2)}, u32[]{:S(2)}) collective-permute-start(bf16[20,2,128,128]{3,2,1,0:T(8,128)(2,1)} %get-tuple-element.140.refs_5_.refs_3_), channel_id=1, source_target_pairs={{0,8},{24,16},{1,9},{25,17},{2,10},{26,18},{3,11},{27,19},{4,12},{... | collective-permute-start | bytes 3932168 | tf_op jit(solution)/shard_map/ppermute | solution.py:507
  19.1 64.5 %collective-permute-start.4 = (bf16[16,2,128,128]{3,2,1,0:T(8,128)(2,1)S(1)}, bf16[16,2,128,128]{3,2,1,0:T(8,128)(2,1)}, u32[]{:S(2)}, u32[]{:S(2)}) collective-permute-start(bf16[16,2,128,128]{3,2,1,0:T(8,128)(2,1)S(1)} %shard_map.65.refs_6_.refs_0_.refs_4_), channel_id=1, source_target_pairs={{0,8},{24,16},{1,9},{25,17},{2,10},{26,18},{3,11},{27,19},{4,12},{... | collective-permute-start | bytes 3145736 | tf_op jit(solution)/shard_map/ppermute | solution.py:507
  22.1 53.7 %collective-permute-start.7 = (bf16[4,2,128,128]{3,2,1,0:T(8,128)(2,1)}, bf16[4,2,128,128]{3,2,1,0:T(8,128)(2,1)}, u32[]{:S(2)}, u32[]{:S(2)}) collective-permute-start(bf16[4,2,128,128]{3,2,1,0:T(8,128)(2,1)} %slice.34), channel_id=1, source_target_pairs={{0,16},{24,8},{1,17},{25,9},{2,18},{26,10},{3,19},{27,11},{4,20},{... | collective-permute-start | bytes 786440 | tf_op jit(solution)/shard_map/ppermute | solution.py:513
  29.3 25.0 %copy-start.2 = (bf16[2,128,1024]{2,1,0:T(8,128)(2,1)S(1)}, bf16[2,128,1024]{2,1,0:T(8,128)(2,1)}, u32[]{:S(2)}) copy-start(bf16[2,128,1024]{2,1,0:T(8,128)(2,1)} %copy-done.1) | copy-start | bytes 1572868
  47.7 1.1 copy-start
  51.6 39.4 %collective-permute-start.6 = (bf16[16,2,128,128]{3,2,1,0:T(8,128)(2,1)}, bf16[16,2,128,128]{3,2,1,0:T(8,128)(2,1)}, u32[]{:S(2)}, u32[]{:S(2)}) collective-permute-start(bf16[16,2,128,128]{3,2,1,0:T(8,128)(2,1)} %shard_map.67), channel_id=1, source_target_pairs={{8,16},{16,8},{9,17},{17,9},{10,18},{18,10},{11,19},{19,11},{12,20... | collective-permute-start | bytes 3145736 | tf_op jit(solution)/shard_map/ppermute | solution.py:510
  54.3 21.6 %slice-start = ((bf16[20,2,128,128]{3,2,1,0:T(8,128)(2,1)}), bf16[4,2,128,128]{3,2,1,0:T(8,128)(2,1)S(1)}, s32[]{:S(2)}) async-start(bf16[20,2,128,128]{3,2,1,0:T(8,128)(2,1)} %copy-done), calls=%async_computation | async-start | bytes 524288 | tf_op jit(solution)/shard_map/slice | solution.py:581
  70.5 25.2 %copy-start.3 = (bf16[2,128,1024]{2,1,0:T(8,128)(2,1)S(1)}, bf16[2,128,1024]{2,1,0:T(8,128)(2,1)}, u32[]{:S(2)}) copy-start(bf16[2,128,1024]{2,1,0:T(8,128)(2,1)} %copy-done.1) | copy-start | bytes 1572868
  78.0 17.7 %collective-permute-start.8 = (bf16[16,2,128,128]{3,2,1,0:T(8,128)(2,1)}, bf16[16,2,128,128]{3,2,1,0:T(8,128)(2,1)}, u32[]{:S(2)}, u32[]{:S(2)}) collective-permute-start(bf16[16,2,128,128]{3,2,1,0:T(8,128)(2,1)} %pad_maximum_fusion.refs_7_.refs_9_), channel_id=1, source_target_pairs={{0,1},{1,2},{2,3},{4,5},{5,6},{6,7},{8,9},{9,10},{10,11},{12,13},{... | collective-permute-start | bytes 3145736 | tf_op jit(solution)/shard_map/ppermute | solution.py:516
  85.4 47.0 %collective-permute-start.9 = (bf16[16,2,128,128]{3,2,1,0:T(8,128)(2,1)}, bf16[16,2,128,128]{3,2,1,0:T(8,128)(2,1)}, u32[]{:S(2)}, u32[]{:S(2)}) collective-permute-start(bf16[16,2,128,128]{3,2,1,0:T(8,128)(2,1)} %shard_map.69), channel_id=1, source_target_pairs={{8,16},{16,8},{9,17},{17,9},{10,18},{18,10},{11,19},{19,11},{12,20... | collective-permute-start | bytes 3145736 | tf_op jit(solution)/shard_map/ppermute | solution.py:510
  89.7 28.1 %collective-permute-start.3 = (bf16[2,128,1024]{2,1,0:T(8,128)(2,1)S(1)}, bf16[2,128,1024]{2,1,0:T(8,128)(2,1)S(1)}, u32[]{:S(2)}, u32[]{:S(2)}) collective-permute-start(bf16[2,128,1024]{2,1,0:T(8,128)(2,1)S(1)} %reshape.24.refs_3_), channel_id=1, source_target_pairs={{0,8},{24,16},{1,9},{25,17},{2,10},{26,18},{3,11},{27,19},{4,12},{... | collective-permute-start | bytes 1572872 | tf_op jit(solution)/shard_map/ppermute | solution.py:507
  143.1 13.4 %collective-permute-start.10 = (bf16[64,4096]{1,0:T(8,128)(2,1)}, bf16[64,4096]{1,0:T(8,128)(2,1)S(1)}, u32[]{:S(2)}, u32[]{:S(2)}) collective-permute-start(bf16[64,4096]{1,0:T(8,128)(2,1)} %get-tuple-element.153), channel_id=1, source_target_pairs={{8,0},{12,4},{16,24},{20,28},{9,1},{13,5},{17,25},{21,29},{10,2},{... | collective-permute-start | bytes 1572872 | tf_op jit(solution)/shard_map/ppermute | solution.py:626
  144.4 12.1 %collective-permute-start.11 = (bf16[64,4096]{1,0:T(8,128)(2,1)}, bf16[64,4096]{1,0:T(8,128)(2,1)S(1)}, u32[]{:S(2)}, u32[]{:S(2)}) collective-permute-start(bf16[64,4096]{1,0:T(8,128)(2,1)} %get-tuple-element.154), channel_id=1, source_target_pairs={{8,12},{12,8},{16,20},{20,16},{9,13},{13,9},{17,21},{21,17},{10,14... | collective-permute-start | bytes 1572872 | tf_op jit(solution)/shard_map/ppermute | solution.py:628
  148.5 15.2 %collective-permute-start.12 = (bf16[64,4096]{1,0:T(8,128)(2,1)}, bf16[64,4096]{1,0:T(8,128)(2,1)S(1)}, u32[]{:S(2)}, u32[]{:S(2)}) collective-permute-start(bf16[64,4096]{1,0:T(8,128)(2,1)} %get-tuple-element.155), channel_id=1, source_target_pairs={{8,4},{12,0},{16,28},{20,24},{9,5},{13,1},{17,29},{21,25},{10,6},{... | collective-permute-start | bytes 1572872 | tf_op jit(solution)/shard_map/ppermute | solution.py:627

commit v5 on v4

--- a/solution.py
+++ b/solution.py
@@ -490,6 +490,36 @@
     )(who, counts, *queries, *arrays, *tile_args, *given)
 
 
+def join_kernel(who_ref, keep_own, kept, swapped_own, swapped_end, out_ref, sems):
+    width = keep_own.shape[1]
+    for middle, same, other in ((1, keep_own, swapped_own), (0, kept, swapped_end)):
+        for group in range(2):
+
+            @pl.when((who_ref[MIDDLE] == middle) & (who_ref[GROUP] == group))
+            def _(same=same, other=other, group=group):
+                copies = [
+                    pltpu.make_async_copy(part, out_ref.at[:, pl.ds(at * width, width)], sems.at[at])
+                    for at, part in ((group, same), (1 - group, other))
+                ]
+                for copy in copies:
+                    copy.start()
+                for copy in copies:
+                    copy.wait()
+
+
+def join_rows(who, *parts):
+    rows, width = parts[0].shape
+    return pl.pallas_call(
+        join_kernel,
+        out_shape=jax.ShapeDtypeStruct((rows, 2 * width), parts[0].dtype),
+        in_specs=[smem()] + [hbm()] * 4,
+        out_specs=vmem(),
+        scratch_shapes=[pltpu.SemaphoreType.DMA((2,))],
+        compiler_params=pltpu.CompilerParams(vmem_limit_bytes=VMEM),
+        cost_estimate=TINY,
+    )(who, *parts)
+
+
 def line_of_four(query, new_keys, new_values, memory_keys, memory_values, retrieved):
     queries = query[0]
     tokens, heads, group_size, width = queries.shape
@@ -626,11 +656,7 @@
     kept = lax.ppermute(keep_end, axes, pairs([(1, 0, 0), (2, 3, 0)]))
     swapped_end = lax.ppermute(send_end, axes, pairs([(1, 0, 1), (2, 3, 1)]))
     swapped_own = lax.ppermute(send_own, axes, pairs([(1, 1, 1), (2, 2, 1)]))
-    same = jnp.where(middle, keep_own, kept)
-    other = jnp.where(middle, swapped_own, swapped_end)
-    left = jnp.where(group == 0, same, other)
-    right = jnp.where(group == 0, other, same)
-    return jnp.concatenate([left, right], axis=1)[None]
+    return join_rows(who, keep_own, kept, swapped_own, swapped_end)[None]
 
 
 def shifted(value, axis, steps):

time: 167 us -> 168 us (level)
  the two profiles are of different devices: /device:TPU:17 before, /device:TPU:2 now
where the time goes in v5:
time: 168 us
  waiting for transfers between devices  96.7 us (58%)
  starting transfers between devices  32 us (19%)
  Pallas kernels  23.7 us (14%)
  local copies, waits for them, and re-layouts  10.3 us (6%)
  between operations  2.99 us (2%)
  other arithmetic  2.28 us (1%)
    ppermute x1, waiting for transfers between devices, line_of_four(): kept = lax.ppermute(keep_end, axes, pairs([(1, 0, 0), (2, 3, 0)]))  47.3 us
    ppermute x1, waiting for transfers between devices, far(): return lax.ppermute(value, 'mem', [(0, 2), (3, 1)])  20.5 us
    ppermute x4, starting transfers between devices, inward(): return lax.ppermute(value, 'mem', [(0, 1), (3, 2)])  19.7 us
    ppermute x4, waiting for transfers between devices, inward(): return lax.ppermute(value, 'mem', [(0, 1), (3, 2)])  15.3 us
    ppermute x1, waiting for transfers between devices, line_of_four(): swapped_end = lax.ppermute(send_end, axes, pairs([(1, 0, 1), (2, 3, 1)]))  9.27 us
    pallas_call x2, Pallas kernels, gather(): pl.pallas_call(functools.partial(gather_kernel, units, pieces, first, til...  9.14 us
    pallas_call x5, Pallas kernels, attend_call(): pl.pallas_call(functools.partial(attend_kernel, scale, chunks, layout, le...  8.47 us
    ppermute x3, starting transfers between devices, across(): return lax.ppermute(value, 'mem', [(1, 2), (2, 1)])  5.07 us
  transfers between devices with their start and end apart: 12, of which 7 were waited for; matrix products, arithmetic and copies ran while one was open for 5% of the time, Pallas kernels for 11%

profile of v5, /device:TPU:2, one launch (start us, length us, event | category | flops | bytes accessed | tf_op | source)
XLA Modules:
  0.0 168.2 jit_solution(6477272452809485070)
XLA Ops:
  0.0 1.4 fusion
  1.4 0.6 copy.16
  2.0 0.2 reshape.20.refs_2_
  2.2 3.5 %collective-permute-start.1 = (bf16[2,128,1024]{2,1,0:T(8,128)(2,1)S(1)}, bf16[2,128,1024]{2,1,0:T(8,128)(2,1)S(1)}, u32[]{:S(2)}, u32[]{:S(2)}) collective-permute-start(bf16[2,128,1024]{2,1,0:T(8,128)(2,1)S(1)} %reshape.20.refs_2_), channel_id=1, source_target_pairs={{0,8},{24,16},{1,9},{25,17},{2,10},{26,18},{3,11},{27,19},{4,12},{... | collective-permute-start | bytes 1572872 | tf_op jit(solution)/shard_map/ppermute | solution.py:537
  5.8 0.1 stack.43.who_ref.refs_0_
  5.8 8.2 %shard_map.64 = (s32[16]{0:T(128)S(1)}, s32[65]{0:T(128)}, bf16[20,2,128,128]{3,2,1,0:T(8,128)(2,1)}) custom-call(s32[8]{0:T(128)S(1)} %stack.43.who_ref.refs_0_, s32[4,16]{1,0:T(4,128)} %bitcast.31, bf16[32,512,128]{2,1,0:T(8,128)(2,1)} %bitcast.23, bf16[32,512,128]{2,1,0:T(8,128)(2,1)} %bitcast.25, bf16[512,128]{1,0:T(8,128)(2,1)} %bitcast.29, ...), custom_call_target="tpu_custom_call" | custom-call | flops 1000 | bytes 1000 | tf_op jit(solution)/shard_map/pallas_call | solution.py:142
  14.1 1.8 %collective-permute-start.5 = (bf16[20,2,128,128]{3,2,1,0:T(8,128)(2,1)}, bf16[20,2,128,128]{3,2,1,0:T(8,128)(2,1)}, u32[]{:S(2)}, u32[]{:S(2)}) collective-permute-start(bf16[20,2,128,128]{3,2,1,0:T(8,128)(2,1)} %get-tuple-element.140.refs_5_.refs_3_), channel_id=1, source_target_pairs={{8,16},{16,8},{9,17},{17,9},{10,18},{18,10},{11,19},{19,11},{12,20... | collective-permute-start | bytes 3932168 | tf_op jit(solution)/shard_map/ppermute | solution.py:540
  15.8 1.0 collective-permute-done.1.refs_4_
  16.9 0.0 copy-start.1
  16.9 4.5 %collective-permute-start.2 = (bf16[20,2,128,128]{3,2,1,0:T(8,128)(2,1)}, bf16[20,2,128,128]{3,2,1,0:T(8,128)(2,1)S(1)}, u32[]{:S(2)}, u32[]{:S(2)}) collective-permute-start(bf16[20,2,128,128]{3,2,1,0:T(8,128)(2,1)} %get-tuple-element.140.refs_5_.refs_3_), channel_id=1, source_target_pairs={{0,8},{24,16},{1,9},{25,17},{2,10},{26,18},{3,11},{27,19},{4,12},{... | collective-permute-start | bytes 3932168 | tf_op jit(solution)/shard_map/ppermute | solution.py:537
  21.3 0.0 copy-done.1
  21.3 0.9 shard_map.65.refs_6_.refs_0_.refs_4_
  22.3 4.9 %collective-permute-start.4 = (bf16[16,2,128,128]{3,2,1,0:T(8,128)(2,1)S(1)}, bf16[16,2,128,128]{3,2,1,0:T(8,128)(2,1)}, u32[]{:S(2)}, u32[]{:S(2)}) collective-permute-start(bf16[16,2,128,128]{3,2,1,0:T(8,128)(2,1)S(1)} %shard_map.65.refs_6_.refs_0_.refs_4_), channel_id=1, source_target_pairs={{0,8},{24,16},{1,9},{25,17},{2,10},{26,18},{3,11},{27,19},{4,12},{... | collective-permute-start | bytes 3145736 | tf_op jit(solution)/shard_map/ppermute | solution.py:537
  27.2 1.7 %slice.34 = bf16[4,2,128,128]{3,2,1,0:T(8,128)(2,1)} slice(bf16[20,2,128,128]{3,2,1,0:T(8,128)(2,1)} %get-tuple-element.140.refs_5_.refs_3_), slice={[0:4], [0:2], [0:128], [0:128]} | slice | bytes 524288 | tf_op jit(solution)/shard_map/slice | solution.py:611
  28.9 2.0 %collective-permute-start.7 = (bf16[4,2,128,128]{3,2,1,0:T(8,128)(2,1)}, bf16[4,2,128,128]{3,2,1,0:T(8,128)(2,1)}, u32[]{:S(2)}, u32[]{:S(2)}) collective-permute-start(bf16[4,2,128,128]{3,2,1,0:T(8,128)(2,1)} %slice.34), channel_id=1, source_target_pairs={{0,16},{24,8},{1,17},{25,9},{2,18},{26,10},{3,19},{27,11},{4,20},{... | collective-permute-start | bytes 786440 | tf_op jit(solution)/shard_map/ppermute | solution.py:543
  30.9 0.1 reshape.23
  31.0 0.1 reduce_sum.9
  31.1 0.7 fusion.1
  34.3 1.4 copy.17
  35.6 1.3 reshape.24.refs_3_
  36.9 0.0 copy-start.2
  36.9 0.9 shard_map.66
  37.9 0.0 collective-permute-done.5.refs_5_
  37.9 1.0 slice.40
  38.8 11.9 %collective-permute-done.2.refs_1_.refs_6_ = bf16[20,2,128,128]{3,2,1,0:T(8,128)(2,1)S(1)} collective-permute-done((bf16[20,2,128,128]{3,2,1,0:T(8,128)(2,1)}, bf16[20,2,128,128]{3,2,1,0:T(8,128)(2,1)S(1)}, u32[]{:S(2)}, u32[]{:S(2)}) %collective-permute-start.2) | collective-permute-done | bytes 1310752 | tf_op jit(solution)/shard_map/ppermute | solution.py:537
  50.8 0.0 copy-start
  50.8 1.1 copy-done
  51.9 1.7 shard_map.67
  53.5 1.6 collective-permute-start.6
  55.2 0.0 copy-done.2
  55.2 0.0 slice-start
  55.2 1.1 shard_map.68
  56.3 0.0 copy-start.3
  56.3 20.5 %collective-permute-done.7 = bf16[4,2,128,128]{3,2,1,0:T(8,128)(2,1)} collective-permute-done((bf16[4,2,128,128]{3,2,1,0:T(8,128)(2,1)}, bf16[4,2,128,128]{3,2,1,0:T(8,128)(2,1)}, u32[]{:S(2)}, u32[]{:S(2)}) %collective-permute-start.7) | collective-permute-done | bytes 262176 | tf_op jit(solution)/shard_map/ppermute | solution.py:543
  76.8 0.0 slice-done
  76.8 2.2 %pad_maximum_fusion.refs_7_.refs_9_ = bf16[16,2,128,128]{3,2,1,0:T(8,128)(2,1)} fusion(bf16[4,2,128,128]{3,2,1,0:T(8,128)(2,1)} %collective-permute-done.7, bf16[4,2,128,128]{3,2,1,0:T(8,128)(2,1)S(1)} %slice.40, bf16[4,2,128,128]{3,2,1,0:T(8,128)(2,1)S(1)} %slice-done, bf16[4,2,128,128]{3,2,1,0:T(8,128)(2,1)} %slice.34), kind=kLoop, calls=%fused_computation | loop fusion | flops 1572864 | bytes 2097152 | tf_op jit(solution)/shard_map/concatenate | solution.py:611
  79.0 1.9 %collective-permute-start.8 = (bf16[16,2,128,128]{3,2,1,0:T(8,128)(2,1)}, bf16[16,2,128,128]{3,2,1,0:T(8,128)(2,1)}, u32[]{:S(2)}, u32[]{:S(2)}) collective-permute-start(bf16[16,2,128,128]{3,2,1,0:T(8,128)(2,1)} %pad_maximum_fusion.refs_7_.refs_9_), channel_id=1, source_target_pairs={{0,1},{1,2},{2,3},{4,5},{5,6},{6,7},{8,9},{9,10},{10,11},{12,13},{... | collective-permute-start | bytes 3145736 | tf_op jit(solution)/shard_map/ppermute | solution.py:546
  80.9 0.0 collective-permute-done.4.refs_2_.refs_5_.refs_7_
  80.9 1.7 shard_map.69
  82.6 1.6 collective-permute-start.9
  84.2 6.8 %collective-permute-start.3 = (bf16[2,128,1024]{2,1,0:T(8,128)(2,1)S(1)}, bf16[2,128,1024]{2,1,0:T(8,128)(2,1)S(1)}, u32[]{:S(2)}, u32[]{:S(2)}) collective-permute-start(bf16[2,128,1024]{2,1,0:T(8,128)(2,1)S(1)} %reshape.24.refs_3_), channel_id=1, source_target_pairs={{0,8},{24,16},{1,9},{25,17},{2,10},{26,18},{3,11},{27,19},{4,12},{... | collective-permute-start | bytes 1572872 | tf_op jit(solution)/shard_map/ppermute | solution.py:537
  91.1 0.0 collective-permute-done.6.refs_6_.refs_8_
  91.1 4.3 %collective-permute-done.8.refs_8_.refs_10_ = bf16[16,2,128,128]{3,2,1,0:T(8,128)(2,1)} collective-permute-done((bf16[16,2,128,128]{3,2,1,0:T(8,128)(2,1)}, bf16[16,2,128,128]{3,2,1,0:T(8,128)(2,1)}, u32[]{:S(2)}, u32[]{:S(2)}) %collective-permute-start.8) | collective-permute-done | bytes 1048608 | tf_op jit(solution)/shard_map/ppermute | solution.py:546
  95.4 0.0 copy-done.3
  95.4 1.9 %shard_map.70 = (f32[8,1,1024]{2,1,0:T(1,128)S(1)}, f32[8,1,1024]{2,1,0:T(1,128)S(1)}, f32[8,128,1024]{2,1,0:T(8,128)}) custom-call(s32[8]{0:T(128)S(1)} %stack.43.who_ref.refs_0_, s32[16]{0:T(128)S(1)} %get-tuple-element.113.refs_1_.count_ref, ...), custom_call_target="tpu_custom_call", output_to_operand_aliasing={{0}: (9, {}), {1}: (10, {}), {2}: (11, {})} | custom-call | flops 1000 | bytes 1000 | tf_op jit(solution)/shard_map/pallas_call | solution.py:462
  97.4 2.4 %collective-permute-done.3.refs_2_ = bf16[2,128,1024]{2,1,0:T(8,128)(2,1)S(1)} collective-permute-done((bf16[2,128,1024]{2,1,0:T(8,128)(2,1)S(1)}, bf16[2,128,1024]{2,1,0:T(8,128)(2,1)S(1)}, u32[]{:S(2)}, u32[]{:S(2)}) %collective-permute-start.3) | collective-permute-done | bytes 524320 | tf_op jit(solution)/shard_map/ppermute | solution.py:537
  99.7 2.5 %shard_map.71 = (f32[8,1,1024]{2,1,0:T(1,128)S(1)}, f32[8,1,1024]{2,1,0:T(1,128)S(1)}, f32[8,128,1024]{2,1,0:T(8,128)}) custom-call(s32[8]{0:T(128)S(1)} %stack.43.who_ref.refs_0_, s32[16]{0:T(128)S(1)} %get-tuple-element.113.refs_1_.count_ref, ...), custom_call_target="tpu_custom_call", output_to_operand_aliasing={{0}: (11, {}), {1}: (12, {}), {2}: (13, {})} | custom-call | flops 1000 | bytes 1000 | tf_op jit(solution)/shard_map/pallas_call | solution.py:462
  102.2 0.0 collective-permute-done.9
  102.2 2.4 %conditional.1 = ((bf16[64,4096]{1,0:T(8,128)(2,1)S(1)}, bf16[64,4096]{1,0:T(8,128)(2,1)S(1)}, bf16[64,4096]{1,0:T(8,128)(2,1)}, bf16[64,4096]{1,0:T(8,128)(2,1)})) conditional(s32[]{:T(128)} %convert_element_type.9, (s32[8]{0:T(128)S(1)}, s32[16]{0:T(128)S(1)}, bf16[2,128,1024]{2,1,0:T(8,128)(2,1)S(1)}, bf16[2,128,1024]{2,1,0:T(8,128)(2,1)S(1)}, ...), branch_computations={%region_1.2_spmd, %region_2.3_spmd} | conditional | flops 1000 | bytes 8389684 | solution.py:644
  102.2 2.1 %branch_0_fun.1 = (bf16[64,4096]{1,0:T(8,128)(2,1)S(1)}, bf16[64,4096]{1,0:T(8,128)(2,1)S(1)}, bf16[64,4096]{1,0:T(8,128)(2,1)}, bf16[64,4096]{1,0:T(8,128)(2,1)}) custom-call(s32[8]{0:T(128)S(1)} %get-tuple-element.47.refs_0_, s32[16]{0:T(128)S(1)} %get-tuple-element.48.refs_1_, bf16[2,128,1024]{2,1,0:T(8,128)(2,1)S(1)} %get-tuple-element.49.refs_2_, ...), custom_call_target="tpu_custom_call" | custom-call | flops 1000 | bytes 1000 | tf_op jit(solution)/shard_map/cond/branch_0_fun/pallas_call | solution.py:462
  104.6 1.3 collective-permute-start.10
  105.9 0.7 collective-permute-start.11
  106.6 1.3 collective-permute-start.12
  107.9 47.3 %collective-permute-done.10.kept = bf16[64,4096]{1,0:T(8,128)(2,1)S(1)} collective-permute-done((bf16[64,4096]{1,0:T(8,128)(2,1)}, bf16[64,4096]{1,0:T(8,128)(2,1)S(1)}, u32[]{:S(2)}, u32[]{:S(2)}) %collective-permute-start.10) | collective-permute-done | bytes 524320 | tf_op jit(solution)/shard_map/ppermute | solution.py:656
  155.2 0.0 copy-start.5
  155.2 0.0 collective-permute-done.11.swapped_own
  155.2 0.0 copy-start.6
  155.2 9.3 %collective-permute-done.12.swapped_end = bf16[64,4096]{1,0:T(8,128)(2,1)S(1)} collective-permute-done((bf16[64,4096]{1,0:T(8,128)(2,1)}, bf16[64,4096]{1,0:T(8,128)(2,1)S(1)}, u32[]{:S(2)}, u32[]{:S(2)}) %collective-permute-start.12) | collective-permute-done | bytes 524320 | tf_op jit(solution)/shard_map/ppermute | solution.py:657
  164.4 0.0 copy-start.7
  164.4 0.0 copy-done.5
  164.4 0.0 copy-done.6
  164.4 0.8 copy-done.7
  165.3 2.7 %shard_map.72 = bf16[64,8192]{1,0:T(8,128)(2,1)} custom-call(s32[8]{0:T(128)S(1)} %stack.43.who_ref.refs_0_, bf16[64,4096]{1,0:T(8,128)(2,1)S(1)} %get-tuple-element.152.keep_own, bf16[64,4096]{1,0:T(8,128)(2,1)} %copy-done.5, bf16[64,4096]{1,0:T(8,128)(2,1)} %copy-done.6, bf16[64,4096]{1,0:T(8,128)(2,1)} %copy-done.7), custom_call_target="tpu_custom_call" | custom-call | flops 1000 | bytes 1000 | tf_op jit(solution)/shard_map/pallas_call | solution.py:512
Async XLA Ops:
  2.2 14.7 %collective-permute-start.1 = (bf16[2,128,1024]{2,1,0:T(8,128)(2,1)S(1)}, bf16[2,128,1024]{2,1,0:T(8,128)(2,1)S(1)}, u32[]{:S(2)}, u32[]{:S(2)}) collective-permute-start(bf16[2,128,1024]{2,1,0:T(8,128)(2,1)S(1)} %reshape.20.refs_2_), channel_id=1, source_target_pairs={{0,8},{24,16},{1,9},{25,17},{2,10},{26,18},{3,11},{27,19},{4,12},{... | collective-permute-start | bytes 1572872 | tf_op jit(solution)/shard_map/ppermute | solution.py:537
  14.1 23.8 %collective-permute-start.5 = (bf16[20,2,128,128]{3,2,1,0:T(8,128)(2,1)}, bf16[20,2,128,128]{3,2,1,0:T(8,128)(2,1)}, u32[]{:S(2)}, u32[]{:S(2)}) collective-permute-start(bf16[20,2,128,128]{3,2,1,0:T(8,128)(2,1)} %get-tuple-element.140.refs_5_.refs_3_), channel_id=1, source_target_pairs={{8,16},{16,8},{9,17},{17,9},{10,18},{18,10},{11,19},{19,11},{12,20... | collective-permute-start | bytes 3932168 | tf_op jit(solution)/shard_map/ppermute | solution.py:540
  16.9 4.5 %copy-start.1 = (bf16[2,128,1024]{2,1,0:T(8,128)(2,1)}, bf16[2,128,1024]{2,1,0:T(8,128)(2,1)S(1)}, u32[]{:S(2)}) copy-start(bf16[2,128,1024]{2,1,0:T(8,128)(2,1)S(1)} %collective-permute-done.1.refs_4_) | copy-start | bytes 1572868
  16.9 33.9 %collective-permute-start.2 = (bf16[20,2,128,128]{3,2,1,0:T(8,128)(2,1)}, bf16[20,2,128,128]{3,2,1,0:T(8,128)(2,1)S(1)}, u32[]{:S(2)}, u32[]{:S(2)}) collective-permute-start(bf16[20,2,128,128]{3,2,1,0:T(8,128)(2,1)} %get-tuple-element.140.refs_5_.refs_3_), channel_id=1, source_target_pairs={{0,8},{24,16},{1,9},{25,17},{2,10},{26,18},{3,11},{27,19},{4,12},{... | collective-permute-start | bytes 3932168 | tf_op jit(solution)/shard_map/ppermute | solution.py:537
  22.3 58.6 %collective-permute-start.4 = (bf16[16,2,128,128]{3,2,1,0:T(8,128)(2,1)S(1)}, bf16[16,2,128,128]{3,2,1,0:T(8,128)(2,1)}, u32[]{:S(2)}, u32[]{:S(2)}) collective-permute-start(bf16[16,2,128,128]{3,2,1,0:T(8,128)(2,1)S(1)} %shard_map.65.refs_6_.refs_0_.refs_4_), channel_id=1, source_target_pairs={{0,8},{24,16},{1,9},{25,17},{2,10},{26,18},{3,11},{27,19},{4,12},{... | collective-permute-start | bytes 3145736 | tf_op jit(solution)/shard_map/ppermute | solution.py:537
  28.9 48.0 %collective-permute-start.7 = (bf16[4,2,128,128]{3,2,1,0:T(8,128)(2,1)}, bf16[4,2,128,128]{3,2,1,0:T(8,128)(2,1)}, u32[]{:S(2)}, u32[]{:S(2)}) collective-permute-start(bf16[4,2,128,128]{3,2,1,0:T(8,128)(2,1)} %slice.34), channel_id=1, source_target_pairs={{0,16},{24,8},{1,17},{25,9},{2,18},{26,10},{3,19},{27,11},{4,20},{... | collective-permute-start | bytes 786440 | tf_op jit(solution)/shard_map/ppermute | solution.py:543
  36.9 18.3 %copy-start.2 = (bf16[2,128,1024]{2,1,0:T(8,128)(2,1)S(1)}, bf16[2,128,1024]{2,1,0:T(8,128)(2,1)}, u32[]{:S(2)}) copy-start(bf16[2,128,1024]{2,1,0:T(8,128)(2,1)} %copy-done.1) | copy-start | bytes 1572868
  50.8 1.1 copy-start
  53.5 37.6 %collective-permute-start.6 = (bf16[16,2,128,128]{3,2,1,0:T(8,128)(2,1)}, bf16[16,2,128,128]{3,2,1,0:T(8,128)(2,1)}, u32[]{:S(2)}, u32[]{:S(2)}) collective-permute-start(bf16[16,2,128,128]{3,2,1,0:T(8,128)(2,1)} %shard_map.67), channel_id=1, source_target_pairs={{8,16},{16,8},{9,17},{17,9},{10,18},{18,10},{11,19},{19,11},{12,20... | collective-permute-start | bytes 3145736 | tf_op jit(solution)/shard_map/ppermute | solution.py:540
  55.2 21.6 %slice-start = ((bf16[20,2,128,128]{3,2,1,0:T(8,128)(2,1)}), bf16[4,2,128,128]{3,2,1,0:T(8,128)(2,1)S(1)}, s32[]{:S(2)}) async-start(bf16[20,2,128,128]{3,2,1,0:T(8,128)(2,1)} %copy-done), calls=%async_computation | async-start | bytes 524288 | tf_op jit(solution)/shard_map/slice | solution.py:611
  56.3 39.1 %copy-start.3 = (bf16[2,128,1024]{2,1,0:T(8,128)(2,1)S(1)}, bf16[2,128,1024]{2,1,0:T(8,128)(2,1)}, u32[]{:S(2)}) copy-start(bf16[2,128,1024]{2,1,0:T(8,128)(2,1)} %copy-done.1) | copy-start | bytes 1572868
  79.0 16.4 %collective-permute-start.8 = (bf16[16,2,128,128]{3,2,1,0:T(8,128)(2,1)}, bf16[16,2,128,128]{3,2,1,0:T(8,128)(2,1)}, u32[]{:S(2)}, u32[]{:S(2)}) collective-permute-start(bf16[16,2,128,128]{3,2,1,0:T(8,128)(2,1)} %pad_maximum_fusion.refs_7_.refs_9_), channel_id=1, source_target_pairs={{0,1},{1,2},{2,3},{4,5},{5,6},{6,7},{8,9},{9,10},{10,11},{12,13},{... | collective-permute-start | bytes 3145736 | tf_op jit(solution)/shard_map/ppermute | solution.py:546
  82.6 19.6 %collective-permute-start.9 = (bf16[16,2,128,128]{3,2,1,0:T(8,128)(2,1)}, bf16[16,2,128,128]{3,2,1,0:T(8,128)(2,1)}, u32[]{:S(2)}, u32[]{:S(2)}) collective-permute-start(bf16[16,2,128,128]{3,2,1,0:T(8,128)(2,1)} %shard_map.69), channel_id=1, source_target_pairs={{8,16},{16,8},{9,17},{17,9},{10,18},{18,10},{11,19},{19,11},{12,20... | collective-permute-start | bytes 3145736 | tf_op jit(solution)/shard_map/ppermute | solution.py:540
  84.2 15.5 %collective-permute-start.3 = (bf16[2,128,1024]{2,1,0:T(8,128)(2,1)S(1)}, bf16[2,128,1024]{2,1,0:T(8,128)(2,1)S(1)}, u32[]{:S(2)}, u32[]{:S(2)}) collective-permute-start(bf16[2,128,1024]{2,1,0:T(8,128)(2,1)S(1)} %reshape.24.refs_3_), channel_id=1, source_target_pairs={{0,8},{24,16},{1,9},{25,17},{2,10},{26,18},{3,11},{27,19},{4,12},{... | collective-permute-start | bytes 1572872 | tf_op jit(solution)/shard_map/ppermute | solution.py:537
  104.6 50.6 %collective-permute-start.10 = (bf16[64,4096]{1,0:T(8,128)(2,1)}, bf16[64,4096]{1,0:T(8,128)(2,1)S(1)}, u32[]{:S(2)}, u32[]{:S(2)}) collective-permute-start(bf16[64,4096]{1,0:T(8,128)(2,1)} %get-tuple-element.153), channel_id=1, source_target_pairs={{8,0},{12,4},{16,24},{20,28},{9,1},{13,5},{17,25},{21,29},{10,2},{... | collective-permute-start | bytes 1572872 | tf_op jit(solution)/shard_map/ppermute | solution.py:656
  105.9 49.3 %collective-permute-start.11 = (bf16[64,4096]{1,0:T(8,128)(2,1)S(1)}, bf16[64,4096]{1,0:T(8,128)(2,1)S(1)}, u32[]{:S(2)}, u32[]{:S(2)}) collective-permute-start(bf16[64,4096]{1,0:T(8,128)(2,1)S(1)} %get-tuple-element.154), channel_id=1, source_target_pairs={{8,12},{12,8},{16,20},{20,16},{9,13},{13,9},{17,21},{21,17},{10,14... | collective-permute-start | bytes 1572872 | tf_op jit(solution)/shard_map/ppermute | solution.py:658
  106.6 57.8 %collective-permute-start.12 = (bf16[64,4096]{1,0:T(8,128)(2,1)}, bf16[64,4096]{1,0:T(8,128)(2,1)S(1)}, u32[]{:S(2)}, u32[]{:S(2)}) collective-permute-start(bf16[64,4096]{1,0:T(8,128)(2,1)} %get-tuple-element.155), channel_id=1, source_target_pairs={{8,4},{12,0},{16,28},{20,24},{9,5},{13,1},{17,29},{21,25},{10,6},{... | collective-permute-start | bytes 1572872 | tf_op jit(solution)/shard_map/ppermute | solution.py:657
  155.2 9.3 %copy-start.5 = (bf16[64,4096]{1,0:T(8,128)(2,1)}, bf16[64,4096]{1,0:T(8,128)(2,1)S(1)}, u32[]{:S(2)}) copy-start(bf16[64,4096]{1,0:T(8,128)(2,1)S(1)} %collective-permute-done.10.kept) | copy-start | bytes 1572868
  155.2 9.3 %copy-start.6 = (bf16[64,4096]{1,0:T(8,128)(2,1)}, bf16[64,4096]{1,0:T(8,128)(2,1)S(1)}, u32[]{:S(2)}) copy-start(bf16[64,4096]{1,0:T(8,128)(2,1)S(1)} %collective-permute-done.11.swapped_own) | copy-start | bytes 1572868
  164.4 0.8 copy-start.7
